TPU v7x, 128 devices: a whole 4x4x4 slice. The times are simulated.
128 devices in a mesh: seq: 4 (over x), vocab: 32 (over y, z, core).
Axes of the slice: x: 4, y: 4, z: 4, core: 2. Of those that a mesh axis runs over, the one named last changes fastest.
Arguments:
- teacher_hidden: bfloat16 [768, 8192], P('seq'), may hold values from -125 to 125, as said below
- teacher_weight: bfloat16 [8192, 65536], P('seq', 'vocab'), may hold values from -0.0625 to 0.0625
- student_hidden: bfloat16 [768, 3072], P(('seq', 'vocab')), may hold values from -125 to 125, as said below
- student_weight: bfloat16 [3072, 32, 2048], P(None, 'vocab', 'seq'), may hold values from -0.109375 to 0.109375
Outputs:
- loss: float32 [], replicated
- grad_hidden: bfloat16 [768, 3072], P(('seq', 'vocab'))
- grad_weight: float32 [3072, 32, 2048], P(None, 'vocab', 'seq')
Inputs may be any that keep to these rules, and one draw needn't show every extreme that they name: `teacher_hidden`: teacher hidden entries lie within this range. `student_hidden`: student hidden entries lie within this range.
All inputs are finite; a program needn't handle non-finite values.
Results may differ from a plain program's by a relative error of at most 0.0085.
Values may be sent and summed in bfloat16 or wider, within the bound.
No kernel may reach another device: no remote copies, remote signals or barrier semaphores. Data moves between devices by JAX's collectives and lax.ppermute only.
A program may use at most 128 MiB of HBM per device.

v0:
```python
import jax
import jax.numpy as jnp
from jax import lax
from jax.sharding import PartitionSpec as P

grad_scale = 64.0


def shards(teacher_hidden, teacher_weight, student_hidden, student_weight):
    teacher_logits = jnp.dot(
        teacher_hidden,
        lax.all_gather(teacher_weight, "seq", axis=0, tiled=True),
        preferred_element_type=jnp.float32,
    )
    regrouped = lax.all_to_all(teacher_logits, "seq", split_axis=1, concat_axis=0, tiled=True)
    weight_local = student_weight[:, 0, :]
    gathered = lax.all_gather(student_hidden, ("seq", "vocab"), axis=0, tiled=True)
    student_logits = jnp.dot(gathered, weight_local, preferred_element_type=jnp.float32)
    t_local = jnp.max(regrouped, axis=1)
    s_local = jnp.max(student_logits, axis=1)
    t_max, s_max = lax.pmax((t_local, s_local), ("seq", "vocab"))
    t_exp = jnp.exp(regrouped - t_max[:, None])
    s_exp = jnp.exp(student_logits - s_max[:, None])
    t_sum, cross, s_sum = lax.psum(
        (
            jnp.sum(t_exp, axis=1),
            jnp.sum(t_exp * (regrouped - student_logits), axis=1),
            jnp.sum(s_exp, axis=1),
        ),
        ("seq", "vocab"),
    )
    kl_rows = cross / t_sum - t_max - jnp.log(t_sum) + s_max + jnp.log(s_sum)
    loss = jnp.mean(kl_rows)
    grad_logits = (grad_scale * (s_exp / s_sum[:, None] - t_exp / t_sum[:, None])).astype(
        jnp.bfloat16
    )
    grad_local = lax.dot_general(
        gathered, grad_logits, (((0,), (0,)), ((), ())), preferred_element_type=jnp.float32
    )
    grad_hidden = lax.psum_scatter(
        lax.dot_general(
            grad_logits, weight_local, (((1,), (1,)), ((), ())), preferred_element_type=jnp.float32
        ),
        ("seq", "vocab"),
        scatter_dimension=0,
        tiled=True,
    ).astype(jnp.bfloat16)
    return (loss, grad_hidden, grad_local[:, None, :])


def solution(mesh):
    in_specs = (
        P("seq", None),
        P("seq", "vocab"),
        P(("seq", "vocab"), None),
        P(None, "vocab", "seq"),
    )
    out_specs = (P(), P(("seq", "vocab"), None), P(None, "vocab", "seq"))
    return jax.shard_map(shards, mesh=mesh, in_specs=in_specs, out_specs=out_specs, check_vma=False)
```

profile of v0, /device:TPU:1, one launch (start us, length us, event | category | flops | bytes accessed | tf_op | source)
XLA Modules:
  0.0 1068.5 jit_solution(2517473349793335373)
XLA Ops:
  8.7 298.1 %all-gather.4.cloned.1.call-done = bf16[8192,2048]{1,0:T(8,128)(2,1)} async-done(((bf16[2048,2048]{1,0:T(8,128)(2,1)}), bf16[8192,2048]{1,0:T(8,128)(2,1)}) %all-gather.4.cloned.1.call-update) | async-done | bytes 33554448 | tf_op jit(solution)/shard_map/all_gather | solution.py:12
  306.8 14.9 %fusion.10 = f32[192,2048]{1,0:T(8,128)S(1)} fusion(bf16[192,8192]{1,0:T(8,128)(2,1)} %param.4, bf16[8192,2048]{1,0:T(8,128)(2,1)} %all-gather.4.cloned.1.call-done), kind=kOutput, calls=%fused_computation.19 | convolution fusion | flops 6442450944 | bytes 38273024 | tf_op jit(solution)/shard_map/dot_general | solution.py:10
  323.0 4.3 all-to-all-start
  327.3 53.6 %all-gather.6.cloned.1.call-done = bf16[128,6,3072]{2,1,0:T(8,128)(2,1)} async-done(((bf16[1,6,3072]{2,1,0:T(8,128)(2,1)}), bf16[128,6,3072]{2,1,0:T(8,128)(2,1)}) %all-gather.6.cloned.1.call-update) | async-done | bytes 4718608 | tf_op jit(solution)/shard_map/all_gather | solution.py:17
  381.0 7.7 reshape.20
  388.7 6.1 fusion.9
  394.8 3.1 copy.14
  399.6 62.6 %all-reduce.3 = (f32[768]{0:T(1024)S(1)}, f32[768]{0:T(1024)S(1)}) all-reduce(f32[768]{0:T(1024)S(1)} %reduce_max.21, f32[768]{0:T(1024)S(1)} %get-tuple-element.50), channel_id=1, replica_groups=mesh['seq'=4,'vocab'=32] {'seq','vocab'}, use_global_device_ids=true, to_apply=%region_1.0 | all-reduce | flops 1536 | bytes 12288 | tf_op jit(solution)/shard_map/pmax | solution.py:21
  464.2 2.4 multiply_reduce_fusion
  466.6 64.4 %all-reduce.2 = (f32[768]{0:T(1024)S(1)}, f32[768]{0:T(1024)S(1)}, f32[768]{0:T(1024)}) all-reduce(f32[768]{0:T(1024)S(1)} %get-tuple-element.13, f32[768]{0:T(1024)S(1)} %reduce_sum.40, f32[768]{0:T(1024)S(1)} %get-tuple-element.12), channel_id=1, replica_groups=mesh['seq'=4,'vocab'=32] {'seq','vocab'}, use_global_device_ids=true, to_apply=%region_9.0 | all-reduce | flops 2304 | bytes 18432 | tf_op jit(solution)/shard_map/psum | solution.py:24
  531.0 7.6 fusion.1
  538.7 358.9 %fusion = f32[8,3072]{1,0:T(8,128)S(1)} fusion(f32[768,3072]{1,0:T(8,128)} %fusion.1), kind=kCustom, calls=%all-reduce-scatter | all-reduce-scatter fusion | flops 3145729 | bytes 9535488
  909.3 12.2 %collective-permute-start.22 = (bf16[8,3072]{1,0:T(8,128)(2,1)S(1)}, bf16[8,3072]{1,0:T(8,128)(2,1)S(1)}, u32[]{:S(2)}, u32[]{:S(2)}) collective-permute-start(bf16[8,3072]{1,0:T(8,128)(2,1)S(1)} %convert.62), channel_id=1, source_target_pairs={{0,23},{1,24},{2,25},{3,26},{4,27},{5,28},{6,29},{7,30},{8,31},{9,... | collective-permute-start | bytes 147464
  921.5 5.9 collective-permute-start.21
  927.5 2.8 collective-permute-start.20
  930.3 2.2 collective-permute-start.19
  932.6 3.4 collective-permute-start.18
  936.0 3.3 collective-permute-start.17
  943.0 2.2 collective-permute-start.14
  945.2 2.1 collective-permute-start.13
  947.3 3.6 collective-permute-start.12
  950.9 3.5 collective-permute-start.11
  954.4 4.1 collective-permute-start.10
  963.1 2.8 collective-permute-start.6
  965.9 3.6 collective-permute-start.5
  969.5 8.7 convolution_bitcast_fusion
  978.2 3.6 collective-permute-start.4
  981.8 3.2 collective-permute-start.3
  985.0 3.4 collective-permute-start.2
  990.4 2.8 collective-permute-start
  993.8 14.1 %copy.16 = f32[3072,1,512]{2,1,0:T(1,128)} copy(f32[3072,1,512]{0,2,1:T(8,128)} %convolution_bitcast_fusion) | data formatting | bytes 12582912
  1008.6 50.4 %concatenate = bf16[262,3072]{1,0:T(8,128)(2,1)} concatenate(bf16[6,3072]{1,0:T(8,128)(2,1)S(1)} %collective-permute-done.31, bf16[8,3072]{1,0:T(8,128)(2,1)S(1)} %collective-permute-done.30, bf16[8,3072]{1,0:T(8,128)(2,1)S(1)} %collective-permute-done.29, bf16[8,3072]{1,0:T(8,128)(2,1)S(1)} %collective-permute-done.28, bf16[8,3072]{1,0:T(8,128)(2,1)S(1)} %collective-permute-done.27, ...), dimensions={0} | concatenate | bytes 3268608
  (100 shorter events, 30.5 us)
Async XLA Ops:
  7.2 299.6 %all-gather.4.cloned.1.call-start = ((), (), s32[]{:S(2)}) async-start(), calls=%async_computation.1 | async-start | bytes 41943040 | tf_op jit(solution)/shard_map/all_gather | solution.py:12
  7.9 373.0 %all-gather.6.cloned.1.call-start = ((), (), s32[]{:S(2)}) async-start(), calls=%async_computation.2 | async-start | bytes 6340608 | tf_op jit(solution)/shard_map/all_gather | solution.py:17
  323.0 71.9 %all-to-all-start = ((f32[192,4,512]{2,0,1:T(8,128)}), f32[192,4,512]{2,0,1:T(8,128)}, u32[]{:S(2)}, u32[]{:S(2)}) async-start(f32[192,4,512]{2,0,1:T(8,128)} %bitcast.29), calls=%async_computation | async-start | bytes 3145728 | tf_op jit(solution)/shard_map/all_to_all | solution.py:15
  897.6 7.8 collective-permute-start.30
  902.8 6.5 collective-permute-start.27
  904.1 17.4 %collective-permute-start.26 = (bf16[8,3072]{1,0:T(8,128)(2,1)S(1)}, bf16[8,3072]{1,0:T(8,128)(2,1)S(1)}, u32[]{:S(2)}, u32[]{:S(2)}) collective-permute-start(bf16[8,3072]{1,0:T(8,128)(2,1)S(1)} %convert.62), channel_id=1, source_target_pairs={{0,27},{1,28},{2,29},{3,30},{4,31},{5,32},{6,33},{7,34},{8,35},{9,... | collective-permute-start | bytes 147464
  905.4 22.0 %collective-permute-start.25 = (bf16[8,3072]{1,0:T(8,128)(2,1)S(1)}, bf16[8,3072]{1,0:T(8,128)(2,1)S(1)}, u32[]{:S(2)}, u32[]{:S(2)}) collective-permute-start(bf16[8,3072]{1,0:T(8,128)(2,1)S(1)} %convert.62), channel_id=1, source_target_pairs={{0,26},{1,27},{2,28},{3,29},{4,30},{5,31},{6,32},{7,33},{8,34},{9,... | collective-permute-start | bytes 147464
  906.7 23.6 %collective-permute-start.24 = (bf16[8,3072]{1,0:T(8,128)(2,1)S(1)}, bf16[8,3072]{1,0:T(8,128)(2,1)S(1)}, u32[]{:S(2)}, u32[]{:S(2)}) collective-permute-start(bf16[8,3072]{1,0:T(8,128)(2,1)S(1)} %convert.62), channel_id=1, source_target_pairs={{0,25},{1,26},{2,27},{3,28},{4,29},{5,30},{6,31},{7,32},{8,33},{9,... | collective-permute-start | bytes 147464
  908.0 24.5 %collective-permute-start.23 = (bf16[8,3072]{1,0:T(8,128)(2,1)S(1)}, bf16[8,3072]{1,0:T(8,128)(2,1)S(1)}, u32[]{:S(2)}, u32[]{:S(2)}) collective-permute-start(bf16[8,3072]{1,0:T(8,128)(2,1)S(1)} %convert.62), channel_id=1, source_target_pairs={{0,24},{1,25},{2,26},{3,27},{4,28},{5,29},{6,30},{7,31},{8,32},{9,... | collective-permute-start | bytes 147464
  909.3 26.7 %collective-permute-start.22 = (bf16[8,3072]{1,0:T(8,128)(2,1)S(1)}, bf16[8,3072]{1,0:T(8,128)(2,1)S(1)}, u32[]{:S(2)}, u32[]{:S(2)}) collective-permute-start(bf16[8,3072]{1,0:T(8,128)(2,1)S(1)} %convert.62), channel_id=1, source_target_pairs={{0,23},{1,24},{2,25},{3,26},{4,27},{5,28},{6,29},{7,30},{8,31},{9,... | collective-permute-start | bytes 147464
  921.5 17.8 %collective-permute-start.21 = (bf16[8,3072]{1,0:T(8,128)(2,1)S(1)}, bf16[8,3072]{1,0:T(8,128)(2,1)S(1)}, u32[]{:S(2)}, u32[]{:S(2)}) collective-permute-start(bf16[8,3072]{1,0:T(8,128)(2,1)S(1)} %convert.62), channel_id=1, source_target_pairs={{0,22},{1,23},{2,24},{3,25},{4,26},{5,27},{6,28},{7,29},{8,30},{9,... | collective-permute-start | bytes 147464
  927.5 13.6 %collective-permute-start.20 = (bf16[8,3072]{1,0:T(8,128)(2,1)S(1)}, bf16[8,3072]{1,0:T(8,128)(2,1)S(1)}, u32[]{:S(2)}, u32[]{:S(2)}) collective-permute-start(bf16[8,3072]{1,0:T(8,128)(2,1)S(1)} %convert.62), channel_id=1, source_target_pairs={{0,21},{1,22},{2,23},{3,24},{4,25},{5,26},{6,27},{7,28},{8,29},{9,... | collective-permute-start | bytes 147464
  930.3 12.7 %collective-permute-start.19 = (bf16[8,3072]{1,0:T(8,128)(2,1)S(1)}, bf16[8,3072]{1,0:T(8,128)(2,1)S(1)}, u32[]{:S(2)}, u32[]{:S(2)}) collective-permute-start(bf16[8,3072]{1,0:T(8,128)(2,1)S(1)} %convert.62), channel_id=1, source_target_pairs={{0,20},{1,21},{2,22},{3,23},{4,24},{5,25},{6,26},{7,27},{8,28},{9,... | collective-permute-start | bytes 147464
  932.6 12.7 %collective-permute-start.18 = (bf16[8,3072]{1,0:T(8,128)(2,1)S(1)}, bf16[8,3072]{1,0:T(8,128)(2,1)S(1)}, u32[]{:S(2)}, u32[]{:S(2)}) collective-permute-start(bf16[8,3072]{1,0:T(8,128)(2,1)S(1)} %convert.62), channel_id=1, source_target_pairs={{0,19},{1,20},{2,21},{3,22},{4,23},{5,24},{6,25},{7,26},{8,27},{9,... | collective-permute-start | bytes 147464
  936.0 11.3 %collective-permute-start.17 = (bf16[8,3072]{1,0:T(8,128)(2,1)S(1)}, bf16[8,3072]{1,0:T(8,128)(2,1)S(1)}, u32[]{:S(2)}, u32[]{:S(2)}) collective-permute-start(bf16[8,3072]{1,0:T(8,128)(2,1)S(1)} %convert.62), channel_id=1, source_target_pairs={{0,18},{1,19},{2,20},{3,21},{4,22},{5,23},{6,24},{7,25},{8,26},{9,... | collective-permute-start | bytes 147464
  939.4 11.5 %collective-permute-start.16 = (bf16[8,3072]{1,0:T(8,128)(2,1)S(1)}, bf16[8,3072]{1,0:T(8,128)(2,1)S(1)}, u32[]{:S(2)}, u32[]{:S(2)}) collective-permute-start(bf16[8,3072]{1,0:T(8,128)(2,1)S(1)} %convert.62), channel_id=1, source_target_pairs={{0,17},{1,18},{2,19},{3,20},{4,21},{5,22},{6,23},{7,24},{8,25},{9,... | collective-permute-start | bytes 147464
  941.1 13.3 %collective-permute-start.15 = (bf16[8,3072]{1,0:T(8,128)(2,1)S(1)}, bf16[8,3072]{1,0:T(8,128)(2,1)S(1)}, u32[]{:S(2)}, u32[]{:S(2)}) collective-permute-start(bf16[8,3072]{1,0:T(8,128)(2,1)S(1)} %convert.62), channel_id=1, source_target_pairs={{0,16},{1,17},{2,18},{3,19},{4,20},{5,21},{6,22},{7,23},{8,24},{9,... | collective-permute-start | bytes 147464
  943.0 15.5 %collective-permute-start.14 = (bf16[8,3072]{1,0:T(8,128)(2,1)S(1)}, bf16[8,3072]{1,0:T(8,128)(2,1)}, u32[]{:S(2)}, u32[]{:S(2)}) collective-permute-start(bf16[8,3072]{1,0:T(8,128)(2,1)S(1)} %convert.62), channel_id=1, source_target_pairs={{0,15},{1,16},{2,17},{3,18},{4,19},{5,20},{6,21},{7,22},{8,23},{9,... | collective-permute-start | bytes 147464
  945.2 14.6 %collective-permute-start.13 = (bf16[8,3072]{1,0:T(8,128)(2,1)S(1)}, bf16[8,3072]{1,0:T(8,128)(2,1)}, u32[]{:S(2)}, u32[]{:S(2)}) collective-permute-start(bf16[8,3072]{1,0:T(8,128)(2,1)S(1)} %convert.62), channel_id=1, source_target_pairs={{0,14},{1,15},{2,16},{3,17},{4,18},{5,19},{6,20},{7,21},{8,22},{9,... | collective-permute-start | bytes 147464
  947.3 14.5 %collective-permute-start.12 = (bf16[8,3072]{1,0:T(8,128)(2,1)S(1)}, bf16[8,3072]{1,0:T(8,128)(2,1)}, u32[]{:S(2)}, u32[]{:S(2)}) collective-permute-start(bf16[8,3072]{1,0:T(8,128)(2,1)S(1)} %convert.62), channel_id=1, source_target_pairs={{0,13},{1,14},{2,15},{3,16},{4,17},{5,18},{6,19},{7,20},{8,21},{9,... | collective-permute-start | bytes 147464
  950.9 12.2 %collective-permute-start.11 = (bf16[8,3072]{1,0:T(8,128)(2,1)S(1)}, bf16[8,3072]{1,0:T(8,128)(2,1)}, u32[]{:S(2)}, u32[]{:S(2)}) collective-permute-start(bf16[8,3072]{1,0:T(8,128)(2,1)S(1)} %convert.62), channel_id=1, source_target_pairs={{0,12},{1,13},{2,14},{3,15},{4,16},{5,17},{6,18},{7,19},{8,20},{9,... | collective-permute-start | bytes 147464
  954.4 11.5 %collective-permute-start.10 = (bf16[8,3072]{1,0:T(8,128)(2,1)S(1)}, bf16[8,3072]{1,0:T(8,128)(2,1)}, u32[]{:S(2)}, u32[]{:S(2)}) collective-permute-start(bf16[8,3072]{1,0:T(8,128)(2,1)S(1)} %convert.62), channel_id=1, source_target_pairs={{0,11},{1,12},{2,13},{3,14},{4,15},{5,16},{6,17},{7,18},{8,19},{9,... | collective-permute-start | bytes 147464
  958.6 19.7 %collective-permute-start.9 = (bf16[8,3072]{1,0:T(8,128)(2,1)S(1)}, bf16[8,3072]{1,0:T(8,128)(2,1)S(1)}, u32[]{:S(2)}, u32[]{:S(2)}) collective-permute-start(bf16[8,3072]{1,0:T(8,128)(2,1)S(1)} %convert.62), channel_id=1, source_target_pairs={{0,10},{1,11},{2,12},{3,13},{4,14},{5,15},{6,16},{7,17},{8,18},{9,... | collective-permute-start | bytes 147464
  959.9 22.0 %collective-permute-start.8 = (bf16[8,3072]{1,0:T(8,128)(2,1)S(1)}, bf16[8,3072]{1,0:T(8,128)(2,1)S(1)}, u32[]{:S(2)}, u32[]{:S(2)}) collective-permute-start(bf16[8,3072]{1,0:T(8,128)(2,1)S(1)} %convert.62), channel_id=1, source_target_pairs={{0,9},{1,10},{2,11},{3,12},{4,13},{5,14},{6,15},{7,16},{8,17},{9,1... | collective-permute-start | bytes 147464
  961.8 23.2 %collective-permute-start.7 = (bf16[8,3072]{1,0:T(8,128)(2,1)S(1)}, bf16[8,3072]{1,0:T(8,128)(2,1)S(1)}, u32[]{:S(2)}, u32[]{:S(2)}) collective-permute-start(bf16[8,3072]{1,0:T(8,128)(2,1)S(1)} %convert.62), channel_id=1, source_target_pairs={{0,8},{1,9},{2,10},{3,11},{4,12},{5,13},{6,14},{7,15},{8,16},{9,17... | collective-permute-start | bytes 147464
  963.1 25.3 %collective-permute-start.6 = (bf16[8,3072]{1,0:T(8,128)(2,1)S(1)}, bf16[8,3072]{1,0:T(8,128)(2,1)S(1)}, u32[]{:S(2)}, u32[]{:S(2)}) collective-permute-start(bf16[8,3072]{1,0:T(8,128)(2,1)S(1)} %convert.62), channel_id=1, source_target_pairs={{0,7},{1,8},{2,9},{3,10},{4,11},{5,12},{6,13},{7,14},{8,15},{9,16}... | collective-permute-start | bytes 147464
  965.9 24.5 %collective-permute-start.5 = (bf16[8,3072]{1,0:T(8,128)(2,1)S(1)}, bf16[8,3072]{1,0:T(8,128)(2,1)S(1)}, u32[]{:S(2)}, u32[]{:S(2)}) collective-permute-start(bf16[8,3072]{1,0:T(8,128)(2,1)S(1)} %convert.62), channel_id=1, source_target_pairs={{0,6},{1,7},{2,8},{3,9},{4,10},{5,11},{6,12},{7,13},{8,14},{9,15},... | collective-permute-start | bytes 147464
  978.2 30.3 %collective-permute-start.4 = (bf16[8,3072]{1,0:T(8,128)(2,1)S(1)}, bf16[8,3072]{1,0:T(8,128)(2,1)}, u32[]{:S(2)}, u32[]{:S(2)}) collective-permute-start(bf16[8,3072]{1,0:T(8,128)(2,1)S(1)} %convert.62), channel_id=1, source_target_pairs={{0,5},{1,6},{2,7},{3,8},{4,9},{5,10},{6,11},{7,12},{8,13},{9,14},{... | collective-permute-start | bytes 147464
  981.8 26.8 %collective-permute-start.3 = (bf16[8,3072]{1,0:T(8,128)(2,1)S(1)}, bf16[8,3072]{1,0:T(8,128)(2,1)}, u32[]{:S(2)}, u32[]{:S(2)}) collective-permute-start(bf16[8,3072]{1,0:T(8,128)(2,1)S(1)} %convert.62), channel_id=1, source_target_pairs={{0,4},{1,5},{2,6},{3,7},{4,8},{5,9},{6,10},{7,11},{8,12},{9,13},{1... | collective-permute-start | bytes 147464
  985.0 23.6 %collective-permute-start.2 = (bf16[8,3072]{1,0:T(8,128)(2,1)S(1)}, bf16[8,3072]{1,0:T(8,128)(2,1)}, u32[]{:S(2)}, u32[]{:S(2)}) collective-permute-start(bf16[8,3072]{1,0:T(8,128)(2,1)S(1)} %convert.62), channel_id=1, source_target_pairs={{0,3},{1,4},{2,5},{3,6},{4,7},{5,8},{6,9},{7,10},{8,11},{9,12},{10... | collective-permute-start | bytes 147464
  988.4 20.2 %collective-permute-start.1 = (bf16[8,3072]{1,0:T(8,128)(2,1)S(1)}, bf16[8,3072]{1,0:T(8,128)(2,1)}, u32[]{:S(2)}, u32[]{:S(2)}) collective-permute-start(bf16[8,3072]{1,0:T(8,128)(2,1)S(1)} %convert.62), channel_id=1, source_target_pairs={{0,2},{1,3},{2,4},{3,5},{4,6},{5,7},{6,8},{7,9},{8,10},{9,11},{10,... | collective-permute-start | bytes 147464
  990.4 18.2 %collective-permute-start = (bf16[8,3072]{1,0:T(8,128)(2,1)S(1)}, bf16[8,3072]{1,0:T(8,128)(2,1)}, u32[]{:S(2)}, u32[]{:S(2)}) collective-permute-start(bf16[8,3072]{1,0:T(8,128)(2,1)S(1)} %convert.62), channel_id=1, source_target_pairs={{0,1},{1,2},{2,3},{3,4},{4,5},{5,6},{6,7},{7,8},{8,9},{9,10},{10,1... | collective-permute-start | bytes 147464
  (22 other events, 705.0 us)
Sparse Core Ops, SparseCore 0:
  9.7 297.0 all-gather.3
  309.8 71.1 all-gather.5
where the time goes:
time: 1070 us
  blocking collectives  486 us (45%)
  waiting for transfers between devices  353 us (33%)
  starting transfers between devices  90.7 us (8%)
  local copies, waits for them, and re-layouts  78.5 us (7%)
  matrix products  37.4 us (3%)
  between operations  16.4 us (2%)
    unnamed x1, blocking collectives  359 us
    all_gather x1, waiting for transfers between devices, shards(): lax.all_gather(teacher_weight, 'seq', axis=0, tiled=True)  298 us
    unnamed x32, starting transfers between devices  86.3 us
    unnamed x42, local copies, waits for them, and re-layouts  72.3 us
    psum x1, blocking collectives, shards(): lax.psum((jnp.sum(t_exp, axis=1), jnp.sum(t_exp * (regrouped - student_lo...  64.4 us
    pmax x1, blocking collectives, shards(): t_max, s_max = lax.pmax((t_local, s_local), ('seq', 'vocab'))  62.6 us
    all_gather x1, waiting for transfers between devices, shards(): lax.all_gather(student_hidden, ('seq', 'vocab'), axis=0, tiled=True)  53.6 us
  transfers between devices with their start and end apart: 35, of which 2 were waited for; matrix products, arithmetic and copies ran while one was open for 5% of the time, Pallas kernels for 0%

commit v1 on v0

v1 whole, which is shorter than its diff:
```python
import functools

import jax
import jax.numpy as jnp
import numpy as np
from jax import lax
from jax.experimental import pallas as pl
from jax.experimental.pallas import tpu as pltpu
from jax.sharding import Mesh
from jax.sharding import PartitionSpec as P

grad_scale = 64.0
ROWS = (8, 4)
ALL = ("x", "y", "z", "c")
CHIPS = ("x", "y", "z")
SWAP = [(0, 1), (1, 0)]
F32, BF16 = jnp.float32, jnp.bfloat16
NT = (((1,), (1,)), ((), ()))
TN = (((0,), (0,)), ((), ()))
VMEM_BYTES = 20 * 2**20


def shift(k):
    return [(i, (i + k) % 4) for i in range(4)]


def dot(a, b, dims=(((1,), (0,)), ((), ()))):
    return lax.dot_general(a, b, dims, preferred_element_type=F32)


def call(body, scalars, args, in_specs, outs, out_specs, grid=(1,), scratch=(), flops=0):
    nbytes = sum(a.size * a.dtype.itemsize for a in list(args) + list(outs))
    return pl.pallas_call(
        body,
        out_shape=outs,
        grid_spec=pltpu.PrefetchScalarGridSpec(
            num_scalar_prefetch=1, grid=grid, in_specs=in_specs, out_specs=out_specs, scratch_shapes=scratch
        ),
        compiler_params=pltpu.CompilerParams(vmem_limit_bytes=VMEM_BYTES),
        cost_estimate=pl.CostEstimate(flops=flops, bytes_accessed=nbytes, transcendentals=0),
    )(scalars, *args)


def whole(shape):
    return pl.BlockSpec(shape, lambda *_: (0,) * len(shape))


def sds(shape, dtype):
    return jax.ShapeDtypeStruct(shape, dtype)


def cut_body(where, order, th, own, *sends):
    ks = th.shape[1] // 4
    x, c = where[0], where[1]
    halves = []
    for s, n in ((0, 16 * ROWS[0]), (16 * ROWS[0], 16 * ROWS[1])):
        halves.append(order[pl.ds(pl.multiple_of(s + c * (n // 2), n // 2), n // 2), :])
    pick = jnp.concatenate(halves, axis=0)
    for k in (1, 2, 3):
        block = th[:, pl.ds(pl.multiple_of(lax.rem(x + k, 4) * ks, ks), ks)]
        sends[k - 1][...] = dot(pick, block).astype(BF16)
    block = th[:, pl.ds(pl.multiple_of(x * ks, ks), ks)]
    own[...] = dot(order[...], block).astype(BF16)


def cut(where, order, th):
    rows, d = th.shape
    ks = d // 4
    outs = [sds((rows, ks), BF16)] + [sds((rows // 2, ks), BF16)] * 3
    return call(
        cut_body, where, (order, th), [whole(order.shape), whole(th.shape)], outs, [whole(o.shape) for o in outs],
        flops=4 * rows * rows * d,
    )


def first_body(group, where, own, g1, g2, g3, o1, o2, o3, tw, h, r, l, wr, wl, sems):
    n = 16 * ROWS[group]
    nh = n // 2
    at = 16 * ROWS[0] * group
    x, c = where[0], where[1]
    cols = wr.shape[1]
    copies = []
    for i, (step, to) in enumerate(((3, wr), (1, wl))):
        block = tw.at[:, pl.ds(pl.multiple_of(lax.rem(x + step, 4) * cols, cols), cols)]
        copies.append(pltpu.make_async_copy(block, to, sems.at[i]))
        copies[-1].start()
    h[pl.ds(pl.multiple_of(x * n, n), n), :] = own[at : at + n, :]
    at = at // 2
    for k, (a, b) in enumerate(((g1, o1), (g2, o2), (g3, o3))):
        to = lax.rem(x + 3 - k, 4) * n
        h[pl.ds(pl.multiple_of(to + c * nh, nh), nh), :] = a[at : at + nh, :]
        h[pl.ds(pl.multiple_of(to + (1 - c) * nh, nh), nh), :] = b[at : at + nh, :]
    copies[0].wait()
    r[...] = dot(h[: 2 * n, :], wr[...])
    copies[1].wait()
    l[...] = dot(h[2 * n :, :], wl[...])


def first(where, group, own, got, other, tw):
    n, ks = 16 * ROWS[group], own.shape[1]
    cols = tw.shape[1] // 4
    outs = [sds((4 * n, ks), BF16), sds((2 * n, cols), F32), sds((2 * n, cols), F32)]
    pieces = [own, *got, *other]
    specs = [whole(p.shape) for p in pieces] + [pl.BlockSpec(memory_space=pltpu.HBM)]
    body = functools.partial(first_body, group)
    scratch = [pltpu.VMEM((ks, cols), BF16)] * 2 + [pltpu.SemaphoreType.DMA((2,))]
    return call(
        body, where, (*pieces, tw), specs, outs, [whole(o.shape) for o in outs], scratch=scratch, flops=8 * n * ks * cols
    )


def rest_body(where, h, w, wl, out):
    half = h.shape[0] // 2
    step = pl.program_id(0)

    @pl.when(step != 1)
    def _():
        out[0] = dot(h[...], w[...])

    @pl.when(step == 1)
    def _():
        out[0, :half, :] = dot(h[:half, :], w[...])
        out[0, half:, :] = dot(h[half:, :], wl[...])


def rest(where, h, tw):
    rows, ks = h.shape
    cols = tw.shape[1] // 4
    out = sds((3, rows, cols), F32)
    specs = [
        whole(h.shape),
        pl.BlockSpec((ks, cols), lambda i, w: (0, lax.rem(w[0] + 6 - i, 4))),
        pl.BlockSpec((ks, cols), lambda i, w: (0, lax.rem(w[0] + 3, 4))),
    ]
    step = pl.BlockSpec((1, rows, cols), lambda i, w: (i, 0, 0))
    return call(rest_body, where, (h, tw, tw), specs, [out], [step], grid=(3,), flops=6 * rows * ks * cols)[0]


def hop_body(where, p, right, left, r, l):
    half = right.shape[0]
    r[...] = p[0, :half, :] + right[...]
    l[...] = p[0, half:, :] + left[...]


def hop(where, p, step, right, left):
    half, cols = right.shape
    out = sds(right.shape, F32)
    specs = [pl.BlockSpec((1, 2 * half, cols), lambda i, w: (step, 0, 0)), whole(right.shape), whole(left.shape)]
    return call(hop_body, where, (p, right, left), specs, [out, out], [whole(out.shape)] * 2)


def student_body(where, pick_mine, pick_other, mine, other, w, hs, sl):
    rows = (dot(pick_mine[...], mine[...]) + dot(pick_other[...], other[...])).astype(BF16)
    hs[...] = rows

    @pl.when(pl.program_id(0) == 0)
    def _():
        sl[...] = jnp.zeros_like(sl)

    sl[...] += dot(rows, w[...])


def student(where, picks, mine, other, w):
    tokens, room = picks[0].shape
    d, cols = w.shape
    tile = d // 6
    block = pl.BlockSpec((room, tile), lambda i, s: (0, i))
    specs = [whole((tokens, room))] * 2 + [block, block, pl.BlockSpec((tile, cols), lambda i, s: (i, 0))]
    outs = [sds((tokens, d), BF16), sds((tokens, cols), F32)]
    return call(
        student_body, where, (*picks, mine, other, w), specs, outs,
        [pl.BlockSpec((tokens, tile), lambda i, s: (0, i)), whole(outs[1].shape)],
        grid=(6,), flops=2 * tokens * d * (2 * room + cols),
    )


def local_body(where, p, rr, lr, sl, *rest):
    tl, st = rest[-2:]
    half, cols = rr.shape
    tl[:half, :] = p[0, :half, :] + rr[...]
    tl[half:, :] = p[0, half:, :] + lr[...]
    t, s = tl[...], sl[...]
    t_max = jnp.max(t, axis=1, keepdims=True)
    s_max = jnp.max(s, axis=1, keepdims=True)
    te = jnp.exp(t - t_max)
    t_sum = jnp.sum(te, axis=1, keepdims=True)
    cross = jnp.sum(te * (t - s), axis=1, keepdims=True)
    s_sum = jnp.sum(jnp.exp(s - s_max), axis=1, keepdims=True)
    lane = lax.broadcasted_iota(jnp.int32, (2 * half, 128), 1)
    packed = jnp.zeros((2 * half, 128), F32)
    for i, v in enumerate((t_max, t_sum, cross, s_max, s_sum)):
        packed = jnp.where(lane == i, v, packed)
    if len(rest) == 3:
        st[:, : rest[0].shape[1]] = rest[0][...]
    st[:, st.shape[1] - 2 * half :] = jnp.transpose(packed)[:8, :]


def local(where, p, right, left, sl, at, earlier=None):
    half, cols = right.shape
    n = 2 * half
    args = (p, right, left, sl) + (() if earlier is None else (earlier,))
    outs = [sds((n, cols), F32), sds((8, n if earlier is None else n + earlier.shape[1]), F32)]
    specs = [
        pl.BlockSpec((1, n, cols), lambda i, s: (2, 0, 0)),
        whole(right.shape),
        whole(left.shape),
        pl.BlockSpec((n, cols), lambda i, s: (at, 0)),
    ] + [whole(a.shape) for a in args[4:]]
    return call(local_body, where, args, specs, outs, [whole(o.shape) for o in outs], flops=40 * half * cols)


def merged(parts):
    t_max = jnp.max(parts[0], axis=0, keepdims=True)
    s_max = jnp.max(parts[3], axis=0, keepdims=True)
    t_w = jnp.exp(parts[0] - t_max)
    s_w = jnp.exp(parts[3] - s_max)
    total = lambda v: jnp.sum(v, axis=0, keepdims=True)
    return [t_max, total(parts[1] * t_w), total(parts[2] * t_w), s_max, total(parts[4] * s_w)]


def spread_body(where, mine, other, out):
    lead = where[1] == 0
    a = jnp.where(lead, mine[...], other[...])
    b = jnp.where(lead, other[...], mine[...])
    t_max, s_max = jnp.maximum(a[0:1], b[0:1]), jnp.maximum(a[3:4], b[3:4])
    ta, tb = jnp.exp(a[0:1] - t_max), jnp.exp(b[0:1] - t_max)
    sa, sb = jnp.exp(a[3:4] - s_max), jnp.exp(b[3:4] - s_max)
    rows = [t_max, a[1:2] * ta + b[1:2] * tb, a[2:3] * ta + b[2:3] * tb, s_max, a[4:5] * sa + b[4:5] * sb]
    chip = jnp.concatenate(rows + [jnp.zeros_like(a[:3])], axis=0)
    out[...] = jnp.broadcast_to(chip[None], out.shape)


def spread(where, mine, other):
    out = sds((64,) + mine.shape, F32)
    return call(spread_body, where, (mine, other), [whole(mine.shape)] * 2, [out], [whole(out.shape)])[0]


def back(grad, place, w):
    if place is None:
        return dot(grad, w[...], NT)
    half = w.shape[0] // 2
    top = dot(dot(place[0], grad).astype(BF16), w[:half, :], NT)
    return top + dot(dot(place[1], grad).astype(BF16), w[half:, :], NT)


def grad_body(where, parts, tl, sl, w, *rest):
    place = rest[0] if len(rest) == 4 else None
    g, away, kl = rest[-3:]
    t_max, t_sum, cross, s_max, s_sum = merged([parts[:, i, :] for i in range(5)])
    rows = cross / t_sum - t_max - jnp.log(t_sum) + s_max + jnp.log(s_sum)
    kl[...] = jnp.broadcast_to(jnp.sum(rows, axis=1, keepdims=True), kl.shape)
    stats = jnp.concatenate([t_max, grad_scale / t_sum, s_max, grad_scale / s_sum], axis=0)
    stats = jnp.concatenate([stats, jnp.zeros((124, stats.shape[1]), F32)], axis=0)
    cols = jnp.transpose(stats)
    grad = jnp.exp(sl[...] - cols[:, 2:3]) * cols[:, 3:4] - jnp.exp(tl[...] - cols[:, 0:1]) * cols[:, 1:2]
    grad = grad.astype(BF16)
    g[...] = grad
    away[...] = back(grad, place, w).astype(BF16)


def back_shape(tokens, d, place):
    return (tokens, d // 2) if place is None else (place.shape[1], d // 4)


def grad_of(where, parts, tl, sl, at, w, place):
    tokens, cols = tl.shape
    d = w.shape[0]
    outs = [sds((tokens, cols), BF16), sds(back_shape(tokens, d, place), BF16), sds((8, 128), F32)]
    args = (parts, tl, sl, w) + (() if place is None else (place,))
    specs = [whole(a.shape) for a in args]
    specs[0] = pl.BlockSpec((64, 8, tokens), lambda i, s: (0, 0, at))
    specs[2] = pl.BlockSpec((tokens, cols), lambda i, s: (at, 0))
    specs[3] = pl.BlockSpec((d // 2, cols), lambda i, s: (1 - s[1], 0))
    return call(grad_body, where, args, specs, outs, [whole(o.shape) for o in outs], flops=tokens * cols * d)


def keep_body(where, g, w, *rest):
    rest[-1][...] = back(g[...], rest[0] if len(rest) == 2 else None, w)


def keep_of(where, g, w, place):
    tokens, cols = g.shape
    d = w.shape[0]
    out = sds(back_shape(tokens, d, place), F32)
    args = (g, w) + (() if place is None else (place,))
    specs = [whole(a.shape) for a in args]
    specs[1] = pl.BlockSpec((d // 2, cols), lambda i, s: (s[1], 0))
    return call(keep_body, where, args, specs, [out], [whole(out.shape)], flops=tokens * cols * d)[0]


def weight_body(where, hs, ga, gb, out, done):
    n = ga.shape[0]
    out[...] = (dot(hs[:n, :], ga[...], TN) + dot(hs[n:, :], gb[...], TN))[:, None, :]
    done[...] = jnp.zeros_like(done)


def weight_of(where, hs, gs):
    tokens, d = hs.shape
    cols = gs[0].shape[1]
    tile = 256
    outs = [sds((d, 1, cols), F32), sds((8, 128), F32)]
    specs = [pl.BlockSpec((tokens, tile), lambda i, s: (0, i))] + [whole(g.shape) for g in gs]
    return call(
        weight_body, where, (hs, *gs), specs, outs,
        [pl.BlockSpec((tile, 1, cols), lambda i, s: (i, 0, 0)), whole((8, 128))],
        grid=(d // tile,), flops=2 * tokens * d * cols,
    )


def row_order(rows):
    chips = np.arange(rows).reshape(16, -1)
    order = np.concatenate([chips[:, : ROWS[0]].reshape(-1), chips[:, ROWS[0] :].reshape(-1)])
    return np.eye(rows, dtype=np.float32)[order]


def place_of(m):
    if m == 8:
        return None
    place = np.zeros((2, 64, 2, m, 64, m), np.float32)
    for chip in range(64):
        for r in range(m):
            for h in range(2):
                place[h, chip, h, r, chip, r] = 1.0
    return jnp.asarray(place.reshape(2, 128 * m, 64 * m), BF16)


def picks_of(x, c, start, m, piece):
    i = jnp.arange(64 * m)
    row = start + i % m
    at = i % (16 * m) // m * 32 + (x + 4 - i // (16 * m)) % 4 * 8 + row % piece
    hit = at[:, None] == jnp.arange(512)[None, :]
    own = (row // piece == c)[:, None]
    return (hit & own).astype(BF16), (hit & ~own).astype(BF16)


def tie(values, *after):
    return lax.optimization_barrier((values, after))[0]


def shards(th, tw, sh, sw):
    x, c = lax.axis_index("x"), lax.axis_index("c")
    where = jnp.stack([x, c]).astype(jnp.int32)
    rows = th.shape[0]
    piece, d_s = sh.shape
    w = sw[:, 0, :]
    picks = [picks_of(x, c, s, m, piece) for s, m in zip((0, ROWS[0]), ROWS)]
    picks = [jnp.concatenate(p, axis=0) for p in zip(*picks)]
    places = [place_of(m) for m in ROWS]
    at = (0, 4 * 16 * ROWS[0] // (4 * 16 * ROWS[1]))

    def exchange(sends):
        return [lax.ppermute(s, "x", shift(k + 1)) for k, s in enumerate(sends)]

    def both_ways(r, l):
        return lax.ppermute(r, "x", shift(1)), lax.ppermute(l, "x", shift(-1))

    def swap(v):
        return lax.ppermute(v, "c", SWAP)

    own, *sends = cut(where, jnp.asarray(row_order(rows), BF16), th)
    got = [lax.ppermute(s, "x", shift(k + 1)) for k, s in enumerate(sends)]

    sh8 = jnp.pad(tie(sh, own), ((0, 8 - piece), (0, 0)))
    row = jnp.concatenate([sh8] + [lax.ppermute(sh8, "x", shift(k)) for k in (1, 2, 3)], axis=0)
    mine = lax.all_gather(row, ("y", "z"), axis=0, tiled=True)

    other = [swap(v) for v in got]
    h_a, r0_a, l0_a = first(where, 0, own, got, other, tw)
    right_a, left_a = both_ways(r0_a, l0_a)
    h_b, r0_b, l0_b = first(where, 1, tie(own, r0_a), got, other, tw)
    right_b, left_b = both_ways(r0_b, l0_b)
    p_a = rest(where, tie(h_a, r0_b), tw)
    r1_a, l1_a = hop(where, p_a, 0, right_a, left_a)
    right_a, left_a = both_ways(r1_a, l1_a)
    p_b = rest(where, tie(h_b, r1_a), tw)
    r1_b, l1_b = hop(where, p_b, 0, right_b, left_b)
    right_b, left_b = both_ways(r1_b, l1_b)
    r2_a, l2_a = hop(where, p_a, 1, right_a, tie(left_a, r1_b))
    right_a, left_a = both_ways(r2_a, l2_a)
    r2_b, l2_b = hop(where, p_b, 1, right_b, tie(left_b, r2_a))
    right_b, left_b = both_ways(r2_b, l2_b)
    mine = tie(mine, r2_b)
    theirs = swap(mine)
    hs, sl = student(where, picks, mine, theirs, w)
    tl_a, st_a = local(where, p_a, right_a, left_a, sl, at[0])
    tl_b, st = local(where, p_b, right_b, left_b, sl, at[1], st_a)
    sent = spread(where, st, swap(st))
    parts = lax.all_to_all(sent, CHIPS, split_axis=0, concat_axis=0, tiled=True)

    def finish(parts, tl, g):
        grad, away, kl = grad_of(where, parts, tl, sl, at[g], w, places[g])
        got = swap(away)
        chip = (keep_of(where, grad, w, places[g]) + got.astype(F32)).astype(BF16)
        return grad, chip.reshape(64, 8, -1), kl[0, 0]

    def scatter(chip):
        return lax.all_to_all(chip, CHIPS, split_axis=0, concat_axis=0, tiled=True)

    def total(parts):
        return jnp.sum(parts.astype(F32), axis=0).astype(BF16)

    g_a, chip_a, kl_a = finish(parts, tl_a, 0)
    to_a = scatter(chip_a)
    g_b, chip_b, kl_b = finish(tie(parts, chip_a), tl_b, 1)
    to_b = scatter(chip_b)
    loss = (kl_a + kl_b) / (4 * rows)
    grad_weight, done = weight_of(where, hs, tie((g_a, g_b), chip_b))

    sum_a = total(tie(to_a, done))
    sum_b = total(tie(to_b, done)).reshape(2, ROWS[1], -1).transpose(1, 0, 2).reshape(ROWS[1], -1)
    both = jnp.concatenate([sum_a, sum_b], axis=0)
    cores = (both[:piece], both[piece:])
    mine = jnp.where(c == 0, *cores)
    got = swap(jnp.where(c == 0, cores[1], cores[0]))
    grad_hidden = jnp.where(c == 0, jnp.concatenate([mine, got], 1), jnp.concatenate([got, mine], 1))
    return (loss, grad_hidden, grad_weight)


def solution(mesh):
    mesh = Mesh(mesh.devices.reshape(4, 4, 4, 2), ALL)
    vocab = ("y", "z", "c")
    in_specs = (P("x", None), P("x", vocab), P(ALL, None), P(None, vocab, "x"))
    out_specs = (P(), P(ALL, None), P(None, vocab, "x"))
    return jax.shard_map(shards, mesh=mesh, in_specs=in_specs, out_specs=out_specs, check_vma=False)
```

time: 1070 us -> 231 us (0.22)
  blocking collectives: 486 us -> 33.4 us
  waiting for transfers between devices: 353 us -> 49.4 us
  local copies, waits for them, and re-layouts: 78.5 us -> 21.4 us
  Pallas kernels: 0 us -> 49.4 us
  starting transfers between devices: 90.7 us -> 53.1 us
  matrix products: 37.4 us -> 0 us
    unnamed x1 -> x0, blocking collectives: 359 us -> none
    all_gather x2 -> x1, waiting for transfers between devices: 352 us -> 0.01 us  [shards(): mine = lax.all_gather(row, ('y', 'z'), axis=0, tiled=True)]
    unnamed x32 -> x0, starting transfers between devices: 86.3 us -> none
    psum x1 -> x0, blocking collectives: 64.4 us -> none  [shards(): lax.psum((jnp.sum(t_exp, axis=1), jnp.sum(t_exp * (regrouped - student_lo...]
    pmax x1 -> x0, blocking collectives: 62.6 us -> none  [shards(): t_max, s_max = lax.pmax((t_local, s_local), ('seq', 'vocab'))]
    unnamed x42 -> x50, local copies, waits for them, and re-layouts: 72.3 us -> 20.4 us
    pallas_call x0 -> x18, Pallas kernels: none -> 49.4 us  [call(): pl.pallas_call(body, out_shape=outs, grid_spec=pltpu.PrefetchScalarGridSp...]
    ppermute x0 -> x26, starting transfers between devices: none -> 40.9 us  [the longest x8 22.8 us: swap(): return lax.ppermute(v, 'c', SWAP)]
  transfers between devices with their start and end apart: 35 -> 29, of which waited for: 2 -> 18; matrix products, arithmetic and copies ran while one was open for 5% -> 2% of each run, Pallas kernels for 0% -> 19%
where the time goes in v1:
time: 231 us
  starting transfers between devices  53.1 us (23%)
  Pallas kernels  49.4 us (21%)
  waiting for transfers between devices  49.4 us (21%)
  blocking collectives  33.4 us (14%)
  local copies, waits for them, and re-layouts  21.4 us (9%)
  between operations  16.8 us (7%)
  other arithmetic  6.99 us (3%)
    pallas_call x18, Pallas kernels, call(): pl.pallas_call(body, out_shape=outs, grid_spec=pltpu.PrefetchScalarGridSp...  49.4 us
    all_to_all x1, blocking collectives, shards(): parts = lax.all_to_all(sent, CHIPS, split_axis=0, concat_axis=0, tiled=True)  33.4 us
    ppermute x8, starting transfers between devices, swap(): return lax.ppermute(v, 'c', SWAP)  22.8 us
    ppermute x12, waiting for transfers between devices, both_ways(): return (lax.ppermute(r, 'x', shift(1)), lax.ppermute(l, 'x', shift(-1)))  22 us
    unnamed x50, local copies, waits for them, and re-layouts  20.4 us
    all_to_all x2, starting transfers between devices, scatter(): return lax.all_to_all(chip, CHIPS, split_axis=0, concat_axis=0, tiled=True)  12.2 us
    all_to_all x2, waiting for transfers between devices, scatter(): return lax.all_to_all(chip, CHIPS, split_axis=0, concat_axis=0, tiled=True)  12 us
    ppermute x12, starting transfers between devices, both_ways(): return (lax.ppermute(r, 'x', shift(1)), lax.ppermute(l, 'x', shift(-1)))  10.3 us
  transfers between devices with their start and end apart: 29, of which 18 were waited for; matrix products, arithmetic and copies ran while one was open for 2% of the time, Pallas kernels for 19%

profile of v1, /device:TPU:1, one launch (start us, length us, event | category | flops | bytes accessed | tf_op | source)
XLA Modules:
  0.0 230.5 jit_solution(13648956852340891518)
XLA Ops:
  7.3 1.9 copy-done.14
  11.3 3.4 %collective-permute-start.18 = (bf16[8,3072]{1,0:T(8,128)(2,1)S(1)}, bf16[8,3072]{1,0:T(8,128)(2,1)S(1)}, u32[]{:S(2)}, u32[]{:S(2)}) collective-permute-start(bf16[8,3072]{1,0:T(8,128)(2,1)S(1)} %pad.4), channel_id=1, source_target_pairs={{0,96},{32,0},{64,32},{96,64},{1,97},{33,1},{65,33},{97,65},{2,98}... | collective-permute-start | bytes 147464 | tf_op jit(solution)/shard_map/ppermute | solution.py:364
  15.9 3.3 %collective-permute-done.17 = bf16[8,3072]{1,0:T(8,128)(2,1)S(1)} collective-permute-done((bf16[8,3072]{1,0:T(8,128)(2,1)S(1)}, bf16[8,3072]{1,0:T(8,128)(2,1)S(1)}, u32[]{:S(2)}, u32[]{:S(2)}) %collective-permute-start.17) | collective-permute-done | bytes 49184 | tf_op jit(solution)/shard_map/ppermute | solution.py:364
  23.8 7.0 %collective-permute-done.g1 = bf16[96,2048]{1,0:T(8,128)(2,1)S(1)} collective-permute-done((bf16[96,2048]{1,0:T(8,128)(2,1)S(1)}, bf16[96,2048]{1,0:T(8,128)(2,1)S(1)}, u32[]{:S(2)}, u32[]{:S(2)}) %collective-permute-start) | collective-permute-done | bytes 393248 | tf_op jit(solution)/shard_map/ppermute | solution.py:361
  30.8 10.8 %collective-permute-start.3 = (bf16[96,2048]{1,0:T(8,128)(2,1)S(1)}, bf16[96,2048]{1,0:T(8,128)(2,1)S(1)}, u32[]{:S(2)}, u32[]{:S(2)}) collective-permute-start(bf16[96,2048]{1,0:T(8,128)(2,1)S(1)} %collective-permute-done.g1), channel_id=1, source_target_pairs={{0,1},{1,0},{2,3},{3,2},{4,5},{5,4},{6,7},{7,6},{8,9},{9,8},{10,11... | collective-permute-start | bytes 1179656 | tf_op jit(solution)/shard_map/ppermute | solution.py:358
  44.1 3.4 %copy-done = bf16[2048,2048]{1,0:T(8,128)(2,1)S(1)} copy-done((bf16[2048,2048]{1,0:T(8,128)(2,1)S(1)}, bf16[2048,2048]{1,0:T(8,128)(2,1)}, u32[]{:S(2)}) %copy-start) | copy-done | bytes 8388632
  47.5 2.8 %shard_map.86 = (bf16[512,2048]{1,0:T(8,128)(2,1)S(1)}, f32[256,512]{1,0:T(8,128)S(1)}, f32[256,512]{1,0:T(8,128)S(1)}) custom-call(s32[2]{0:T(128)S(1)} %pad_add_fusion.where, bf16[192,2048]{1,0:T(8,128)(2,1)S(1)} %get-tuple-element.52.own, bf16[96,2048]{1,0:T(8,128)(2,1)S(1)} %collective-permute-done.g1, bf16[96,2048]{1,0:T(8,128)(2,1)S(1)} %collective-permute-done.1.g2, ...), custom_call_target="tpu_custom_call" | custom-call | flops 1073741824 | bytes 14680064 | tf_op jit(solution)/shard_map/pallas_call | solution.py:33
  50.3 1.9 collective-permute-start.7
  52.2 2.2 shard_map.87
  54.7 5.1 %shard_map.88.p = f32[3,512,512]{2,1,0:T(8,128)S(1)} custom-call(s32[2]{0:T(128)S(1)} %pad_add_fusion.where, bf16[512,2048]{1,0:T(8,128)(2,1)S(1)} %get-tuple-element.56.h, bf16[2048,2048]{1,0:T(8,128)(2,1)S(1)} %bitcast.12, bf16[2048,2048]{1,0:T(8,128)(2,1)S(1)} %bitcast.12), custom_call_target="tpu_custom_call" | custom-call | flops 3221225472 | bytes 22020096 | tf_op jit(solution)/shard_map/pallas_call | solution.py:33
  59.8 3.8 %collective-permute-done.7.left = f32[256,512]{1,0:T(8,128)S(1)} collective-permute-done((f32[256,512]{1,0:T(8,128)S(1)}, f32[256,512]{1,0:T(8,128)S(1)}, u32[]{:S(2)}, u32[]{:S(2)}) %collective-permute-start.7) | collective-permute-done | bytes 524320 | tf_op jit(solution)/shard_map/ppermute | solution.py:355
  63.6 2.7 %collective-permute-done.6.right = f32[256,512]{1,0:T(8,128)S(1)} collective-permute-done((f32[256,512]{1,0:T(8,128)S(1)}, f32[256,512]{1,0:T(8,128)S(1)}, u32[]{:S(2)}, u32[]{:S(2)}) %collective-permute-start.6) | collective-permute-done | bytes 524320 | tf_op jit(solution)/shard_map/ppermute | solution.py:355
  68.9 3.5 %shard_map.90.p = f32[3,256,512]{2,1,0:T(8,128)S(1)} custom-call(s32[2]{0:T(128)S(1)} %pad_add_fusion.where, bf16[256,2048]{1,0:T(8,128)(2,1)S(1)} %get-tuple-element.59.h, bf16[2048,2048]{1,0:T(8,128)(2,1)S(1)} %bitcast.12, bf16[2048,2048]{1,0:T(8,128)(2,1)S(1)} %bitcast.12), custom_call_target="tpu_custom_call" | custom-call | flops 1610612736 | bytes 19398656 | tf_op jit(solution)/shard_map/pallas_call | solution.py:33
  72.4 11.1 %collective-permute-done.9.left = f32[128,512]{1,0:T(8,128)S(1)} collective-permute-done((f32[128,512]{1,0:T(8,128)S(1)}, f32[128,512]{1,0:T(8,128)S(1)}, u32[]{:S(2)}, u32[]{:S(2)}) %collective-permute-start.9) | collective-permute-done | bytes 262176 | tf_op jit(solution)/shard_map/ppermute | solution.py:355
  84.2 2.2 collective-permute-start.11
  89.7 3.1 %collective-permute-done.10.right = f32[128,512]{1,0:T(8,128)S(1)} collective-permute-done((f32[128,512]{1,0:T(8,128)S(1)}, f32[128,512]{1,0:T(8,128)S(1)}, u32[]{:S(2)}, u32[]{:S(2)}) %collective-permute-start.10) | collective-permute-done | bytes 262176 | tf_op jit(solution)/shard_map/ppermute | solution.py:355
  94.1 4.3 %collective-permute-start.19 = (bf16[512,3072]{1,0:T(8,128)(2,1)}, bf16[512,3072]{1,0:T(8,128)(2,1)}, u32[]{:S(2)}, u32[]{:S(2)}) collective-permute-start(bf16[512,3072]{1,0:T(8,128)(2,1)} %all-gather.2.cloned.1.call-done.mine), channel_id=1, source_target_pairs={{0,1},{1,0},{2,3},{3,2},{4,5},{5,4},{6,7},{7,6},{8,9},{9,8},{10,11... | collective-permute-start | bytes 9437192 | tf_op jit(solution)/shard_map/ppermute | solution.py:358
  99.6 2.7 %collective-permute-start.15 = (f32[128,512]{1,0:T(8,128)}, f32[128,512]{1,0:T(8,128)S(1)}, u32[]{:S(2)}, u32[]{:S(2)}) collective-permute-start(f32[128,512]{1,0:T(8,128)} %copy-done.18), channel_id=1, source_target_pairs={{0,96},{32,0},{64,32},{96,64},{1,97},{33,1},{65,33},{97,65},{2,98}... | collective-permute-start | bytes 786440 | tf_op jit(solution)/shard_map/ppermute | solution.py:355
  104.1 1.9 copy-done.15
  105.9 11.6 %shard_map.94 = (bf16[768,3072]{1,0:T(8,128)(2,1)S(1)}, f32[768,512]{1,0:T(8,128)S(1)}) custom-call(s32[2]{0:T(128)S(1)} %pad_add_fusion.where, bf16[768,512]{1,0:T(8,128)(2,1)S(1)} %add_convert_fusion.2.pick_mine, bf16[768,512]{1,0:T(8,128)(2,1)S(1)} %add_convert_fusion.3.pick_other, bf16[512,3072]{1,0:T(8,128)(2,1)S(1)} %copy-done.15, ...), custom_call_target="tpu_custom_call" | custom-call | flops 7247757312 | bytes 17301504 | tf_op jit(solution)/shard_map/pallas_call | solution.py:33
  117.5 2.2 copy-done.20
  124.9 33.4 %all_to_all.15.parts = f32[64,8,768]{2,1,0:T(8,128)S(1)} all-to-all(f32[64,8,768]{2,1,0:T(8,128)S(1)} %shard_map.97), channel_id=1, replica_groups=mesh['x'=4,'y'=4,'z'=4,'c'=2] {'x','y','z'}, dimensions={0} | all-to-all | bytes 3145728 | tf_op jit(solution)/shard_map/all_to_all | solution.py:388
  158.3 2.4 %shard_map.98 = (bf16[512,512]{1,0:T(8,128)(2,1)S(1)}, bf16[512,1536]{1,0:T(8,128)(2,1)S(1)}, f32[8,128]{1,0:T(8,128)S(1)}) custom-call(s32[2]{0:T(128)S(1)} %pad_add_fusion.where, f32[64,8,768]{2,1,0:T(8,128)S(1)} %all_to_all.15.parts, f32[512,512]{1,0:T(8,128)S(1)} %get-tuple-element.75.tl, f32[768,512]{1,0:T(8,128)S(1)} %get-tuple-element.71.sl, ...), custom_call_target="tpu_custom_call" | custom-call | flops 805306368 | bytes 9441280 | tf_op jit(solution)/shard_map/pallas_call | solution.py:33
  160.7 2.7 %collective-permute-start.23 = (bf16[512,1536]{1,0:T(8,128)(2,1)S(1)}, bf16[512,1536]{1,0:T(8,128)(2,1)S(1)}, u32[]{:S(2)}, u32[]{:S(2)}) collective-permute-start(bf16[512,1536]{1,0:T(8,128)(2,1)S(1)} %get-tuple-element.78), channel_id=1, source_target_pairs={{0,1},{1,0},{2,3},{3,2},{4,5},{5,4},{6,7},{7,6},{8,9},{9,8},{10,11... | collective-permute-start | bytes 4718600 | tf_op jit(solution)/shard_map/ppermute | solution.py:358
  168.2 6.0 %all-to-all-start.1 = ((bf16[64,8,1536]{2,1,0:T(8,128)(2,1)}), bf16[64,8,1536]{2,1,0:T(8,128)(2,1)}, u32[]{:S(2)}, u32[]{:S(2)}) async-start(bf16[64,8,1536]{2,1,0:T(8,128)(2,1)} %fusion), calls=%async_computation.1 | async-start | bytes 3145728 | tf_op jit(solution)/shard_map/all_to_all | solution.py:397
  179.1 2.7 %shard_map.100 = (bf16[256,512]{1,0:T(8,128)(2,1)S(1)}, bf16[512,768]{1,0:T(8,128)(2,1)S(1)}, f32[8,128]{1,0:T(8,128)S(1)}) custom-call(s32[2]{0:T(128)S(1)} %pad_add_fusion.where, f32[64,8,768]{2,1,0:T(8,128)S(1)} %copy-done.8, f32[256,512]{1,0:T(8,128)S(1)} %copy-done.13, f32[768,512]{1,0:T(8,128)S(1)} %copy-done.6, bf16[3072,512]{1,0:T(8,128)(2,1)S(1)} %bitcast.16, ...), custom_call_target="tpu_custom_call" | custom-call | flops 402653184 | bytes 8392704 | tf_op jit(solution)/shard_map/pallas_call | solution.py:33
  182.3 2.0 shard_map.101
  185.4 10.9 %all-to-all-done.1 = bf16[64,8,1536]{2,1,0:T(8,128)(2,1)} async-done(((bf16[64,8,1536]{2,1,0:T(8,128)(2,1)}), bf16[64,8,1536]{2,1,0:T(8,128)(2,1)}, u32[]{:S(2)}, u32[]{:S(2)}) %all-to-all-start.1) | async-done | bytes 1572896 | tf_op jit(solution)/shard_map/all_to_all | solution.py:397
  196.3 6.2 %all-to-all-start.2 = ((bf16[64,8,768]{2,1,0:T(8,128)(2,1)}), bf16[64,8,768]{2,1,0:T(8,128)(2,1)S(1)}, u32[]{:S(2)}, u32[]{:S(2)}) async-start(bf16[64,8,768]{2,1,0:T(8,128)(2,1)} %fusion.3), calls=%async_computation.2 | async-start | bytes 1572864 | tf_op jit(solution)/shard_map/all_to_all | solution.py:397
  202.5 2.3 %copy-done.21 = bf16[768,3072]{1,0:T(8,128)(2,1)S(1)} copy-done((bf16[768,3072]{1,0:T(8,128)(2,1)S(1)}, bf16[768,3072]{1,0:T(8,128)(2,1)}, u32[]{:S(2)}) %copy-start.21) | copy-done | bytes 4718616
  204.9 8.8 %shard_map.102 = (f32[3072,1,512]{2,1,0:T(1,128)}, f32[8,128]{1,0:T(8,128)}) custom-call(s32[2]{0:T(128)S(1)} %pad_add_fusion.where, bf16[768,3072]{1,0:T(8,128)(2,1)S(1)} %copy-done.21, bf16[512,512]{1,0:T(8,128)(2,1)S(1)} %copy-done.11, bf16[256,512]{1,0:T(8,128)(2,1)S(1)} %get-tuple-element.86.g.gb), custom_call_target="tpu_custom_call" | custom-call | flops 2415919104 | bytes 11800576 | tf_op jit(solution)/shard_map/pallas_call | solution.py:33
  216.5 3.1 %collective-permute-start.25 = (bf16[6,1536]{1,0:T(8,128)(2,1)S(1)}, bf16[6,1536]{1,0:T(8,128)(2,1)S(1)}, u32[]{:S(2)}, u32[]{:S(2)}) collective-permute-start(bf16[6,1536]{1,0:T(8,128)(2,1)S(1)} %get-tuple-element.92), channel_id=1, source_target_pairs={{0,1},{1,0},{2,3},{3,2},{4,5},{5,4},{6,7},{7,6},{8,9},{9,8},{10,11... | collective-permute-start | bytes 55304 | tf_op jit(solution)/shard_map/ppermute | solution.py:358
  (117 shorter events, 42.2 us)
Async XLA Ops:
  7.2 86.9 %all-gather.2.cloned.1.call-start = ((), (), s32[]{:S(2)}) async-start(), calls=%async_computation.3 | async-start | bytes 3342336 | tf_op jit(solution)/shard_map/all_gather | solution.py:365
  11.3 4.6 %collective-permute-start.18 = (bf16[8,3072]{1,0:T(8,128)(2,1)S(1)}, bf16[8,3072]{1,0:T(8,128)(2,1)S(1)}, u32[]{:S(2)}, u32[]{:S(2)}) collective-permute-start(bf16[8,3072]{1,0:T(8,128)(2,1)S(1)} %pad.4), channel_id=1, source_target_pairs={{0,96},{32,0},{64,32},{96,64},{1,97},{33,1},{65,33},{97,65},{2,98}... | collective-permute-start | bytes 147464 | tf_op jit(solution)/shard_map/ppermute | solution.py:364
  14.7 4.5 %collective-permute-start.17 = (bf16[8,3072]{1,0:T(8,128)(2,1)S(1)}, bf16[8,3072]{1,0:T(8,128)(2,1)S(1)}, u32[]{:S(2)}, u32[]{:S(2)}) collective-permute-start(bf16[8,3072]{1,0:T(8,128)(2,1)S(1)} %pad.4), channel_id=1, source_target_pairs={{0,64},{32,96},{64,0},{96,32},{1,65},{33,97},{65,1},{97,33},{2,66}... | collective-permute-start | bytes 147464 | tf_op jit(solution)/shard_map/ppermute | solution.py:364
  15.2 4.5 %collective-permute-start.16 = (bf16[8,3072]{1,0:T(8,128)(2,1)S(1)}, bf16[8,3072]{1,0:T(8,128)(2,1)S(1)}, u32[]{:S(2)}, u32[]{:S(2)}) collective-permute-start(bf16[8,3072]{1,0:T(8,128)(2,1)S(1)} %pad.4), channel_id=1, source_target_pairs={{0,32},{32,64},{64,96},{96,0},{1,33},{33,65},{65,97},{97,1},{2,34}... | collective-permute-start | bytes 147464 | tf_op jit(solution)/shard_map/ppermute | solution.py:364
  20.4 10.4 %collective-permute-start = (bf16[96,2048]{1,0:T(8,128)(2,1)S(1)}, bf16[96,2048]{1,0:T(8,128)(2,1)S(1)}, u32[]{:S(2)}, u32[]{:S(2)}) collective-permute-start(bf16[96,2048]{1,0:T(8,128)(2,1)S(1)} %get-tuple-element.48), channel_id=1, source_target_pairs={{0,32},{32,64},{64,96},{96,0},{1,33},{33,65},{65,97},{97,1},{2,34}... | collective-permute-start | bytes 1179656 | tf_op jit(solution)/shard_map/ppermute | solution.py:361
  20.5 21.2 %collective-permute-start.1 = (bf16[96,2048]{1,0:T(8,128)(2,1)S(1)}, bf16[96,2048]{1,0:T(8,128)(2,1)S(1)}, u32[]{:S(2)}, u32[]{:S(2)}) collective-permute-start(bf16[96,2048]{1,0:T(8,128)(2,1)S(1)} %get-tuple-element.49), channel_id=1, source_target_pairs={{0,64},{32,96},{64,0},{96,32},{1,65},{33,97},{65,1},{97,33},{2,66}... | collective-permute-start | bytes 1179656 | tf_op jit(solution)/shard_map/ppermute | solution.py:361
  22.2 19.4 %collective-permute-start.2 = (bf16[96,2048]{1,0:T(8,128)(2,1)S(1)}, bf16[96,2048]{1,0:T(8,128)(2,1)S(1)}, u32[]{:S(2)}, u32[]{:S(2)}) collective-permute-start(bf16[96,2048]{1,0:T(8,128)(2,1)S(1)} %get-tuple-element.50), channel_id=1, source_target_pairs={{0,96},{32,0},{64,32},{96,64},{1,97},{33,1},{65,33},{97,65},{2,98}... | collective-permute-start | bytes 1179656 | tf_op jit(solution)/shard_map/ppermute | solution.py:361
  30.8 12.2 %collective-permute-start.3 = (bf16[96,2048]{1,0:T(8,128)(2,1)S(1)}, bf16[96,2048]{1,0:T(8,128)(2,1)S(1)}, u32[]{:S(2)}, u32[]{:S(2)}) collective-permute-start(bf16[96,2048]{1,0:T(8,128)(2,1)S(1)} %collective-permute-done.g1), channel_id=1, source_target_pairs={{0,1},{1,0},{2,3},{3,2},{4,5},{5,4},{6,7},{7,6},{8,9},{9,8},{10,11... | collective-permute-start | bytes 1179656 | tf_op jit(solution)/shard_map/ppermute | solution.py:358
  41.6 1.9 collective-permute-start.4
  41.7 2.5 %collective-permute-start.5 = (bf16[96,2048]{1,0:T(8,128)(2,1)S(1)}, bf16[96,2048]{1,0:T(8,128)(2,1)S(1)}, u32[]{:S(2)}, u32[]{:S(2)}) collective-permute-start(bf16[96,2048]{1,0:T(8,128)(2,1)S(1)} %collective-permute-done.2.g3), channel_id=1, source_target_pairs={{0,1},{1,0},{2,3},{3,2},{4,5},{5,4},{6,7},{7,6},{8,9},{9,8},{10,11... | collective-permute-start | bytes 1179656 | tf_op jit(solution)/shard_map/ppermute | solution.py:358
  50.3 13.3 %collective-permute-start.7 = (f32[256,512]{1,0:T(8,128)S(1)}, f32[256,512]{1,0:T(8,128)S(1)}, u32[]{:S(2)}, u32[]{:S(2)}) collective-permute-start(f32[256,512]{1,0:T(8,128)S(1)} %get-tuple-element.57), channel_id=1, source_target_pairs={{0,96},{32,0},{64,32},{96,64},{1,97},{33,1},{65,33},{97,65},{2,98}... | collective-permute-start | bytes 1572872 | tf_op jit(solution)/shard_map/ppermute | solution.py:355
  52.2 14.1 %collective-permute-start.6 = (f32[256,512]{1,0:T(8,128)S(1)}, f32[256,512]{1,0:T(8,128)S(1)}, u32[]{:S(2)}, u32[]{:S(2)}) collective-permute-start(f32[256,512]{1,0:T(8,128)S(1)} %get-tuple-element.51), channel_id=1, source_target_pairs={{0,32},{32,64},{64,96},{96,0},{1,33},{33,65},{65,97},{97,1},{2,34}... | collective-permute-start | bytes 1572872 | tf_op jit(solution)/shard_map/ppermute | solution.py:355
  54.5 29.1 %collective-permute-start.8 = (f32[128,512]{1,0:T(8,128)S(1)}, f32[128,512]{1,0:T(8,128)S(1)}, u32[]{:S(2)}, u32[]{:S(2)}) collective-permute-start(f32[128,512]{1,0:T(8,128)S(1)} %get-tuple-element.55), channel_id=1, source_target_pairs={{0,32},{32,64},{64,96},{96,0},{1,33},{33,65},{65,97},{97,1},{2,34}... | collective-permute-start | bytes 786440 | tf_op jit(solution)/shard_map/ppermute | solution.py:355
  67.0 19.4 %collective-permute-start.13 = (f32[256,512]{1,0:T(8,128)S(1)}, f32[256,512]{1,0:T(8,128)S(1)}, u32[]{:S(2)}, u32[]{:S(2)}) collective-permute-start(f32[256,512]{1,0:T(8,128)S(1)} %get-tuple-element.63), channel_id=1, source_target_pairs={{0,96},{32,0},{64,32},{96,64},{1,97},{33,1},{65,33},{97,65},{2,98}... | collective-permute-start | bytes 1572872 | tf_op jit(solution)/shard_map/ppermute | solution.py:355
  67.4 16.2 %collective-permute-start.9 = (f32[128,512]{1,0:T(8,128)S(1)}, f32[128,512]{1,0:T(8,128)S(1)}, u32[]{:S(2)}, u32[]{:S(2)}) collective-permute-start(f32[128,512]{1,0:T(8,128)S(1)} %get-tuple-element.60), channel_id=1, source_target_pairs={{0,96},{32,0},{64,32},{96,64},{1,97},{33,1},{65,33},{97,65},{2,98}... | collective-permute-start | bytes 786440 | tf_op jit(solution)/shard_map/ppermute | solution.py:355
  67.5 18.9 %collective-permute-start.12 = (f32[256,512]{1,0:T(8,128)S(1)}, f32[256,512]{1,0:T(8,128)S(1)}, u32[]{:S(2)}, u32[]{:S(2)}) collective-permute-start(f32[256,512]{1,0:T(8,128)S(1)} %get-tuple-element.58), channel_id=1, source_target_pairs={{0,32},{32,64},{64,96},{96,0},{1,33},{33,65},{65,97},{97,1},{2,34}... | collective-permute-start | bytes 1572872 | tf_op jit(solution)/shard_map/ppermute | solution.py:355
  72.4 20.4 %copy-start.3 = (f32[3,256,512]{2,1,0:T(8,128)}, f32[3,256,512]{2,1,0:T(8,128)S(1)}, u32[]{:S(2)}) copy-start(f32[3,256,512]{2,1,0:T(8,128)S(1)} %shard_map.90.p) | copy-start | bytes 4718596
  84.2 5.5 %collective-permute-start.11 = (f32[128,512]{1,0:T(8,128)S(1)}, f32[128,512]{1,0:T(8,128)S(1)}, u32[]{:S(2)}, u32[]{:S(2)}) collective-permute-start(f32[128,512]{1,0:T(8,128)S(1)} %get-tuple-element.62), channel_id=1, source_target_pairs={{0,96},{32,0},{64,32},{96,64},{1,97},{33,1},{65,33},{97,65},{2,98}... | collective-permute-start | bytes 786440 | tf_op jit(solution)/shard_map/ppermute | solution.py:355
  86.4 6.4 %collective-permute-start.10 = (f32[128,512]{1,0:T(8,128)S(1)}, f32[128,512]{1,0:T(8,128)S(1)}, u32[]{:S(2)}, u32[]{:S(2)}) collective-permute-start(f32[128,512]{1,0:T(8,128)S(1)} %get-tuple-element.61), channel_id=1, source_target_pairs={{0,32},{32,64},{64,96},{96,0},{1,33},{33,65},{65,97},{97,1},{2,34}... | collective-permute-start | bytes 786440 | tf_op jit(solution)/shard_map/ppermute | solution.py:355
  94.1 9.9 %collective-permute-start.19 = (bf16[512,3072]{1,0:T(8,128)(2,1)}, bf16[512,3072]{1,0:T(8,128)(2,1)}, u32[]{:S(2)}, u32[]{:S(2)}) collective-permute-start(bf16[512,3072]{1,0:T(8,128)(2,1)} %all-gather.2.cloned.1.call-done.mine), channel_id=1, source_target_pairs={{0,1},{1,0},{2,3},{3,2},{4,5},{5,4},{6,7},{7,6},{8,9},{9,8},{10,11... | collective-permute-start | bytes 9437192 | tf_op jit(solution)/shard_map/ppermute | solution.py:358
  99.4 21.8 %collective-permute-start.14 = (f32[128,512]{1,0:T(8,128)S(1)}, f32[128,512]{1,0:T(8,128)S(1)}, u32[]{:S(2)}, u32[]{:S(2)}) collective-permute-start(f32[128,512]{1,0:T(8,128)S(1)} %get-tuple-element.67), channel_id=1, source_target_pairs={{0,32},{32,64},{64,96},{96,0},{1,33},{33,65},{65,97},{97,1},{2,34}... | collective-permute-start | bytes 786440 | tf_op jit(solution)/shard_map/ppermute | solution.py:355
  99.5 20.4 %collective-permute-start.20 = (f32[256,512]{1,0:T(8,128)}, f32[256,512]{1,0:T(8,128)S(1)}, u32[]{:S(2)}, u32[]{:S(2)}) collective-permute-start(f32[256,512]{1,0:T(8,128)} %copy-done.16), channel_id=1, source_target_pairs={{0,32},{32,64},{64,96},{96,0},{1,33},{33,65},{65,97},{97,1},{2,34}... | collective-permute-start | bytes 1572872 | tf_op jit(solution)/shard_map/ppermute | solution.py:355
  99.6 21.7 %collective-permute-start.15 = (f32[128,512]{1,0:T(8,128)}, f32[128,512]{1,0:T(8,128)S(1)}, u32[]{:S(2)}, u32[]{:S(2)}) collective-permute-start(f32[128,512]{1,0:T(8,128)} %copy-done.18), channel_id=1, source_target_pairs={{0,96},{32,0},{64,32},{96,64},{1,97},{33,1},{65,33},{97,65},{2,98}... | collective-permute-start | bytes 786440 | tf_op jit(solution)/shard_map/ppermute | solution.py:355
  102.2 17.5 %collective-permute-start.21 = (f32[256,512]{1,0:T(8,128)}, f32[256,512]{1,0:T(8,128)S(1)}, u32[]{:S(2)}, u32[]{:S(2)}) collective-permute-start(f32[256,512]{1,0:T(8,128)} %copy-done.17), channel_id=1, source_target_pairs={{0,96},{32,0},{64,32},{96,64},{1,97},{33,1},{65,33},{97,65},{2,98}... | collective-permute-start | bytes 1572872 | tf_op jit(solution)/shard_map/ppermute | solution.py:355
  119.7 38.6 %copy-start.5 = (f32[768,512]{1,0:T(8,128)}, f32[768,512]{1,0:T(8,128)S(1)}, u32[]{:S(2)}) copy-start(f32[768,512]{1,0:T(8,128)S(1)} %get-tuple-element.71.sl) | copy-start | bytes 4718596
  122.7 35.6 %copy-start.12 = (f32[256,512]{1,0:T(8,128)}, f32[256,512]{1,0:T(8,128)S(1)}, u32[]{:S(2)}) copy-start(f32[256,512]{1,0:T(8,128)S(1)} %get-tuple-element.80.tl) | copy-start | bytes 1572868
  122.7 1.6 collective-permute-start.22
  160.7 5.8 %collective-permute-start.23 = (bf16[512,1536]{1,0:T(8,128)(2,1)S(1)}, bf16[512,1536]{1,0:T(8,128)(2,1)S(1)}, u32[]{:S(2)}, u32[]{:S(2)}) collective-permute-start(bf16[512,1536]{1,0:T(8,128)(2,1)S(1)} %get-tuple-element.78), channel_id=1, source_target_pairs={{0,1},{1,0},{2,3},{3,2},{4,5},{5,4},{6,7},{7,6},{8,9},{9,8},{10,11... | collective-permute-start | bytes 4718600 | tf_op jit(solution)/shard_map/ppermute | solution.py:358
  168.2 28.1 %all-to-all-start.1 = ((bf16[64,8,1536]{2,1,0:T(8,128)(2,1)}), bf16[64,8,1536]{2,1,0:T(8,128)(2,1)}, u32[]{:S(2)}, u32[]{:S(2)}) async-start(bf16[64,8,1536]{2,1,0:T(8,128)(2,1)} %fusion), calls=%async_computation.1 | async-start | bytes 3145728 | tf_op jit(solution)/shard_map/all_to_all | solution.py:397
  181.8 2.5 %collective-permute-start.24 = (bf16[512,768]{1,0:T(8,128)(2,1)S(1)}, bf16[512,768]{1,0:T(8,128)(2,1)S(1)}, u32[]{:S(2)}, u32[]{:S(2)}) collective-permute-start(bf16[512,768]{1,0:T(8,128)(2,1)S(1)} %get-tuple-element.84), channel_id=1, source_target_pairs={{0,1},{1,0},{2,3},{3,2},{4,5},{5,4},{6,7},{7,6},{8,9},{9,8},{10,11... | collective-permute-start | bytes 2359304 | tf_op jit(solution)/shard_map/ppermute | solution.py:358
  196.3 20.0 %all-to-all-start.2 = ((bf16[64,8,768]{2,1,0:T(8,128)(2,1)}), bf16[64,8,768]{2,1,0:T(8,128)(2,1)S(1)}, u32[]{:S(2)}, u32[]{:S(2)}) async-start(bf16[64,8,768]{2,1,0:T(8,128)(2,1)} %fusion.3), calls=%async_computation.2 | async-start | bytes 1572864 | tf_op jit(solution)/shard_map/all_to_all | solution.py:397
  216.5 5.4 %collective-permute-start.25 = (bf16[6,1536]{1,0:T(8,128)(2,1)S(1)}, bf16[6,1536]{1,0:T(8,128)(2,1)S(1)}, u32[]{:S(2)}, u32[]{:S(2)}) collective-permute-start(bf16[6,1536]{1,0:T(8,128)(2,1)S(1)} %get-tuple-element.92), channel_id=1, source_target_pairs={{0,1},{1,0},{2,3},{3,2},{4,5},{5,4},{6,7},{7,6},{8,9},{9,8},{10,11... | collective-permute-start | bytes 55304 | tf_op jit(solution)/shard_map/ppermute | solution.py:358
  (22 other events, 67.8 us)
Sparse Core Ops, SparseCore 0:
  20.5 50.0 all-gather.1

commit v2 on v0

v2 whole, which is shorter than its diff:
```python
import functools

import jax
import jax.numpy as jnp
import numpy as np
from jax import lax
from jax.experimental import pallas as pl
from jax.experimental.pallas import tpu as pltpu
from jax.sharding import Mesh
from jax.sharding import PartitionSpec as P

grad_scale = 64.0
ROWS = (8, 4)
ALL = ("x", "y", "z", "c")
CHIPS = ("x", "y", "z")
SWAP = [(0, 1), (1, 0)]
F32, BF16 = jnp.float32, jnp.bfloat16
NT = (((1,), (1,)), ((), ()))
TN = (((0,), (0,)), ((), ()))
MIB = 2**20


def shift(k):
    return [(i, (i + k) % 4) for i in range(4)]


def dot(a, b, dims=(((1,), (0,)), ((), ()))):
    return lax.dot_general(a, b, dims, preferred_element_type=F32)


def call(body, scalars, args, in_specs, outs, out_specs, grid=(1,), flops=0, after=(), spare=4, scratch=()):
    n = 1 + len(args)
    blocks = [(s.block_shape or (), a.dtype) for s, a in zip([*in_specs, *out_specs], [*args, *outs])]
    held = sum(int(np.prod(shape)) * dtype.itemsize for shape, dtype in blocks) * (1 if grid == (1,) else 2)

    def ordered(*refs):
        body(*refs[:n], *refs[n + len(after) :])

    return pl.pallas_call(
        ordered if after else body,
        out_shape=outs,
        grid_spec=pltpu.PrefetchScalarGridSpec(
            num_scalar_prefetch=1,
            grid=grid,
            in_specs=list(in_specs) + [pl.BlockSpec(memory_space=pl.ANY)] * len(after),
            out_specs=out_specs,
            scratch_shapes=scratch,
        ),
        compiler_params=pltpu.CompilerParams(vmem_limit_bytes=held + spare * MIB),
        cost_estimate=pl.CostEstimate(flops=flops, bytes_accessed=0, transcendentals=0),
    )(scalars, *args, *after)


def whole(shape):
    return pl.BlockSpec(shape, lambda *_: (0,) * len(shape))


def sds(shape, dtype):
    return jax.ShapeDtypeStruct(shape, dtype)


def cut_body(where, th, sh, own, s1, s2, s3):
    ks = th.shape[1] // 4
    x, c = where[0], where[1]
    def block(k):
        return th[:, pl.ds(pl.multiple_of(lax.rem(x + k, 4) * ks, ks), ks)]

    def one_hot(part, of):
        picks = []
        for m, start in zip(ROWS, (0, ROWS[0])):
            n = 16 * m // of
            i = lax.broadcasted_iota(jnp.int32, (n, th.shape[0]), 0) + part * n
            chip = lax.shift_right_logical(i, m.bit_length() - 1)
            row = chip * sum(ROWS) + start + jnp.bitwise_and(i, m - 1)
            picks.append(jnp.where(row == lax.broadcasted_iota(jnp.int32, row.shape, 1), 1.0, 0.0))
        return jnp.concatenate(picks, axis=0).astype(BF16)

    pick = one_hot(c, 2)
    for k, out in ((1, s1), (2, s2), (3, s3)):
        n = pick.shape[0]
        out[:n, :] = dot(pick, block(k)).astype(BF16)
        out[n:, :] = jnp.zeros((16, ks), BF16)
        m, d = sh.shape
        out[n : n + m, :] = sh[:, :ks]
        out[n + 8 : n + 8 + m, : d - ks] = sh[:, ks:]
    own[...] = dot(one_hot(0, 1), block(0)).astype(BF16)


def cut(where, th, sh):
    rows, d = th.shape
    ks = d // 4
    outs = [sds((rows, ks), BF16)] + [sds((rows // 2 + 16, ks), BF16)] * 3
    return call(
        cut_body, where, (th, sh), [whole(th.shape), whole(sh.shape)], outs, [whole(o.shape) for o in outs],
        flops=4 * rows * rows * d, spare=8,
    )


def pad_body(where, sh, out):
    out[...] = jnp.zeros_like(out)
    out[: sh.shape[0], :] = sh[...]


def pad_rows(where, sh):
    out = sds((8, sh.shape[1]), BF16)
    return call(pad_body, where, (sh,), [whole(sh.shape)], [out], [whole(out.shape)])[0]


def stack_body(piece, where, s0, g1, g2, g3, t0, o1, o2, o3, out, held):
    ks = g1.shape[1]
    at = 0
    for first, rest in ((s0, (g1, g2, g3)), (t0, (o1, o2, o3))):
        held[at : at + 8, :] = first[...]
        for k, ref in enumerate(rest):
            n = ref.shape[0] - 16
            to = at + 8 * k + 8
            held[to : to + 8, :ks] = ref[n : n + 8, :]
            held[to : to + 8, ks:] = ref[n + 8 :, : out.shape[1] - ks]
        at += 32
    row = lax.broadcasted_iota(jnp.int32, (out.shape[0], 64), 0)
    block = lax.shift_right_logical(row * 43, 8)
    source = row + (8 - piece) * block
    pick = jnp.where(source == lax.broadcasted_iota(jnp.int32, source.shape, 1), 1.0, 0.0).astype(BF16)
    out[...] = dot(pick, held[...]).astype(BF16)


def stack(where, piece, *pieces):
    d = pieces[0].shape[1]
    out = sds((8 * piece, d), BF16)
    specs = [whole(p.shape) for p in pieces]
    body = functools.partial(stack_body, piece)
    return call(body, where, pieces, specs, [out], [whole(out.shape)], scratch=[pltpu.VMEM((64, d), BF16)])[0]


def pick_body(piece, where, out):
    x, c = where[0], where[1]
    n = 64 * ROWS[0]
    for at, count, m, start in ((0, n, ROWS[0], 0), (n, 64 * ROWS[1], ROWS[1], ROWS[0])):
        i = lax.broadcasted_iota(jnp.int32, (count, 1), 0)
        bits = m.bit_length() - 1
        row = start + jnp.bitwise_and(i, m - 1)
        chip = jnp.bitwise_and(lax.shift_right_logical(i, bits), 15)
        k = jnp.bitwise_and(x + 4 - lax.shift_right_logical(i, bits + 4), 3)
        late = jnp.where(row >= piece, 1, 0)
        source = chip * (8 * piece) + jnp.where(late != c, 4 * piece, 0) + k * piece + row - piece * late
        col = lax.broadcasted_iota(jnp.int32, (count, out.shape[1]), 1)
        out[at : at + count, :] = jnp.where(col == source, 1.0, 0.0).astype(BF16)


def pick_of(where, piece, after):
    tokens = 64 * sum(ROWS)
    out = sds((tokens, tokens), BF16)
    body = functools.partial(pick_body, piece)
    return call(body, where, (), [], [out], [whole(out.shape)], after=after, spare=8)[0]


def columns(where, tw, step):
    n = tw.shape[1] // 4
    return tw[:, pl.ds(pl.multiple_of(lax.rem(where[0] + step, 4) * n, n), n)]


def gather_body(where, own, g1, g2, g3, o1, o2, o3, h):
    x, c = where[0], where[1]
    for m, start in zip(ROWS, (0, ROWS[0])):
        n = 16 * m
        nh = n // 2
        base, at = 64 * start, 16 * start
        h[pl.ds(pl.multiple_of(base + x * n, nh), n), :] = own[at : at + n, :]
        at = at // 2
        for k, (a, b) in enumerate(((g1, o1), (g2, o2), (g3, o3))):
            to = base + lax.rem(x + 3 - k, 4) * n
            h[pl.ds(pl.multiple_of(to + c * nh, nh), nh), :] = a[at : at + nh, :]
            h[pl.ds(pl.multiple_of(to + (1 - c) * nh, nh), nh), :] = b[at : at + nh, :]


def gather(where, own, got, other):
    out = sds((4 * own.shape[0], own.shape[1]), BF16)
    args = (own, *got, *other)
    return call(gather_body, where, args, [whole(a.shape) for a in args], [out], [whole(out.shape)])[0]


def rest_body(where, h, tw, out):
    half = h.shape[0] // 2
    out[0] = dot(h[...], columns(where, tw, 2))
    out[1, :half, :] = dot(h[:half, :], columns(where, tw, 1))
    out[1, half:, :] = dot(h[half:, :], columns(where, tw, 3))
    out[2] = dot(h[...], columns(where, tw, 0))


def rest(where, h, tw):
    rows, ks = h.shape
    cols = tw.shape[1] // 4
    out = sds((3, rows, cols), F32)
    specs = [whole(h.shape), whole(tw.shape)]
    return call(rest_body, where, (h, tw), specs, [out], [whole(out.shape)], flops=6 * rows * ks * cols, spare=6)[0]


def hop_body(where, p, right, left, r, l):
    half = right.shape[0]
    r[...] = p[0, :half, :] + right[...]
    l[...] = p[0, half:, :] + left[...]


def hop(where, p, step, right, left):
    half, cols = right.shape
    out = sds(right.shape, F32)
    specs = [pl.BlockSpec((1, 2 * half, cols), lambda i, w: (step, 0, 0)), whole(right.shape), whole(left.shape)]
    return call(hop_body, where, (p, right, left), specs, [out, out], [whole(out.shape)] * 2)


def student_body(where, pick, rows, w, hs, sl):
    block = dot(pick[...], rows[...]).astype(BF16)
    hs[...] = block

    @pl.when(pl.program_id(0) == 0)
    def _():
        sl[...] = jnp.zeros_like(sl)

    sl[...] += dot(block, w[...])


def student(where, pick, rows, w, after):
    tokens, room = pick.shape
    d, cols = w.shape
    tile = d // 6
    specs = [
        whole(pick.shape),
        pl.BlockSpec((room, tile), lambda i, s: (0, i)),
        pl.BlockSpec((tile, cols), lambda i, s: (i, 0)),
    ]
    outs = [sds((tokens, d), BF16), sds((tokens, cols), F32)]
    return call(
        student_body, where, (pick, rows, w), specs, outs,
        [pl.BlockSpec((tokens, tile), lambda i, s: (0, i)), whole(outs[1].shape)],
        grid=(6,), flops=2 * tokens * d * (room + cols), after=after, spare=6,
    )


def local_body(where, p, rr, lr, sl, tl, st):
    half, cols = rr.shape
    tl[:half, :] = p[0, :half, :] + rr[...]
    tl[half:, :] = p[0, half:, :] + lr[...]
    t, s = tl[...], sl[...]
    t_max = jnp.max(t, axis=1, keepdims=True)
    s_max = jnp.max(s, axis=1, keepdims=True)
    te = jnp.exp(t - t_max)
    t_sum = jnp.sum(te, axis=1, keepdims=True)
    cross = jnp.sum(te * (t - s), axis=1, keepdims=True)
    s_sum = jnp.sum(jnp.exp(s - s_max), axis=1, keepdims=True)
    lane = lax.broadcasted_iota(jnp.int32, (2 * half, 128), 1)
    packed = jnp.zeros((2 * half, 128), F32)
    for i, v in enumerate((t_max, t_sum, cross, s_max, s_sum)):
        packed = jnp.where(lane == i, v, packed)
    st[...] = jnp.transpose(packed)[:8, :]


def local(where, p, right, left, sl):
    outs = [sds(sl.shape, F32), sds((8, sl.shape[0]), F32)]
    args = (p, right, left, sl)
    specs = [pl.BlockSpec((1,) + sl.shape, lambda i, s: (2, 0, 0))] + [whole(a.shape) for a in args[1:]]
    return call(local_body, where, args, specs, outs, [whole(o.shape) for o in outs], flops=40 * sl.size, spare=10)


def merged(i, pieces):
    n = len(pieces)
    ordered = []
    for j in range(n):
        v = pieces[0]
        for k in range(1, n):
            v = jnp.where(lax.rem(i - j + n, n) == k, pieces[k], v)
        ordered.append(v)
    t_max = functools.reduce(jnp.maximum, [v[0:1] for v in ordered])
    s_max = functools.reduce(jnp.maximum, [v[3:4] for v in ordered])
    t_w = [jnp.exp(v[0:1] - t_max) for v in ordered]
    s_w = [jnp.exp(v[3:4] - s_max) for v in ordered]
    t_sum = sum(v[1:2] * a for v, a in zip(ordered, t_w))
    cross = sum(v[2:3] * a for v, a in zip(ordered, t_w))
    s_sum = sum(v[4:5] * a for v, a in zip(ordered, s_w))
    return [t_max, t_sum, cross, s_max, s_sum]


def merge_body(axis, where, *refs):
    pieces = [r[...] for r in refs[:-1]]
    rows = merged(where[axis], pieces)
    refs[-1][...] = jnp.concatenate(rows + [jnp.zeros_like(pieces[0][:3])], axis=0)


def merge(where, axis, *pieces):
    shape = pieces[0].shape
    body = functools.partial(merge_body, axis)
    return call(body, where, pieces, [whole(shape)] * len(pieces), [sds(shape, F32)], [whole(shape)])[0]


def back(grad, place, w):
    n = 64 * ROWS[0]
    half = w.shape[0] // 2
    b = grad[n:, :]
    low = dot(dot(place[0], b).astype(BF16), w[:half, :], NT)
    low += dot(dot(place[1], b).astype(BF16), w[half:, :], NT)
    return dot(grad[:n, :], w[...], NT), low


def grad_body(where, own, g1, g2, g3, tl, sl, place, w, g, away, kl):
    t_max, t_sum, cross, s_max, s_sum = merged(where[0], [own[...], g1[...], g2[...], g3[...]])
    rows = cross / t_sum - t_max - jnp.log(t_sum) + s_max + jnp.log(s_sum)
    kl[0, 0] = jnp.sum(rows) / rows.shape[1]
    stats = jnp.concatenate([t_max, grad_scale / t_sum, s_max, grad_scale / s_sum], axis=0)
    stats = jnp.concatenate([stats, jnp.zeros((124, stats.shape[1]), F32)], axis=0)
    cols = jnp.transpose(stats)
    s = jnp.exp(sl[...] - cols[:, 2:3]) * cols[:, 3:4]
    g[...] = (s - jnp.exp(tl[...] - cols[:, 0:1]) * cols[:, 1:2]).astype(BF16)
    split = w.shape[0]
    a, b = back(g[...], place, w)
    away[:, :split] = a.astype(BF16)
    away[:, split:] = b.astype(BF16)


def grad_of(where, pieces, tl, sl, place, w):
    tokens, cols = sl.shape
    d = w.shape[0]
    outs = [sds((tokens, cols), BF16), sds((512, d // 4 * 3), BF16), sds((1, 1), F32)]
    args = (*pieces, tl, sl, place, w)
    specs = [whole(a.shape) for a in args[:-1]] + [pl.BlockSpec((d // 2, cols), lambda i, s: (1 - s[1], 0))]
    out_specs = [whole(o.shape) for o in outs[:2]] + [pl.BlockSpec(memory_space=pltpu.SMEM)]
    return call(grad_body, where, args, specs, outs, out_specs, flops=tokens * cols * d, spare=16)


def keep_body(where, g, place, w, out):
    split = w.shape[0]
    a, b = back(g[...], place, w)
    out[:, :split] = a
    out[:, split:] = b


def keep_of(where, g, place, w):
    tokens, cols = g.shape
    d = w.shape[0]
    out = sds((512, d // 4 * 3), F32)
    specs = [whole(g.shape), whole(place.shape), pl.BlockSpec((d // 2, cols), lambda i, s: (s[1], 0))]
    return call(keep_body, where, (g, place, w), specs, [out], [whole(out.shape)], flops=tokens * cols * d, spare=12)[0]


def add_body(where, kept, got, out):
    out[...] = (kept[...] + got[...].astype(F32)).astype(BF16)


def add(where, kept, got):
    specs = [whole(kept.shape)] * 2
    return call(add_body, where, (kept, got), specs, [sds(kept.shape, BF16)], [whole(kept.shape)], spare=6)[0]


def total_body(where, parts, mine, theirs):
    both = jnp.sum(parts[...].astype(F32), axis=0)
    half = both.shape[1] // 3
    a, b = both[:, : 2 * half], both[:, 2 * half :]
    n = sum(ROWS) // 2
    late = jnp.concatenate([b[: ROWS[1]], b[ROWS[1] :]], axis=1)
    second = jnp.concatenate([a[n:], late, jnp.zeros_like(a[n:])], axis=0)
    mine[...] = jnp.where(where[1] == 0, a, second).astype(BF16)
    theirs[...] = jnp.where(where[1] == 0, second, a).astype(BF16)


def total(where, parts, after):
    out = sds((8, parts.shape[2] // 3 * 2), BF16)
    return call(total_body, where, (parts,), [whole(parts.shape)], [out, out], [whole(out.shape)] * 2, after=after, spare=10)


def join_body(where, mine, got, out):
    half = mine.shape[1]
    n = out.shape[0]
    out[:, pl.ds(pl.multiple_of(where[1] * half, half), half)] = mine[:n, :]
    out[:, pl.ds(pl.multiple_of((1 - where[1]) * half, half), half)] = got[:n, :]


def join(where, mine, got, shape):
    return call(join_body, where, (mine, got), [whole(mine.shape)] * 2, [sds(shape, BF16)], [whole(shape)])[0]


def weight_body(where, hs, g, out, done):
    out[...] = dot(hs[...], g[...], TN)[:, None, :]
    done[...] = jnp.zeros_like(done)


def weight_of(where, hs, g, after):
    tokens, d = hs.shape
    cols = g.shape[1]
    tile = 256
    outs = [sds((d, 1, cols), F32), sds((8, 128), F32)]
    specs = [pl.BlockSpec((tokens, tile), lambda i, s: (0, i)), whole(g.shape)]
    return call(
        weight_body, where, (hs, g), specs, outs,
        [pl.BlockSpec((tile, 1, cols), lambda i, s: (i, 0, 0)), whole((8, 128))],
        grid=(d // tile,), flops=2 * tokens * d * cols, after=after,
    )


def place_of(m):
    place = np.zeros((2, 64, 2, m, 64, m), np.float32)
    for chip in range(64):
        for r in range(m):
            for h in range(2):
                place[h, chip, h, r, chip, r] = 1.0
    return jnp.asarray(place.reshape(2, 128 * m, 64 * m), BF16)


def shards(th, tw, sh, sw):
    x = lax.axis_index("x")
    where = jnp.stack([lax.axis_index(a) for a in ("x", "c", "y", "z")]).astype(jnp.int32)
    piece = sh.shape[0]
    w = sw[:, 0, :]
    place = place_of(ROWS[1])

    def both_ways(r, l):
        return lax.ppermute(r, "x", shift(1)), lax.ppermute(l, "x", shift(-1))

    def others(v, axis):
        return [lax.ppermute(v, axis, shift(k)) for k in (1, 2, 3)]

    def swap(v):
        return lax.ppermute(v, "c", SWAP)

    own, *sends = cut(where, th, sh)
    got = [lax.ppermute(s, "x", shift(k + 1)) for k, s in enumerate(sends)]
    other = [swap(v) for v in got]

    sh8 = pad_rows(where, sh)
    every = lax.all_gather(stack(where, piece, sh8, *got, swap(sh8), *other), ("y", "z"), axis=0, tiled=True)
    h = gather(where, own, got, other)
    cols = tw.shape[1] // 4

    def product(rows, step):
        block = lax.dynamic_slice(tw, (0, (x + step) % 4 * cols), (tw.shape[0], cols))
        return jnp.dot(rows, block, preferred_element_type=F32)

    half = h.shape[0] // 2
    right, left = both_ways(product(h[:half], 3), product(h[half:], 1))
    p = rest(where, h, tw)
    r, l = hop(where, p, 0, right, left)
    right, left = both_ways(r, l)
    r, l = hop(where, p, 1, right, left)
    right, left = both_ways(r, l)
    pick = pick_of(where, piece, (p,))
    hs, sl = student(where, pick, every, w, (r,))
    tl, st = local(where, p, right, left, sl)

    st = merge(where, 1, st, swap(st))
    st = merge(where, 3, st, *others(st, "z"))
    st = merge(where, 2, st, *others(st, "y"))
    grad, away, kl = grad_of(where, [st, *others(st, "x")], tl, sl, place, w)
    got = swap(away)
    chip = add(where, keep_of(where, grad, place, w), got)
    parts = lax.all_to_all(chip.reshape(64, 8, -1), CHIPS, split_axis=0, concat_axis=0, tiled=True)
    grad_weight, done = weight_of(where, hs, grad, (chip,))
    mine, theirs = total(where, parts, (done,))
    grad_hidden = join(where, mine, swap(theirs), sh.shape)
    return (kl.reshape(()), grad_hidden, grad_weight)


def solution(mesh):
    mesh = Mesh(mesh.devices.reshape(4, 4, 4, 2), ALL)
    vocab = ("y", "z", "c")
    in_specs = (P("x", None), P("x", vocab), P(ALL, None), P(None, vocab, "x"))
    out_specs = (P(), P(ALL, None), P(None, vocab, "x"))
    return jax.shard_map(shards, mesh=mesh, in_specs=in_specs, out_specs=out_specs, check_vma=False)
```

time: 1070 us -> 205 us (0.19)
  blocking collectives: 486 us -> 0 us
  waiting for transfers between devices: 353 us -> 74.7 us
  local copies, waits for them, and re-layouts: 78.5 us -> 13.1 us
  Pallas kernels: 0 us -> 47.2 us
  starting transfers between devices: 90.7 us -> 49.3 us
  matrix products: 37.4 us -> 5.56 us
    unnamed x1 -> x0, blocking collectives: 359 us -> none
    all_gather x2 -> x1, waiting for transfers between devices: 352 us -> 2.93 us  [shards(): lax.all_gather(stack(where, piece, sh8, *got, swap(sh8), *other), ('y', '...]
    unnamed x32 -> x0, starting transfers between devices: 86.3 us -> none
    psum x1 -> x0, blocking collectives: 64.4 us -> none  [shards(): lax.psum((jnp.sum(t_exp, axis=1), jnp.sum(t_exp * (regrouped - student_lo...]
    pmax x1 -> x0, blocking collectives: 62.6 us -> none  [shards(): t_max, s_max = lax.pmax((t_local, s_local), ('seq', 'vocab'))]
    unnamed x42 -> x36, local copies, waits for them, and re-layouts: 72.3 us -> 13.1 us
    ppermute x0 -> x25, waiting for transfers between devices: none -> 54.1 us  [the longest x6 27.4 us: both_ways(): return (lax.ppermute(r, 'x', shift(1)), lax.ppermute(l, 'x', shift(-1)))]
    pallas_call x0 -> x19, Pallas kernels: none -> 47.2 us  [call(): pl.pallas_call(ordered if after else body, out_shape=outs, grid_spec=pltp...]
  transfers between devices with their start and end apart: 35 -> 27, of which waited for: 2 -> 17; matrix products, arithmetic and copies ran while one was open for 5% -> 3% of each run, Pallas kernels for 0% -> 15%
where the time goes in v2:
time: 205 us; the launch traced here: 204 us
  waiting for transfers between devices  74.7 us (36%)
  starting transfers between devices  49.3 us (24%)
  Pallas kernels  47.2 us (23%)
  between operations  14.3 us (7%)
  local copies, waits for them, and re-layouts  13.1 us (6%)
  matrix products  5.56 us (3%)
    pallas_call x19, Pallas kernels, call(): pl.pallas_call(ordered if after else body, out_shape=outs, grid_spec=pltp...  47.2 us
    ppermute x6, waiting for transfers between devices, both_ways(): return (lax.ppermute(r, 'x', shift(1)), lax.ppermute(l, 'x', shift(-1)))  27.4 us
    all_to_all x1, waiting for transfers between devices, shards(): lax.all_to_all(chip.reshape(64, 8, -1), CHIPS, split_axis=0, concat_axis=...  17.7 us
    ppermute x3, waiting for transfers between devices, shards(): got = [lax.ppermute(s, 'x', shift(k + 1)) for k, s in enumerate(sends)]  16.9 us
    ppermute x9, starting transfers between devices, others(): return [lax.ppermute(v, axis, shift(k)) for k in (1, 2, 3)]  14.1 us
    unnamed x36, local copies, waits for them, and re-layouts  13.1 us
    ppermute x7, starting transfers between devices, swap(): return lax.ppermute(v, 'c', SWAP)  12.9 us
    ppermute x6, starting transfers between devices, both_ways(): return (lax.ppermute(r, 'x', shift(1)), lax.ppermute(l, 'x', shift(-1)))  8.63 us
  transfers between devices with their start and end apart: 27, of which 17 were waited for; matrix products, arithmetic and copies ran while one was open for 3% of the time, Pallas kernels for 15%

profile of v2, /device:TPU:1, one launch (start us, length us, event | category | flops | bytes accessed | tf_op | source)
XLA Modules:
  0.0 204.3 jit_solution(4848040575659558068)
XLA Ops:
  8.1 1.9 copy-done.11
  11.2 2.1 %collective-permute-start = (bf16[112,2048]{1,0:T(8,128)(2,1)S(1)}, bf16[112,2048]{1,0:T(8,128)(2,1)S(1)}, u32[]{:S(2)}, u32[]{:S(2)}) collective-permute-start(bf16[112,2048]{1,0:T(8,128)(2,1)S(1)} %get-tuple-element.23), channel_id=1, source_target_pairs={{0,32},{32,64},{64,96},{96,0},{1,33},{33,65},{65,97},{97,1},{2,34}... | collective-permute-start | bytes 1376264 | tf_op jit(solution)/shard_map/ppermute | solution.py:423
  13.3 2.4 %collective-permute-start.1 = (bf16[112,2048]{1,0:T(8,128)(2,1)S(1)}, bf16[112,2048]{1,0:T(8,128)(2,1)S(1)}, u32[]{:S(2)}, u32[]{:S(2)}) collective-permute-start(bf16[112,2048]{1,0:T(8,128)(2,1)S(1)} %get-tuple-element.24), channel_id=1, source_target_pairs={{0,64},{32,96},{64,0},{96,32},{1,65},{33,97},{65,1},{97,33},{2,66}... | collective-permute-start | bytes 1376264 | tf_op jit(solution)/shard_map/ppermute | solution.py:423
  16.9 7.5 %collective-permute-done.g1 = bf16[112,2048]{1,0:T(8,128)(2,1)S(1)} collective-permute-done((bf16[112,2048]{1,0:T(8,128)(2,1)S(1)}, bf16[112,2048]{1,0:T(8,128)(2,1)S(1)}, u32[]{:S(2)}, u32[]{:S(2)}) %collective-permute-start) | collective-permute-done | bytes 458784 | tf_op jit(solution)/shard_map/ppermute | solution.py:423
  24.4 1.7 collective-permute-start.3
  26.1 9.4 %collective-permute-done.1.g2 = bf16[112,2048]{1,0:T(8,128)(2,1)S(1)} collective-permute-done((bf16[112,2048]{1,0:T(8,128)(2,1)S(1)}, bf16[112,2048]{1,0:T(8,128)(2,1)S(1)}, u32[]{:S(2)}, u32[]{:S(2)}) %collective-permute-start.1) | collective-permute-done | bytes 458784 | tf_op jit(solution)/shard_map/ppermute | solution.py:423
  41.6 3.0 %fusion.2 = f32[384,512]{1,0:T(8,128)S(1)} fusion(bf16[2048,2048]{1,0:T(8,128)(2,1)} %tw.1, s32[]{:T(128)S(6)} %select_n.18, bf16[768,2048]{1,0:T(8,128)(2,1)S(1)} %shard_map.77.h), kind=kOutput, calls=%fused_computation.2 | convolution fusion | flops 805306368 | bytes 4456452 | tf_op jit(solution)/shard_map/dot_general | solution.py:433
  45.3 2.6 %fusion = f32[384,512]{1,0:T(8,128)S(1)} fusion(bf16[2048,2048]{1,0:T(8,128)(2,1)} %tw.1, s32[]{:T(128)S(6)} %select_n.20, bf16[768,2048]{1,0:T(8,128)(2,1)S(1)} %shard_map.77.h), kind=kOutput, calls=%fused_computation | convolution fusion | flops 805306368 | bytes 4456452 | tf_op jit(solution)/shard_map/dot_general | solution.py:433
  47.9 2.1 %collective-permute-start.7 = (f32[384,512]{1,0:T(8,128)S(1)}, f32[384,512]{1,0:T(8,128)S(1)}, u32[]{:S(2)}, u32[]{:S(2)}) collective-permute-start(f32[384,512]{1,0:T(8,128)S(1)} %fusion), channel_id=1, source_target_pairs={{0,96},{32,0},{64,32},{96,64},{1,97},{33,1},{65,33},{97,65},{2,98}... | collective-permute-start | bytes 2359304 | tf_op jit(solution)/shard_map/ppermute | solution.py:414
  50.0 5.6 %shard_map.78.p.refs_1_ = f32[3,768,512]{2,1,0:T(8,128)S(1)} custom-call(s32[4]{0:T(128)S(1)} %pad_add_fusion.where.refs_0_, bf16[768,2048]{1,0:T(8,128)(2,1)S(1)} %shard_map.77.h, bf16[2048,2048]{1,0:T(8,128)(2,1)S(1)} %bitcast.14), custom_call_target="tpu_custom_call" | custom-call | flops 4831838208 | tf_op jit(solution)/shard_map/pallas_call | solution.py:39
  55.6 9.0 %collective-permute-done.6.right = f32[384,512]{1,0:T(8,128)S(1)} collective-permute-done((f32[384,512]{1,0:T(8,128)S(1)}, f32[384,512]{1,0:T(8,128)S(1)}, u32[]{:S(2)}, u32[]{:S(2)}) %collective-permute-start.6) | collective-permute-done | bytes 786464 | tf_op jit(solution)/shard_map/ppermute | solution.py:414
  64.6 2.0 %collective-permute-done.7.left = f32[384,512]{1,0:T(8,128)S(1)} collective-permute-done((f32[384,512]{1,0:T(8,128)S(1)}, f32[384,512]{1,0:T(8,128)S(1)}, u32[]{:S(2)}, u32[]{:S(2)}) %collective-permute-start.7) | collective-permute-done | bytes 786464 | tf_op jit(solution)/shard_map/ppermute | solution.py:414
  68.5 1.9 collective-permute-start.9
  70.5 16.3 %collective-permute-done.8.right = f32[384,512]{1,0:T(8,128)S(1)} collective-permute-done((f32[384,512]{1,0:T(8,128)S(1)}, f32[384,512]{1,0:T(8,128)S(1)}, u32[]{:S(2)}, u32[]{:S(2)}) %collective-permute-start.8) | collective-permute-done | bytes 786464 | tf_op jit(solution)/shard_map/ppermute | solution.py:414
  86.8 1.9 shard_map.80
  89.3 2.1 %collective-permute-start.11 = (f32[384,512]{1,0:T(8,128)}, f32[384,512]{1,0:T(8,128)}, u32[]{:S(2)}, u32[]{:S(2)}) collective-permute-start(f32[384,512]{1,0:T(8,128)} %get-tuple-element.29), channel_id=1, source_target_pairs={{0,96},{32,0},{64,32},{96,64},{1,97},{33,1},{65,33},{97,65},{2,98}... | collective-permute-start | bytes 2359304 | tf_op jit(solution)/shard_map/ppermute | solution.py:414
  93.3 2.9 %all-gather.2.cloned.1.call-done.refs_2_ = bf16[768,3072]{1,0:T(8,128)(2,1)} async-done(((bf16[48,3072]{1,0:T(8,128)(2,1)}), bf16[768,3072]{1,0:T(8,128)(2,1)}) %all-gather.2.cloned.1.call-update) | async-done | bytes 4718608 | tf_op jit(solution)/shard_map/all_gather | solution.py:427
  97.7 2.5 %copy-done.10 = bf16[768,3072]{1,0:T(8,128)(2,1)S(1)} copy-done((bf16[768,3072]{1,0:T(8,128)(2,1)S(1)}, bf16[768,3072]{1,0:T(8,128)(2,1)}, u32[]{:S(2)}) %copy-start.10) | copy-done | bytes 4718616
  100.2 9.5 %shard_map.84 = (bf16[768,3072]{1,0:T(8,128)(2,1)S(1)}, f32[768,512]{1,0:T(8,128)S(1)}) custom-call(s32[4]{0:T(128)S(1)} %pad_add_fusion.where.refs_0_, bf16[768,768]{1,0:T(8,128)(2,1)S(1)} %copy-done.6, bf16[768,3072]{1,0:T(8,128)(2,1)S(1)} %copy-done.10, bf16[3072,512]{1,0:T(8,128)(2,1)S(1)} %bitcast.9, f32[384,512]{1,0:T(8,128)} %get-tuple-element.28.refs_4_), custom_call_target="tpu_custom_call" | custom-call | flops 6039797760 | tf_op jit(solution)/shard_map/pallas_call | solution.py:39
  109.8 4.4 %shard_map.85 = (f32[768,512]{1,0:T(8,128)S(1)}, f32[8,768]{1,0:T(8,128)S(1)}) custom-call(s32[4]{0:T(128)S(1)} %pad_add_fusion.where.refs_0_, f32[3,768,512]{2,1,0:T(8,128)S(1)} %bitcast.8, f32[384,512]{1,0:T(8,128)} %collective-permute-done.10.rr, f32[384,512]{1,0:T(8,128)} %collective-permute-done.11.lr, f32[768,512]{1,0:T(8,128)S(1)} %get-tuple-element.30.sl), custom_call_target="tpu_custom_call" | custom-call | flops 15728640 | tf_op jit(solution)/shard_map/pallas_call | solution.py:39
  117.6 2.9 %collective-permute-start.15 = (f32[8,768]{1,0:T(8,128)S(1)}, f32[8,768]{1,0:T(8,128)S(1)}, u32[]{:S(2)}, u32[]{:S(2)}) collective-permute-start(f32[8,768]{1,0:T(8,128)S(1)} %shard_map.86.refs_0_), channel_id=1, source_target_pairs={{0,4},{2,6},{4,0},{6,2},{1,5},{3,7},{5,1},{7,3},{8,12},{10,14},{12... | collective-permute-start | bytes 73736 | tf_op jit(solution)/shard_map/ppermute | solution.py:417
  125.1 2.6 %collective-permute-start.18 = (f32[8,768]{1,0:T(8,128)S(1)}, f32[8,768]{1,0:T(8,128)S(1)}, u32[]{:S(2)}, u32[]{:S(2)}) collective-permute-start(f32[8,768]{1,0:T(8,128)S(1)} %shard_map.87.refs_0_), channel_id=1, source_target_pairs={{0,16},{8,24},{16,0},{24,8},{1,17},{9,25},{17,1},{25,9},{2,18},{10... | collective-permute-start | bytes 73736 | tf_op jit(solution)/shard_map/ppermute | solution.py:417
  131.5 3.0 %collective-permute-start.21 = (f32[8,768]{1,0:T(8,128)S(1)}, f32[8,768]{1,0:T(8,128)S(1)}, u32[]{:S(2)}, u32[]{:S(2)}) collective-permute-start(f32[8,768]{1,0:T(8,128)S(1)} %shard_map.88.own), channel_id=1, source_target_pairs={{0,64},{32,96},{64,0},{96,32},{1,65},{33,97},{65,1},{97,33},{2,66}... | collective-permute-start | bytes 73736 | tf_op jit(solution)/shard_map/ppermute | solution.py:417
  137.2 3.7 %shard_map.89 = (bf16[768,512]{1,0:T(8,128)(2,1)S(1)}, bf16[512,2304]{1,0:T(8,128)(2,1)S(1)}, f32[1,1]{1,0:T(1,128)}) custom-call(s32[4]{0:T(128)S(1)} %pad_add_fusion.where.refs_0_, f32[8,768]{1,0:T(8,128)S(1)} %shard_map.88.own, f32[8,768]{1,0:T(8,128)S(1)} %collective-permute-done.20.g1, f32[8,768]{1,0:T(8,128)S(1)} %collective-permute-done.21.g2, ...), custom_call_target="tpu_custom_call" | custom-call | flops 1207959552 | tf_op jit(solution)/shard_map/pallas_call | solution.py:39
  141.0 5.4 %collective-permute-start.23 = (bf16[512,2304]{1,0:T(8,128)(2,1)S(1)}, bf16[512,2304]{1,0:T(8,128)(2,1)S(1)}, u32[]{:S(2)}, u32[]{:S(2)}) collective-permute-start(bf16[512,2304]{1,0:T(8,128)(2,1)S(1)} %get-tuple-element.35), channel_id=1, source_target_pairs={{0,1},{1,0},{2,3},{3,2},{4,5},{5,4},{6,7},{7,6},{8,9},{9,8},{10,11... | collective-permute-start | bytes 7077896 | tf_op jit(solution)/shard_map/ppermute | solution.py:420
  146.4 2.6 %shard_map.90.kept = f32[512,2304]{1,0:T(8,128)S(1)} custom-call(s32[4]{0:T(128)S(1)} %pad_add_fusion.where.refs_0_, bf16[768,512]{1,0:T(8,128)(2,1)S(1)} %get-tuple-element.34.g.refs_2_, bf16[2,512,256]{2,1,0:T(8,128)(2,1)S(1)} %copy-done.4, bf16[3072,512]{1,0:T(8,128)(2,1)S(1)} %bitcast.11), custom_call_target="tpu_custom_call" | custom-call | flops 1207959552 | tf_op jit(solution)/shard_map/pallas_call | solution.py:39
  153.2 7.9 %all-to-all-start = ((bf16[64,8,2304]{2,1,0:T(8,128)(2,1)}), bf16[64,8,2304]{2,1,0:T(8,128)(2,1)S(1)}, u32[]{:S(2)}, u32[]{:S(2)}) async-start(bf16[64,8,2304]{2,1,0:T(8,128)(2,1)} %bitcast.12), calls=%async_computation | async-start | bytes 4718592 | tf_op jit(solution)/shard_map/all_to_all | solution.py:452
  161.1 1.7 copy-done.3
  162.8 2.3 %copy-done.13 = bf16[768,3072]{1,0:T(8,128)(2,1)S(1)} copy-done((bf16[768,3072]{1,0:T(8,128)(2,1)S(1)}, bf16[768,3072]{1,0:T(8,128)(2,1)}, u32[]{:S(2)}) %copy-start.13) | copy-done | bytes 4718616
  165.1 8.8 %shard_map.92 = (f32[3072,1,512]{2,1,0:T(1,128)}, f32[8,128]{1,0:T(8,128)S(1)}) custom-call(s32[4]{0:T(128)S(1)} %pad_add_fusion.where.refs_0_, bf16[768,3072]{1,0:T(8,128)(2,1)S(1)} %copy-done.13, bf16[768,512]{1,0:T(8,128)(2,1)S(1)} %copy-done.8, bf16[512,2304]{1,0:T(8,128)(2,1)S(1)} %copy-done.3), custom_call_target="tpu_custom_call" | custom-call | flops 2415919104 | tf_op jit(solution)/shard_map/pallas_call | solution.py:39
  173.9 17.7 %all-to-all-done.refs_1_ = bf16[64,8,2304]{2,1,0:T(8,128)(2,1)S(1)} async-done(((bf16[64,8,2304]{2,1,0:T(8,128)(2,1)}), bf16[64,8,2304]{2,1,0:T(8,128)(2,1)S(1)}, u32[]{:S(2)}, u32[]{:S(2)}) %all-to-all-start) | async-done | bytes 2359328 | tf_op jit(solution)/shard_map/all_to_all | solution.py:452
  192.5 2.9 %collective-permute-start.24 = (bf16[8,1536]{1,0:T(8,128)(2,1)S(1)}, bf16[8,1536]{1,0:T(8,128)(2,1)S(1)}, u32[]{:S(2)}, u32[]{:S(2)}) collective-permute-start(bf16[8,1536]{1,0:T(8,128)(2,1)S(1)} %get-tuple-element.39), channel_id=1, source_target_pairs={{0,1},{1,0},{2,3},{3,2},{4,5},{5,4},{6,7},{7,6},{8,9},{9,8},{10,11... | collective-permute-start | bytes 73736 | tf_op jit(solution)/shard_map/ppermute | solution.py:420
  (83 shorter events, 37.5 us)
Async XLA Ops:
  7.2 89.1 %all-gather.2.cloned.1.call-start = ((), (), s32[]{:S(2)}) async-start(), calls=%async_computation.1 | async-start | bytes 5013504 | tf_op jit(solution)/shard_map/all_gather | solution.py:427
  11.2 13.2 %collective-permute-start = (bf16[112,2048]{1,0:T(8,128)(2,1)S(1)}, bf16[112,2048]{1,0:T(8,128)(2,1)S(1)}, u32[]{:S(2)}, u32[]{:S(2)}) collective-permute-start(bf16[112,2048]{1,0:T(8,128)(2,1)S(1)} %get-tuple-element.23), channel_id=1, source_target_pairs={{0,32},{32,64},{64,96},{96,0},{1,33},{33,65},{65,97},{97,1},{2,34}... | collective-permute-start | bytes 1376264 | tf_op jit(solution)/shard_map/ppermute | solution.py:423
  13.3 22.2 %collective-permute-start.1 = (bf16[112,2048]{1,0:T(8,128)(2,1)S(1)}, bf16[112,2048]{1,0:T(8,128)(2,1)S(1)}, u32[]{:S(2)}, u32[]{:S(2)}) collective-permute-start(bf16[112,2048]{1,0:T(8,128)(2,1)S(1)} %get-tuple-element.24), channel_id=1, source_target_pairs={{0,64},{32,96},{64,0},{96,32},{1,65},{33,97},{65,1},{97,33},{2,66}... | collective-permute-start | bytes 1376264 | tf_op jit(solution)/shard_map/ppermute | solution.py:423
  15.8 21.3 %collective-permute-start.2 = (bf16[112,2048]{1,0:T(8,128)(2,1)S(1)}, bf16[112,2048]{1,0:T(8,128)(2,1)S(1)}, u32[]{:S(2)}, u32[]{:S(2)}) collective-permute-start(bf16[112,2048]{1,0:T(8,128)(2,1)S(1)} %get-tuple-element.25), channel_id=1, source_target_pairs={{0,96},{32,0},{64,32},{96,64},{1,97},{33,1},{65,33},{97,65},{2,98}... | collective-permute-start | bytes 1376264 | tf_op jit(solution)/shard_map/ppermute | solution.py:423
  24.4 14.9 %collective-permute-start.3 = (bf16[112,2048]{1,0:T(8,128)(2,1)S(1)}, bf16[112,2048]{1,0:T(8,128)(2,1)S(1)}, u32[]{:S(2)}, u32[]{:S(2)}) collective-permute-start(bf16[112,2048]{1,0:T(8,128)(2,1)S(1)} %collective-permute-done.g1), channel_id=1, source_target_pairs={{0,1},{1,0},{2,3},{3,2},{4,5},{5,4},{6,7},{7,6},{8,9},{9,8},{10,11... | collective-permute-start | bytes 1376264 | tf_op jit(solution)/shard_map/ppermute | solution.py:420
  35.5 3.7 %collective-permute-start.4 = (bf16[112,2048]{1,0:T(8,128)(2,1)S(1)}, bf16[112,2048]{1,0:T(8,128)(2,1)S(1)}, u32[]{:S(2)}, u32[]{:S(2)}) collective-permute-start(bf16[112,2048]{1,0:T(8,128)(2,1)S(1)} %collective-permute-done.1.g2), channel_id=1, source_target_pairs={{0,1},{1,0},{2,3},{3,2},{4,5},{5,4},{6,7},{7,6},{8,9},{9,8},{10,11... | collective-permute-start | bytes 1376264 | tf_op jit(solution)/shard_map/ppermute | solution.py:420
  37.1 2.2 %collective-permute-start.5 = (bf16[112,2048]{1,0:T(8,128)(2,1)S(1)}, bf16[112,2048]{1,0:T(8,128)(2,1)S(1)}, u32[]{:S(2)}, u32[]{:S(2)}) collective-permute-start(bf16[112,2048]{1,0:T(8,128)(2,1)S(1)} %collective-permute-done.2.g3), channel_id=1, source_target_pairs={{0,1},{1,0},{2,3},{3,2},{4,5},{5,4},{6,7},{7,6},{8,9},{9,8},{10,11... | collective-permute-start | bytes 1376264 | tf_op jit(solution)/shard_map/ppermute | solution.py:420
  37.6 1.6 collective-permute-start.12
  40.8 9.2 %slice-start.2 = ((s8[8388608]{0:T(1024)(128)(4,1)}), s8[4194304]{0:T(1024)(128)(4,1)S(1)}, s32[]{:S(2)}) async-start(s8[8388608]{0:T(1024)(128)(4,1)} %bitcast.13), calls=%async_computation.4 | async-start | bytes 8388608
  44.5 20.0 %collective-permute-start.6 = (f32[384,512]{1,0:T(8,128)S(1)}, f32[384,512]{1,0:T(8,128)S(1)}, u32[]{:S(2)}, u32[]{:S(2)}) collective-permute-start(f32[384,512]{1,0:T(8,128)S(1)} %fusion.2), channel_id=1, source_target_pairs={{0,32},{32,64},{64,96},{96,0},{1,33},{33,65},{65,97},{97,1},{2,34}... | collective-permute-start | bytes 2359304 | tf_op jit(solution)/shard_map/ppermute | solution.py:414
  47.9 18.7 %collective-permute-start.7 = (f32[384,512]{1,0:T(8,128)S(1)}, f32[384,512]{1,0:T(8,128)S(1)}, u32[]{:S(2)}, u32[]{:S(2)}) collective-permute-start(f32[384,512]{1,0:T(8,128)S(1)} %fusion), channel_id=1, source_target_pairs={{0,96},{32,0},{64,32},{96,64},{1,97},{33,1},{65,33},{97,65},{2,98}... | collective-permute-start | bytes 2359304 | tf_op jit(solution)/shard_map/ppermute | solution.py:414
  55.6 35.8 %copy-start = (f32[3,768,512]{2,1,0:T(8,128)}, f32[3,768,512]{2,1,0:T(8,128)S(1)}, u32[]{:S(2)}) copy-start(f32[3,768,512]{2,1,0:T(8,128)S(1)} %shard_map.78.p.refs_1_) | copy-start | bytes 14155780
  67.3 19.5 %collective-permute-start.8 = (f32[384,512]{1,0:T(8,128)S(1)}, f32[384,512]{1,0:T(8,128)S(1)}, u32[]{:S(2)}, u32[]{:S(2)}) collective-permute-start(f32[384,512]{1,0:T(8,128)S(1)} %get-tuple-element.26), channel_id=1, source_target_pairs={{0,32},{32,64},{64,96},{96,0},{1,33},{33,65},{65,97},{97,1},{2,34}... | collective-permute-start | bytes 2359304 | tf_op jit(solution)/shard_map/ppermute | solution.py:414
  68.5 18.3 %collective-permute-start.9 = (f32[384,512]{1,0:T(8,128)S(1)}, f32[384,512]{1,0:T(8,128)S(1)}, u32[]{:S(2)}, u32[]{:S(2)}) collective-permute-start(f32[384,512]{1,0:T(8,128)S(1)} %get-tuple-element.27), channel_id=1, source_target_pairs={{0,96},{32,0},{64,32},{96,64},{1,97},{33,1},{65,33},{97,65},{2,98}... | collective-permute-start | bytes 2359304 | tf_op jit(solution)/shard_map/ppermute | solution.py:414
  88.7 21.0 %collective-permute-start.10 = (f32[384,512]{1,0:T(8,128)}, f32[384,512]{1,0:T(8,128)}, u32[]{:S(2)}, u32[]{:S(2)}) collective-permute-start(f32[384,512]{1,0:T(8,128)} %get-tuple-element.28.refs_4_), channel_id=1, source_target_pairs={{0,32},{32,64},{64,96},{96,0},{1,33},{33,65},{65,97},{97,1},{2,34}... | collective-permute-start | bytes 2359304 | tf_op jit(solution)/shard_map/ppermute | solution.py:414
  89.3 20.5 %collective-permute-start.11 = (f32[384,512]{1,0:T(8,128)}, f32[384,512]{1,0:T(8,128)}, u32[]{:S(2)}, u32[]{:S(2)}) collective-permute-start(f32[384,512]{1,0:T(8,128)} %get-tuple-element.29), channel_id=1, source_target_pairs={{0,96},{32,0},{64,32},{96,64},{1,97},{33,1},{65,33},{97,65},{2,98}... | collective-permute-start | bytes 2359304 | tf_op jit(solution)/shard_map/ppermute | solution.py:414
  96.3 13.5 %slice-start = ((s8[4718592]{0:T(1024)(128)(4,1)}), s8[4194304]{0:T(1024)(128)(4,1)S(1)}, s32[]{:S(2)}) async-start(s8[4718592]{0:T(1024)(128)(4,1)} %bitcast.7), calls=%async_computation.2 | async-start | bytes 8388608
  100.2 9.5 %slice-start.1 = ((s8[4718592]{0:T(1024)(128)(4,1)}), s8[524288]{0:T(1024)(128)(4,1)S(1)}, s32[]{:S(2)}) async-start(s8[4718592]{0:T(1024)(128)(4,1)} %bitcast.7), calls=%async_computation.3 | async-start | bytes 1048576
  109.8 27.5 %copy-start.4 = (bf16[2,512,256]{2,1,0:T(8,128)(2,1)S(1)}, bf16[2,512,256]{2,1,0:T(8,128)(2,1)}, u32[]{:S(2)}) copy-start(bf16[2,512,256]{2,1,0:T(8,128)(2,1)} %constant.42.clone.place) | copy-start | bytes 1572868
  114.2 1.6 collective-permute-start.13
  116.4 4.8 %collective-permute-start.14 = (f32[8,768]{1,0:T(8,128)S(1)}, f32[8,768]{1,0:T(8,128)S(1)}, u32[]{:S(2)}, u32[]{:S(2)}) collective-permute-start(f32[8,768]{1,0:T(8,128)S(1)} %shard_map.86.refs_0_), channel_id=1, source_target_pairs={{0,2},{2,4},{4,6},{6,0},{1,3},{3,5},{5,7},{7,1},{8,10},{10,12},{12... | collective-permute-start | bytes 73736 | tf_op jit(solution)/shard_map/ppermute | solution.py:417
  117.6 4.3 %collective-permute-start.15 = (f32[8,768]{1,0:T(8,128)S(1)}, f32[8,768]{1,0:T(8,128)S(1)}, u32[]{:S(2)}, u32[]{:S(2)}) collective-permute-start(f32[8,768]{1,0:T(8,128)S(1)} %shard_map.86.refs_0_), channel_id=1, source_target_pairs={{0,4},{2,6},{4,0},{6,2},{1,5},{3,7},{5,1},{7,3},{8,12},{10,14},{12... | collective-permute-start | bytes 73736 | tf_op jit(solution)/shard_map/ppermute | solution.py:417
  120.4 2.7 %collective-permute-start.16 = (f32[8,768]{1,0:T(8,128)S(1)}, f32[8,768]{1,0:T(8,128)S(1)}, u32[]{:S(2)}, u32[]{:S(2)}) collective-permute-start(f32[8,768]{1,0:T(8,128)S(1)} %shard_map.86.refs_0_), channel_id=1, source_target_pairs={{0,6},{2,0},{4,2},{6,4},{1,7},{3,1},{5,3},{7,5},{8,14},{10,8},{12,... | collective-permute-start | bytes 73736 | tf_op jit(solution)/shard_map/ppermute | solution.py:417
  123.7 5.0 %collective-permute-start.17 = (f32[8,768]{1,0:T(8,128)S(1)}, f32[8,768]{1,0:T(8,128)S(1)}, u32[]{:S(2)}, u32[]{:S(2)}) collective-permute-start(f32[8,768]{1,0:T(8,128)S(1)} %shard_map.87.refs_0_), channel_id=1, source_target_pairs={{0,8},{8,16},{16,24},{24,0},{1,9},{9,17},{17,25},{25,1},{2,10},{10... | collective-permute-start | bytes 73736 | tf_op jit(solution)/shard_map/ppermute | solution.py:417
  125.1 4.2 %collective-permute-start.18 = (f32[8,768]{1,0:T(8,128)S(1)}, f32[8,768]{1,0:T(8,128)S(1)}, u32[]{:S(2)}, u32[]{:S(2)}) collective-permute-start(f32[8,768]{1,0:T(8,128)S(1)} %shard_map.87.refs_0_), channel_id=1, source_target_pairs={{0,16},{8,24},{16,0},{24,8},{1,17},{9,25},{17,1},{25,9},{2,18},{10... | collective-permute-start | bytes 73736 | tf_op jit(solution)/shard_map/ppermute | solution.py:417
  127.7 2.8 %collective-permute-start.19 = (f32[8,768]{1,0:T(8,128)S(1)}, f32[8,768]{1,0:T(8,128)S(1)}, u32[]{:S(2)}, u32[]{:S(2)}) collective-permute-start(f32[8,768]{1,0:T(8,128)S(1)} %shard_map.87.refs_0_), channel_id=1, source_target_pairs={{0,24},{8,0},{16,8},{24,16},{1,25},{9,1},{17,9},{25,17},{2,26},{10... | collective-permute-start | bytes 73736 | tf_op jit(solution)/shard_map/ppermute | solution.py:417
  131.1 4.3 %collective-permute-start.20 = (f32[8,768]{1,0:T(8,128)S(1)}, f32[8,768]{1,0:T(8,128)S(1)}, u32[]{:S(2)}, u32[]{:S(2)}) collective-permute-start(f32[8,768]{1,0:T(8,128)S(1)} %shard_map.88.own), channel_id=1, source_target_pairs={{0,32},{32,64},{64,96},{96,0},{1,33},{33,65},{65,97},{97,1},{2,34}... | collective-permute-start | bytes 73736 | tf_op jit(solution)/shard_map/ppermute | solution.py:417
  131.5 4.5 %collective-permute-start.21 = (f32[8,768]{1,0:T(8,128)S(1)}, f32[8,768]{1,0:T(8,128)S(1)}, u32[]{:S(2)}, u32[]{:S(2)}) collective-permute-start(f32[8,768]{1,0:T(8,128)S(1)} %shard_map.88.own), channel_id=1, source_target_pairs={{0,64},{32,96},{64,0},{96,32},{1,65},{33,97},{65,1},{97,33},{2,66}... | collective-permute-start | bytes 73736 | tf_op jit(solution)/shard_map/ppermute | solution.py:417
  134.5 2.7 %collective-permute-start.22 = (f32[8,768]{1,0:T(8,128)S(1)}, f32[8,768]{1,0:T(8,128)S(1)}, u32[]{:S(2)}, u32[]{:S(2)}) collective-permute-start(f32[8,768]{1,0:T(8,128)S(1)} %shard_map.88.own), channel_id=1, source_target_pairs={{0,96},{32,0},{64,32},{96,64},{1,97},{33,1},{65,33},{97,65},{2,98}... | collective-permute-start | bytes 73736 | tf_op jit(solution)/shard_map/ppermute | solution.py:417
  141.0 9.6 %collective-permute-start.23 = (bf16[512,2304]{1,0:T(8,128)(2,1)S(1)}, bf16[512,2304]{1,0:T(8,128)(2,1)S(1)}, u32[]{:S(2)}, u32[]{:S(2)}) collective-permute-start(bf16[512,2304]{1,0:T(8,128)(2,1)S(1)} %get-tuple-element.35), channel_id=1, source_target_pairs={{0,1},{1,0},{2,3},{3,2},{4,5},{5,4},{6,7},{7,6},{8,9},{9,8},{10,11... | collective-permute-start | bytes 7077896 | tf_op jit(solution)/shard_map/ppermute | solution.py:420
  153.2 38.4 %all-to-all-start = ((bf16[64,8,2304]{2,1,0:T(8,128)(2,1)}), bf16[64,8,2304]{2,1,0:T(8,128)(2,1)S(1)}, u32[]{:S(2)}, u32[]{:S(2)}) async-start(bf16[64,8,2304]{2,1,0:T(8,128)(2,1)} %bitcast.12), calls=%async_computation | async-start | bytes 4718592 | tf_op jit(solution)/shard_map/all_to_all | solution.py:452
  192.5 3.7 %collective-permute-start.24 = (bf16[8,1536]{1,0:T(8,128)(2,1)S(1)}, bf16[8,1536]{1,0:T(8,128)(2,1)S(1)}, u32[]{:S(2)}, u32[]{:S(2)}) collective-permute-start(bf16[8,1536]{1,0:T(8,128)(2,1)S(1)} %get-tuple-element.39), channel_id=1, source_target_pairs={{0,1},{1,0},{2,3},{3,2},{4,5},{5,4},{6,7},{7,6},{8,9},{9,8},{10,11... | collective-permute-start | bytes 73736 | tf_op jit(solution)/shard_map/ppermute | solution.py:420
  (13 other events, 49.6 us)
Sparse Core Ops, SparseCore 0:
  40.9 55.3 all-gather.1

commit v3 on v2

--- a/solution.py
+++ b/solution.py
@@ -59,7 +59,7 @@
     return jax.ShapeDtypeStruct(shape, dtype)
 
 
-def cut_body(where, th, sh, own, s1, s2, s3):
+def cut_body(where, th, sh, own, s1, s2, s3, sh8):
     ks = th.shape[1] // 4
     x, c = where[0], where[1]
     def block(k):
@@ -84,56 +84,46 @@
         out[n : n + m, :] = sh[:, :ks]
         out[n + 8 : n + 8 + m, : d - ks] = sh[:, ks:]
     own[...] = dot(one_hot(0, 1), block(0)).astype(BF16)
+    sh8[...] = jnp.zeros_like(sh8)
+    sh8[: sh.shape[0], :] = sh[...]
 
 
 def cut(where, th, sh):
     rows, d = th.shape
     ks = d // 4
-    outs = [sds((rows, ks), BF16)] + [sds((rows // 2 + 16, ks), BF16)] * 3
+    outs = [sds((rows, ks), BF16)] + [sds((rows // 2 + 16, ks), BF16)] * 3 + [sds((8, sh.shape[1]), BF16)]
     return call(
         cut_body, where, (th, sh), [whole(th.shape), whole(sh.shape)], outs, [whole(o.shape) for o in outs],
         flops=4 * rows * rows * d, spare=8,
     )
 
 
-def pad_body(where, sh, out):
-    out[...] = jnp.zeros_like(out)
-    out[: sh.shape[0], :] = sh[...]
-
-
-def pad_rows(where, sh):
-    out = sds((8, sh.shape[1]), BF16)
-    return call(pad_body, where, (sh,), [whole(sh.shape)], [out], [whole(out.shape)])[0]
-
-
-def stack_body(piece, where, s0, g1, g2, g3, t0, o1, o2, o3, out, held):
+def stack_body(piece, where, s0, g1, g2, g3, out, held):
     ks = g1.shape[1]
-    at = 0
-    for first, rest in ((s0, (g1, g2, g3)), (t0, (o1, o2, o3))):
-        held[at : at + 8, :] = first[...]
-        for k, ref in enumerate(rest):
-            n = ref.shape[0] - 16
-            to = at + 8 * k + 8
-            held[to : to + 8, :ks] = ref[n : n + 8, :]
-            held[to : to + 8, ks:] = ref[n + 8 :, : out.shape[1] - ks]
-        at += 32
-    row = lax.broadcasted_iota(jnp.int32, (out.shape[0], 64), 0)
-    block = lax.shift_right_logical(row * 43, 8)
-    source = row + (8 - piece) * block
+    held[:8, :] = s0[...]
+    for k, ref in enumerate((g1, g2, g3)):
+        n = ref.shape[0] - 16
+        to = 8 * k + 8
+        held[to : to + 8, :ks] = ref[n : n + 8, :]
+        held[to : to + 8, ks:] = ref[n + 8 :, : out.shape[1] - ks]
+    row = lax.broadcasted_iota(jnp.int32, (out.shape[0], 32), 0)
+    source = row
+    for k in (1, 2, 3):
+        source += jnp.where(row >= k * piece, 8 - piece, 0)
     pick = jnp.where(source == lax.broadcasted_iota(jnp.int32, source.shape, 1), 1.0, 0.0).astype(BF16)
     out[...] = dot(pick, held[...]).astype(BF16)
 
 
 def stack(where, piece, *pieces):
     d = pieces[0].shape[1]
-    out = sds((8 * piece, d), BF16)
+    out = sds((4 * piece, d), BF16)
     specs = [whole(p.shape) for p in pieces]
     body = functools.partial(stack_body, piece)
-    return call(body, where, pieces, specs, [out], [whole(out.shape)], scratch=[pltpu.VMEM((64, d), BF16)])[0]
+    return call(body, where, pieces, specs, [out], [whole(out.shape)], scratch=[pltpu.VMEM((32, d), BF16)])[0]
 
 
 def pick_body(piece, where, out):
-    x, c = where[0], where[1]
+    x = where[0]
     n = 64 * ROWS[0]
     for at, count, m, start in ((0, n, ROWS[0], 0), (n, 64 * ROWS[1], ROWS[1], ROWS[0])):
         i = lax.broadcasted_iota(jnp.int32, (count, 1), 0)
@@ -142,7 +132,7 @@
         chip = jnp.bitwise_and(lax.shift_right_logical(i, bits), 15)
         k = jnp.bitwise_and(x + 4 - lax.shift_right_logical(i, bits + 4), 3)
         late = jnp.where(row >= piece, 1, 0)
-        source = chip * (8 * piece) + jnp.where(late != c, 4 * piece, 0) + k * piece + row - piece * late
+        source = chip * (8 * piece) + late * (4 * piece) + k * piece + row - piece * late
         col = lax.broadcasted_iota(jnp.int32, (count, out.shape[1]), 1)
         out[at : at + count, :] = jnp.where(col == source, 1.0, 0.0).astype(BF16)
 
@@ -195,51 +185,60 @@
     return call(rest_body, where, (h, tw), specs, [out], [whole(out.shape)], flops=6 * rows * ks * cols, spare=6)[0]
 
 
-def hop_body(where, p, right, left, r, l):
-    half = right.shape[0]
-    r[...] = p[0, :half, :] + right[...]
-    l[...] = p[0, half:, :] + left[...]
-
-
-def hop(where, p, step, right, left):
-    half, cols = right.shape
+def hop_body(where, pr, pl_, right, left, r, l):
+    r[...] = pr[0] + right[...]
+    l[...] = pl_[0] + left[...]
+
+
+def hop(where, p, step, i, right, left, after=(), flops=0):
+    n, cols = right.shape
     out = sds(right.shape, F32)
-    specs = [pl.BlockSpec((1, 2 * half, cols), lambda i, w: (step, 0, 0)), whole(right.shape), whole(left.shape)]
-    return call(hop_body, where, (p, right, left), specs, [out, out], [whole(out.shape)] * 2)
-
-
-def student_body(where, pick, rows, w, hs, sl):
-    block = dot(pick[...], rows[...]).astype(BF16)
-    hs[...] = block
-
+    specs = [pl.BlockSpec((1, n, cols), lambda _, w, j=j: (step, j, 0)) for j in (i, i + 2)]
+    specs += [whole(right.shape), whole(left.shape)]
+    return call(hop_body, where, (p, p, right, left), specs, [out, out], [whole(out.shape)] * 2, after=after, flops=flops)
+
+
+def student_body(where, pick, rows, w, sl, total):
     @pl.when(pl.program_id(0) == 0)
     def _():
-        sl[...] = jnp.zeros_like(sl)
-
-    sl[...] += dot(block, w[...])
+        total[...] = jnp.zeros_like(total)
+
+    total[...] += dot(rows[...], w[...])
+
+    @pl.when(pl.program_id(0) == pl.num_programs(0) - 1)
+    def _():
+        rest = total[...]
+        out = jnp.zeros_like(rest)
+        for _ in range(3):
+            part = rest.astype(BF16)
+            out += dot(pick[...], part)
+            rest -= part.astype(F32)
+        sl[...] = out
 
 
 def student(where, pick, rows, w, after):
-    tokens, room = pick.shape
-    d, cols = w.shape
+    tokens, d = rows.shape
+    cols = w.shape[1]
     tile = d // 6
     specs = [
         whole(pick.shape),
-        pl.BlockSpec((room, tile), lambda i, s: (0, i)),
+        pl.BlockSpec((tokens, tile), lambda i, s: (0, i)),
         pl.BlockSpec((tile, cols), lambda i, s: (i, 0)),
     ]
-    outs = [sds((tokens, d), BF16), sds((tokens, cols), F32)]
+    out = sds((tokens, cols), F32)
     return call(
-        student_body, where, (pick, rows, w), specs, outs,
-        [pl.BlockSpec((tokens, tile), lambda i, s: (0, i)), whole(outs[1].shape)],
-        grid=(6,), flops=2 * tokens * d * (room + cols), after=after, spare=6,
-    )
-
-
-def local_body(where, p, rr, lr, sl, tl, st):
-    half, cols = rr.shape
-    tl[:half, :] = p[0, :half, :] + rr[...]
-    tl[half:, :] = p[0, half:, :] + lr[...]
+        student_body, where, (pick, rows, w), specs, [out], [whole(out.shape)],
+        grid=(6,), after=after, spare=8, scratch=[pltpu.VMEM(out.shape, F32)],
+    )[0]
+
+
+def local_body(where, p, r0, l0, r1, l1, sl, tl, st):
+    n = r0.shape[0]
+    half = 2 * n
+    tl[:n, :] = r0[...]
+    tl[2 * n : 3 * n, :] = l0[...]
+    tl[n : 2 * n, :] = p[0, n : 2 * n, :] + r1[...]
+    tl[3 * n :, :] = p[0, 3 * n :, :] + l1[...]
     t, s = tl[...], sl[...]
     t_max = jnp.max(t, axis=1, keepdims=True)
     s_max = jnp.max(s, axis=1, keepdims=True)
@@ -254,9 +253,9 @@
     st[...] = jnp.transpose(packed)[:8, :]
 
 
-def local(where, p, right, left, sl):
+def local(where, p, chains, sl):
     outs = [sds(sl.shape, F32), sds((8, sl.shape[0]), F32)]
-    args = (p, right, left, sl)
+    args = (p, *chains, sl)
     specs = [pl.BlockSpec((1,) + sl.shape, lambda i, s: (2, 0, 0))] + [whole(a.shape) for a in args[1:]]
     return call(local_body, where, args, specs, outs, [whole(o.shape) for o in outs], flops=40 * sl.size, spare=10)
 
@@ -376,21 +375,25 @@
     return call(join_body, where, (mine, got), [whole(mine.shape)] * 2, [sds(shape, BF16)], [whole(shape)])[0]
 
 
-def weight_body(where, hs, g, out, done):
-    out[...] = dot(hs[...], g[...], TN)[:, None, :]
+def weight_body(where, rows, g, pick, out, done, placed):
+    @pl.when(pl.program_id(0) == 0)
+    def _():
+        placed[...] = dot(pick[...], g[...], TN).astype(BF16)
+
+    out[...] = dot(rows[...], placed[...], TN)[:, None, :]
     done[...] = jnp.zeros_like(done)
 
 
-def weight_of(where, hs, g, after):
-    tokens, d = hs.shape
+def weight_of(where, rows, g, pick, after):
+    tokens, d = rows.shape
     cols = g.shape[1]
     tile = 256
     outs = [sds((d, 1, cols), F32), sds((8, 128), F32)]
-    specs = [pl.BlockSpec((tokens, tile), lambda i, s: (0, i)), whole(g.shape)]
+    specs = [pl.BlockSpec((tokens, tile), lambda i, s: (0, i)), whole(g.shape), whole(pick.shape)]
     return call(
-        weight_body, where, (hs, g), specs, outs,
+        weight_body, where, (rows, g, pick), specs, outs,
         [pl.BlockSpec((tile, 1, cols), lambda i, s: (i, 0, 0)), whole((8, 128))],
-        grid=(d // tile,), flops=2 * tokens * d * cols, after=after,
+        grid=(d // tile,), flops=2 * tokens * d * cols, after=after, scratch=[pltpu.VMEM(g.shape, BF16)],
     )
 
 
@@ -419,12 +422,11 @@
     def swap(v):
         return lax.ppermute(v, "c", SWAP)
 
-    own, *sends = cut(where, th, sh)
+    own, *sends, sh8 = cut(where, th, sh)
     got = [lax.ppermute(s, "x", shift(k + 1)) for k, s in enumerate(sends)]
     other = [swap(v) for v in got]
 
-    sh8 = pad_rows(where, sh)
-    every = lax.all_gather(stack(where, piece, sh8, *got, swap(sh8), *other), ("y", "z"), axis=0, tiled=True)
+    every = lax.all_gather(stack(where, piece, sh8, *got), ("y", "z", "c"), axis=0, tiled=True)
     h = gather(where, own, got, other)
     cols = tw.shape[1] // 4
 
@@ -432,16 +434,19 @@
         block = lax.dynamic_slice(tw, (0, (x + step) % 4 * cols), (tw.shape[0], cols))
         return jnp.dot(rows, block, preferred_element_type=F32)
 
-    half = h.shape[0] // 2
-    right, left = both_ways(product(h[:half], 3), product(h[half:], 1))
+    n = h.shape[0] // 4
+    chains = [both_ways(product(h[i * n : (i + 1) * n], 3), product(h[(i + 2) * n : (i + 3) * n], 1)) for i in (0, 1)]
     p = rest(where, h, tw)
-    r, l = hop(where, p, 0, right, left)
-    right, left = both_ways(r, l)
-    r, l = hop(where, p, 1, right, left)
-    right, left = both_ways(r, l)
     pick = pick_of(where, piece, (p,))
-    hs, sl = student(where, pick, every, w, (r,))
-    tl, st = local(where, p, right, left, sl)
+    before = ()
+    for step in (0, 1):
+        for i in (0, 1):
+            r, l = hop(where, p, step, i, *chains[i], before)
+            chains[i] = both_ways(r, l)
+            before = (r, pick)
+    sl = student(where, pick, every, w, before[:1])
+    whole_sums = hop(where, p, 2, 0, *chains[0], (sl,), flops=6 * 10**9)
+    tl, st = local(where, p, [*whole_sums, *chains[1]], sl)
 
     st = merge(where, 1, st, swap(st))
     st = merge(where, 3, st, *others(st, "z"))
@@ -450,7 +455,7 @@
     got = swap(away)
     chip = add(where, keep_of(where, grad, place, w), got)
     parts = lax.all_to_all(chip.reshape(64, 8, -1), CHIPS, split_axis=0, concat_axis=0, tiled=True)
-    grad_weight, done = weight_of(where, hs, grad, (chip,))
+    grad_weight, done = weight_of(where, every, grad, pick, (chip,))
     mine, theirs = total(where, parts, (done,))
     grad_hidden = join(where, mine, swap(theirs), sh.shape)
     return (kl.reshape(()), grad_hidden, grad_weight)

time: 205 us -> 196 us (0.956)
  waiting for transfers between devices: 74.7 us -> 67.4 us
  starting transfers between devices: 49.3 us -> 53.6 us
  local copies, waits for them, and re-layouts: 13.1 us -> 10.4 us
    ppermute x6 -> x12, waiting for transfers between devices: 27.4 us -> 15.3 us  [both_ways(): return (lax.ppermute(r, 'x', shift(1)), lax.ppermute(l, 'x', shift(-1)))]
    ppermute x6 -> x12, starting transfers between devices: 8.63 us -> 15.7 us  [both_ways(): return (lax.ppermute(r, 'x', shift(1)), lax.ppermute(l, 'x', shift(-1)))]
    ppermute x9, waiting for transfers between devices: 5.51 us -> 10.4 us  [others(): return [lax.ppermute(v, axis, shift(k)) for k in (1, 2, 3)]]
    all_gather x1, waiting for transfers between devices: 2.93 us -> 0.15 us  [shards(): lax.all_gather(stack(where, piece, sh8, *got), ('y', 'z', 'c'), axis=0, t...]
    unnamed x36 -> x24, local copies, waits for them, and re-layouts: 13.1 us -> 10.4 us
    pallas_call x19 -> x21, Pallas kernels: 47.2 us -> 45.4 us  [call(): pl.pallas_call(ordered if after else body, out_shape=outs, grid_spec=pltp...]
    dot_general x2 -> x4, matrix products: 5.56 us -> 4.3 us  [product(): return jnp.dot(rows, block, preferred_element_type=F32)]
    ppermute x7 -> x6, waiting for transfers between devices: 4.27 us -> 5.49 us  [swap(): return lax.ppermute(v, 'c', SWAP)]
  transfers between devices with their start and end apart: 27 -> 32, of which waited for: 17 -> 21; matrix products, arithmetic and copies ran while one was open for 3% -> 2% of each run, Pallas kernels for 15% -> 16%
where the time goes in v3:
time: 196 us
  waiting for transfers between devices  67.4 us (34%)
  starting transfers between devices  53.6 us (27%)
  Pallas kernels  45.4 us (23%)
  between operations  14.3 us (7%)
  local copies, waits for them, and re-layouts  10.4 us (5%)
  matrix products  4.3 us (2%)
    pallas_call x21, Pallas kernels, call(): pl.pallas_call(ordered if after else body, out_shape=outs, grid_spec=pltp...  45.4 us
    ppermute x3, waiting for transfers between devices, shards(): got = [lax.ppermute(s, 'x', shift(k + 1)) for k, s in enumerate(sends)]  18.6 us
    all_to_all x1, waiting for transfers between devices, shards(): lax.all_to_all(chip.reshape(64, 8, -1), CHIPS, split_axis=0, concat_axis=...  17.5 us
    ppermute x12, starting transfers between devices, both_ways(): return (lax.ppermute(r, 'x', shift(1)), lax.ppermute(l, 'x', shift(-1)))  15.7 us
    ppermute x12, waiting for transfers between devices, both_ways(): return (lax.ppermute(r, 'x', shift(1)), lax.ppermute(l, 'x', shift(-1)))  15.3 us
    ppermute x6, starting transfers between devices, swap(): return lax.ppermute(v, 'c', SWAP)  13.2 us
    ppermute x9, starting transfers between devices, others(): return [lax.ppermute(v, axis, shift(k)) for k in (1, 2, 3)]  12.1 us
    unnamed x24, local copies, waits for them, and re-layouts  10.4 us
  transfers between devices with their start and end apart: 32, of which 21 were waited for; matrix products, arithmetic and copies ran while one was open for 2% of the time, Pallas kernels for 16%

profile of v3, /device:TPU:1, one launch (start us, length us, event | category | flops | bytes accessed | tf_op | source)
XLA Modules:
  0.0 195.6 jit_solution(18325592042296319197)
XLA Ops:
  7.3 1.9 copy-done.10
  11.2 2.1 %collective-permute-start = (bf16[112,2048]{1,0:T(8,128)(2,1)S(1)}, bf16[112,2048]{1,0:T(8,128)(2,1)S(1)}, u32[]{:S(2)}, u32[]{:S(2)}) collective-permute-start(bf16[112,2048]{1,0:T(8,128)(2,1)S(1)} %get-tuple-element.28), channel_id=1, source_target_pairs={{0,32},{32,64},{64,96},{96,0},{1,33},{33,65},{65,97},{97,1},{2,34}... | collective-permute-start | bytes 1376264 | tf_op jit(solution)/shard_map/ppermute | solution.py:426
  13.3 2.5 %collective-permute-start.1 = (bf16[112,2048]{1,0:T(8,128)(2,1)S(1)}, bf16[112,2048]{1,0:T(8,128)(2,1)S(1)}, u32[]{:S(2)}, u32[]{:S(2)}) collective-permute-start(bf16[112,2048]{1,0:T(8,128)(2,1)S(1)} %get-tuple-element.29), channel_id=1, source_target_pairs={{0,64},{32,96},{64,0},{96,32},{1,65},{33,97},{65,1},{97,33},{2,66}... | collective-permute-start | bytes 1376264 | tf_op jit(solution)/shard_map/ppermute | solution.py:426
  16.9 7.5 %collective-permute-done.g1 = bf16[112,2048]{1,0:T(8,128)(2,1)S(1)} collective-permute-done((bf16[112,2048]{1,0:T(8,128)(2,1)S(1)}, bf16[112,2048]{1,0:T(8,128)(2,1)S(1)}, u32[]{:S(2)}, u32[]{:S(2)}) %collective-permute-start) | collective-permute-done | bytes 458784 | tf_op jit(solution)/shard_map/ppermute | solution.py:426
  24.4 11.1 %collective-permute-done.1.g2 = bf16[112,2048]{1,0:T(8,128)(2,1)S(1)} collective-permute-done((bf16[112,2048]{1,0:T(8,128)(2,1)S(1)}, bf16[112,2048]{1,0:T(8,128)(2,1)S(1)}, u32[]{:S(2)}, u32[]{:S(2)}) %collective-permute-start.1) | collective-permute-done | bytes 458784 | tf_op jit(solution)/shard_map/ppermute | solution.py:426
  42.1 2.5 %fusion.6 = f32[192,512]{1,0:T(8,128)S(1)} fusion(bf16[2048,2048]{1,0:T(8,128)(2,1)} %tw.1, s32[]{:T(128)S(6)} %select_n.24, bf16[768,2048]{1,0:T(8,128)(2,1)S(1)} %shard_map.77.h), kind=kOutput, calls=%fused_computation.6 | convolution fusion | flops 402653184 | bytes 3276804 | tf_op jit(solution)/shard_map/dot_general | solution.py:435
  50.8 5.6 %shard_map.78.pr.pl_.refs_1_.refs_2_.p = f32[3,768,512]{2,1,0:T(8,128)S(1)} custom-call(s32[4]{0:T(128)S(1)} %pad_add_fusion.where.refs_0_, bf16[768,2048]{1,0:T(8,128)(2,1)S(1)} %shard_map.77.h, bf16[2048,2048]{1,0:T(8,128)(2,1)S(1)} %copy-done.9), custom_call_target="tpu_custom_call" | custom-call | flops 4831838208 | tf_op jit(solution)/shard_map/pallas_call | solution.py:39
  58.4 2.9 %collective-permute-start.9 = (f32[192,512]{1,0:T(8,128)S(1)}, f32[192,512]{1,0:T(8,128)S(1)}, u32[]{:S(2)}, u32[]{:S(2)}) collective-permute-start(f32[192,512]{1,0:T(8,128)S(1)} %get-tuple-element.32), channel_id=1, source_target_pairs={{0,96},{32,0},{64,32},{96,64},{1,97},{33,1},{65,33},{97,65},{2,98}... | collective-permute-start | bytes 1179656 | tf_op jit(solution)/shard_map/ppermute | solution.py:417
  62.2 2.5 %collective-permute-done.10.refs_3_ = f32[192,512]{1,0:T(8,128)S(1)} collective-permute-done((f32[192,512]{1,0:T(8,128)S(1)}, f32[192,512]{1,0:T(8,128)S(1)}, u32[]{:S(2)}, u32[]{:S(2)}) %collective-permute-start.10) | collective-permute-done | bytes 393248 | tf_op jit(solution)/shard_map/ppermute | solution.py:417
  66.8 2.9 %collective-permute-start.15 = (f32[192,512]{1,0:T(8,128)S(1)}, f32[192,512]{1,0:T(8,128)S(1)}, u32[]{:S(2)}, u32[]{:S(2)}) collective-permute-start(f32[192,512]{1,0:T(8,128)S(1)} %get-tuple-element.37), channel_id=1, source_target_pairs={{0,96},{32,0},{64,32},{96,64},{1,97},{33,1},{65,33},{97,65},{2,98}... | collective-permute-start | bytes 1179656 | tf_op jit(solution)/shard_map/ppermute | solution.py:417
  69.6 5.1 %collective-permute-done.9.refs_4_ = f32[192,512]{1,0:T(8,128)S(1)} collective-permute-done((f32[192,512]{1,0:T(8,128)S(1)}, f32[192,512]{1,0:T(8,128)S(1)}, u32[]{:S(2)}, u32[]{:S(2)}) %collective-permute-start.9) | collective-permute-done | bytes 393248 | tf_op jit(solution)/shard_map/ppermute | solution.py:417
  75.3 2.9 %collective-permute-start.13 = (f32[192,512]{1,0:T(8,128)S(1)}, f32[192,512]{1,0:T(8,128)S(1)}, u32[]{:S(2)}, u32[]{:S(2)}) collective-permute-start(f32[192,512]{1,0:T(8,128)S(1)} %get-tuple-element.35), channel_id=1, source_target_pairs={{0,96},{32,0},{64,32},{96,64},{1,97},{33,1},{65,33},{97,65},{2,98}... | collective-permute-start | bytes 1179656 | tf_op jit(solution)/shard_map/ppermute | solution.py:417
  78.2 4.9 %collective-permute-done.15.refs_4_ = f32[192,512]{1,0:T(8,128)S(1)} collective-permute-done((f32[192,512]{1,0:T(8,128)S(1)}, f32[192,512]{1,0:T(8,128)S(1)}, u32[]{:S(2)}, u32[]{:S(2)}) %collective-permute-start.15) | collective-permute-done | bytes 393248 | tf_op jit(solution)/shard_map/ppermute | solution.py:417
  84.5 2.8 %collective-permute-start.17 = (f32[192,512]{1,0:T(8,128)}, f32[192,512]{1,0:T(8,128)S(1)}, u32[]{:S(2)}, u32[]{:S(2)}) collective-permute-start(f32[192,512]{1,0:T(8,128)} %get-tuple-element.41), channel_id=1, source_target_pairs={{0,96},{32,0},{64,32},{96,64},{1,97},{33,1},{65,33},{97,65},{2,98}... | collective-permute-start | bytes 1179656 | tf_op jit(solution)/shard_map/ppermute | solution.py:417
  89.3 2.3 %copy-done.4 = bf16[768,3072]{1,0:T(8,128)(2,1)S(1)} copy-done((bf16[768,3072]{1,0:T(8,128)(2,1)S(1)}, bf16[768,3072]{1,0:T(8,128)(2,1)}, u32[]{:S(2)}) %copy-start.4) | copy-done | bytes 4718616
  91.7 6.6 %shard_map.85.refs_5_.sl = f32[768,512]{1,0:T(8,128)S(1)} custom-call(s32[4]{0:T(128)S(1)} %pad_add_fusion.where.refs_0_, bf16[768,768]{1,0:T(8,128)(2,1)S(1)} %shard_map.80.refs_6_.refs_1_.refs_3_, bf16[768,3072]{1,0:T(8,128)(2,1)S(1)} %copy-done.4, bf16[3072,512]{1,0:T(8,128)(2,1)S(1)} %bitcast.7, f32[192,512]{1,0:T(8,128)S(1)} %get-tuple-element.38.refs_4_), custom_call_target="tpu_custom_call" | custom-call | tf_op jit(solution)/shard_map/pallas_call | solution.py:39
  101.8 3.4 %collective-permute-start.18 = (f32[8,768]{1,0:T(8,128)S(1)}, f32[8,768]{1,0:T(8,128)S(1)}, u32[]{:S(2)}, u32[]{:S(2)}) collective-permute-start(f32[8,768]{1,0:T(8,128)S(1)} %get-tuple-element.42.refs_0_), channel_id=1, source_target_pairs={{0,1},{1,0},{2,3},{3,2},{4,5},{5,4},{6,7},{7,6},{8,9},{9,8},{10,11... | collective-permute-start | bytes 73736 | tf_op jit(solution)/shard_map/ppermute | solution.py:423
  106.6 3.9 %collective-permute-start.21 = (f32[8,768]{1,0:T(8,128)S(1)}, f32[8,768]{1,0:T(8,128)S(1)}, u32[]{:S(2)}, u32[]{:S(2)}) collective-permute-start(f32[8,768]{1,0:T(8,128)S(1)} %shard_map.88.refs_0_), channel_id=1, source_target_pairs={{0,6},{2,0},{4,2},{6,4},{1,7},{3,1},{5,3},{7,5},{8,14},{10,8},{12,... | collective-permute-start | bytes 73736 | tf_op jit(solution)/shard_map/ppermute | solution.py:420
  111.5 3.2 %collective-permute-done.20.refs_2_ = f32[8,768]{1,0:T(8,128)S(1)} collective-permute-done((f32[8,768]{1,0:T(8,128)S(1)}, f32[8,768]{1,0:T(8,128)S(1)}, u32[]{:S(2)}, u32[]{:S(2)}) %collective-permute-start.20) | collective-permute-done | bytes 24608 | tf_op jit(solution)/shard_map/ppermute | solution.py:420
  115.3 2.8 %collective-permute-start.24 = (f32[8,768]{1,0:T(8,128)S(1)}, f32[8,768]{1,0:T(8,128)S(1)}, u32[]{:S(2)}, u32[]{:S(2)}) collective-permute-start(f32[8,768]{1,0:T(8,128)S(1)} %shard_map.89.refs_0_), channel_id=1, source_target_pairs={{0,24},{8,0},{16,8},{24,16},{1,25},{9,1},{17,9},{25,17},{2,26},{10... | collective-permute-start | bytes 73736 | tf_op jit(solution)/shard_map/ppermute | solution.py:420
  119.2 3.2 %collective-permute-done.23.refs_2_ = f32[8,768]{1,0:T(8,128)S(1)} collective-permute-done((f32[8,768]{1,0:T(8,128)S(1)}, f32[8,768]{1,0:T(8,128)S(1)}, u32[]{:S(2)}, u32[]{:S(2)}) %collective-permute-start.23) | collective-permute-done | bytes 24608 | tf_op jit(solution)/shard_map/ppermute | solution.py:420
  123.2 3.0 %collective-permute-start.27 = (f32[8,768]{1,0:T(8,128)S(1)}, f32[8,768]{1,0:T(8,128)S(1)}, u32[]{:S(2)}, u32[]{:S(2)}) collective-permute-start(f32[8,768]{1,0:T(8,128)S(1)} %shard_map.90.own), channel_id=1, source_target_pairs={{0,96},{32,0},{64,32},{96,64},{1,97},{33,1},{65,33},{97,65},{2,98}... | collective-permute-start | bytes 73736 | tf_op jit(solution)/shard_map/ppermute | solution.py:420
  127.1 3.2 %collective-permute-done.26.g2 = f32[8,768]{1,0:T(8,128)S(1)} collective-permute-done((f32[8,768]{1,0:T(8,128)S(1)}, f32[8,768]{1,0:T(8,128)S(1)}, u32[]{:S(2)}, u32[]{:S(2)}) %collective-permute-start.26) | collective-permute-done | bytes 24608 | tf_op jit(solution)/shard_map/ppermute | solution.py:420
  130.4 3.7 %shard_map.91 = (bf16[768,512]{1,0:T(8,128)(2,1)S(1)}, bf16[512,2304]{1,0:T(8,128)(2,1)S(1)}, f32[1,1]{1,0:T(1,128)}) custom-call(s32[4]{0:T(128)S(1)} %pad_add_fusion.where.refs_0_, f32[8,768]{1,0:T(8,128)S(1)} %shard_map.90.own, f32[8,768]{1,0:T(8,128)S(1)} %collective-permute-done.25.g1, f32[8,768]{1,0:T(8,128)S(1)} %collective-permute-done.26.g2, ...), custom_call_target="tpu_custom_call" | custom-call | flops 1207959552 | tf_op jit(solution)/shard_map/pallas_call | solution.py:39
  134.1 4.8 %collective-permute-start.28 = (bf16[512,2304]{1,0:T(8,128)(2,1)S(1)}, bf16[512,2304]{1,0:T(8,128)(2,1)S(1)}, u32[]{:S(2)}, u32[]{:S(2)}) collective-permute-start(bf16[512,2304]{1,0:T(8,128)(2,1)S(1)} %get-tuple-element.46), channel_id=1, source_target_pairs={{0,1},{1,0},{2,3},{3,2},{4,5},{5,4},{6,7},{7,6},{8,9},{9,8},{10,11... | collective-permute-start | bytes 7077896 | tf_op jit(solution)/shard_map/ppermute | solution.py:423
  138.9 2.6 %shard_map.92.kept = f32[512,2304]{1,0:T(8,128)S(1)} custom-call(s32[4]{0:T(128)S(1)} %pad_add_fusion.where.refs_0_, bf16[768,512]{1,0:T(8,128)(2,1)S(1)} %get-tuple-element.45.g.refs_2_, bf16[2,512,256]{2,1,0:T(8,128)(2,1)S(1)} %copy-done.8, bf16[3072,512]{1,0:T(8,128)(2,1)S(1)} %bitcast.9), custom_call_target="tpu_custom_call" | custom-call | flops 1207959552 | tf_op jit(solution)/shard_map/pallas_call | solution.py:39
  143.0 2.5 %shard_map.93.refs_4_ = bf16[512,2304]{1,0:T(8,128)(2,1)} custom-call(s32[4]{0:T(128)S(1)} %pad_add_fusion.where.refs_0_, f32[512,2304]{1,0:T(8,128)S(1)} %shard_map.92.kept, bf16[512,2304]{1,0:T(8,128)(2,1)S(1)} %collective-permute-done.28.got), custom_call_target="tpu_custom_call" | custom-call | tf_op jit(solution)/shard_map/pallas_call | solution.py:39
  145.6 6.8 %all-to-all-start = ((bf16[64,8,2304]{2,1,0:T(8,128)(2,1)}), bf16[64,8,2304]{2,1,0:T(8,128)(2,1)S(1)}, u32[]{:S(2)}, u32[]{:S(2)}) async-start(bf16[64,8,2304]{2,1,0:T(8,128)(2,1)} %bitcast.6), calls=%async_computation | async-start | bytes 4718592 | tf_op jit(solution)/shard_map/all_to_all | solution.py:457
  152.4 2.3 %copy-done.5 = bf16[768,3072]{1,0:T(8,128)(2,1)S(1)} copy-done((bf16[768,3072]{1,0:T(8,128)(2,1)S(1)}, bf16[768,3072]{1,0:T(8,128)(2,1)}, u32[]{:S(2)}) %copy-start.5) | copy-done | bytes 4718616
  155.9 9.6 %shard_map.94 = (f32[3072,1,512]{2,1,0:T(1,128)}, f32[8,128]{1,0:T(8,128)S(1)}) custom-call(s32[4]{0:T(128)S(1)} %pad_add_fusion.where.refs_0_, bf16[768,3072]{1,0:T(8,128)(2,1)S(1)} %copy-done.5, bf16[768,512]{1,0:T(8,128)(2,1)S(1)} %copy-done.7, bf16[768,768]{1,0:T(8,128)(2,1)S(1)} %shard_map.80.refs_6_.refs_1_.refs_3_, bf16[512,2304]{1,0:T(8,128)(2,1)} %shard_map.93.refs_4_), custom_call_target="tpu_custom_call" | custom-call | flops 2415919104 | tf_op jit(solution)/shard_map/pallas_call | solution.py:39
  165.4 17.5 %all-to-all-done.refs_1_ = bf16[64,8,2304]{2,1,0:T(8,128)(2,1)S(1)} async-done(((bf16[64,8,2304]{2,1,0:T(8,128)(2,1)}), bf16[64,8,2304]{2,1,0:T(8,128)(2,1)S(1)}, u32[]{:S(2)}, u32[]{:S(2)}) %all-to-all-start) | async-done | bytes 2359328 | tf_op jit(solution)/shard_map/all_to_all | solution.py:457
  183.8 2.9 %collective-permute-start.29 = (bf16[8,1536]{1,0:T(8,128)(2,1)S(1)}, bf16[8,1536]{1,0:T(8,128)(2,1)S(1)}, u32[]{:S(2)}, u32[]{:S(2)}) collective-permute-start(bf16[8,1536]{1,0:T(8,128)(2,1)S(1)} %get-tuple-element.49), channel_id=1, source_target_pairs={{0,1},{1,0},{2,3},{3,2},{4,5},{5,4},{6,7},{7,6},{8,9},{9,8},{10,11... | collective-permute-start | bytes 73736 | tf_op jit(solution)/shard_map/ppermute | solution.py:423
  (83 shorter events, 40.0 us)
Async XLA Ops:
  7.2 80.3 %all-gather.2.cloned.1.call-start = ((), (), s32[]{:S(2)}) async-start(), calls=%async_computation.1 | async-start | bytes 4866048 | tf_op jit(solution)/shard_map/all_gather | solution.py:429
  11.2 13.2 %collective-permute-start = (bf16[112,2048]{1,0:T(8,128)(2,1)S(1)}, bf16[112,2048]{1,0:T(8,128)(2,1)S(1)}, u32[]{:S(2)}, u32[]{:S(2)}) collective-permute-start(bf16[112,2048]{1,0:T(8,128)(2,1)S(1)} %get-tuple-element.28), channel_id=1, source_target_pairs={{0,32},{32,64},{64,96},{96,0},{1,33},{33,65},{65,97},{97,1},{2,34}... | collective-permute-start | bytes 1376264 | tf_op jit(solution)/shard_map/ppermute | solution.py:426
  13.3 22.2 %collective-permute-start.1 = (bf16[112,2048]{1,0:T(8,128)(2,1)S(1)}, bf16[112,2048]{1,0:T(8,128)(2,1)S(1)}, u32[]{:S(2)}, u32[]{:S(2)}) collective-permute-start(bf16[112,2048]{1,0:T(8,128)(2,1)S(1)} %get-tuple-element.29), channel_id=1, source_target_pairs={{0,64},{32,96},{64,0},{96,32},{1,65},{33,97},{65,1},{97,33},{2,66}... | collective-permute-start | bytes 1376264 | tf_op jit(solution)/shard_map/ppermute | solution.py:426
  15.8 19.8 %collective-permute-start.2 = (bf16[112,2048]{1,0:T(8,128)(2,1)S(1)}, bf16[112,2048]{1,0:T(8,128)(2,1)S(1)}, u32[]{:S(2)}, u32[]{:S(2)}) collective-permute-start(bf16[112,2048]{1,0:T(8,128)(2,1)S(1)} %get-tuple-element.30), channel_id=1, source_target_pairs={{0,96},{32,0},{64,32},{96,64},{1,97},{33,1},{65,33},{97,65},{2,98}... | collective-permute-start | bytes 1376264 | tf_op jit(solution)/shard_map/ppermute | solution.py:426
  37.0 3.1 %collective-permute-start.3 = (bf16[112,2048]{1,0:T(8,128)(2,1)S(1)}, bf16[112,2048]{1,0:T(8,128)(2,1)S(1)}, u32[]{:S(2)}, u32[]{:S(2)}) collective-permute-start(bf16[112,2048]{1,0:T(8,128)(2,1)S(1)} %collective-permute-done.g1), channel_id=1, source_target_pairs={{0,1},{1,0},{2,3},{3,2},{4,5},{5,4},{6,7},{7,6},{8,9},{9,8},{10,11... | collective-permute-start | bytes 1376264 | tf_op jit(solution)/shard_map/ppermute | solution.py:423
  38.6 2.1 %collective-permute-start.4 = (bf16[112,2048]{1,0:T(8,128)(2,1)S(1)}, bf16[112,2048]{1,0:T(8,128)(2,1)S(1)}, u32[]{:S(2)}, u32[]{:S(2)}) collective-permute-start(bf16[112,2048]{1,0:T(8,128)(2,1)S(1)} %collective-permute-done.1.g2), channel_id=1, source_target_pairs={{0,1},{1,0},{2,3},{3,2},{4,5},{5,4},{6,7},{7,6},{8,9},{9,8},{10,11... | collective-permute-start | bytes 1376264 | tf_op jit(solution)/shard_map/ppermute | solution.py:423
  38.7 2.7 %collective-permute-start.5 = (bf16[112,2048]{1,0:T(8,128)(2,1)S(1)}, bf16[112,2048]{1,0:T(8,128)(2,1)S(1)}, u32[]{:S(2)}, u32[]{:S(2)}) collective-permute-start(bf16[112,2048]{1,0:T(8,128)(2,1)S(1)} %collective-permute-done.2.g3), channel_id=1, source_target_pairs={{0,1},{1,0},{2,3},{3,2},{4,5},{5,4},{6,7},{7,6},{8,9},{9,8},{10,11... | collective-permute-start | bytes 1376264 | tf_op jit(solution)/shard_map/ppermute | solution.py:423
  44.6 11.8 %collective-permute-start.6 = (f32[192,512]{1,0:T(8,128)S(1)}, f32[192,512]{1,0:T(8,128)S(1)}, u32[]{:S(2)}, u32[]{:S(2)}) collective-permute-start(f32[192,512]{1,0:T(8,128)S(1)} %fusion.6), channel_id=1, source_target_pairs={{0,32},{32,64},{64,96},{96,0},{1,33},{33,65},{65,97},{97,1},{2,34}... | collective-permute-start | bytes 1179656 | tf_op jit(solution)/shard_map/ppermute | solution.py:417
  46.2 18.4 %collective-permute-start.10 = (f32[192,512]{1,0:T(8,128)S(1)}, f32[192,512]{1,0:T(8,128)S(1)}, u32[]{:S(2)}, u32[]{:S(2)}) collective-permute-start(f32[192,512]{1,0:T(8,128)S(1)} %fusion.4), channel_id=1, source_target_pairs={{0,32},{32,64},{64,96},{96,0},{1,33},{33,65},{65,97},{97,1},{2,34}... | collective-permute-start | bytes 1179656 | tf_op jit(solution)/shard_map/ppermute | solution.py:417
  48.0 9.8 %collective-permute-start.7 = (f32[192,512]{1,0:T(8,128)S(1)}, f32[192,512]{1,0:T(8,128)S(1)}, u32[]{:S(2)}, u32[]{:S(2)}) collective-permute-start(f32[192,512]{1,0:T(8,128)S(1)} %fusion.2), channel_id=1, source_target_pairs={{0,96},{32,0},{64,32},{96,64},{1,97},{33,1},{65,33},{97,65},{2,98}... | collective-permute-start | bytes 1179656 | tf_op jit(solution)/shard_map/ppermute | solution.py:417
  50.2 15.9 %collective-permute-start.11 = (f32[192,512]{1,0:T(8,128)S(1)}, f32[192,512]{1,0:T(8,128)S(1)}, u32[]{:S(2)}, u32[]{:S(2)}) collective-permute-start(f32[192,512]{1,0:T(8,128)S(1)} %fusion), channel_id=1, source_target_pairs={{0,96},{32,0},{64,32},{96,64},{1,97},{33,1},{65,33},{97,65},{2,98}... | collective-permute-start | bytes 1179656 | tf_op jit(solution)/shard_map/ppermute | solution.py:417
  58.4 16.3 %collective-permute-start.9 = (f32[192,512]{1,0:T(8,128)S(1)}, f32[192,512]{1,0:T(8,128)S(1)}, u32[]{:S(2)}, u32[]{:S(2)}) collective-permute-start(f32[192,512]{1,0:T(8,128)S(1)} %get-tuple-element.32), channel_id=1, source_target_pairs={{0,96},{32,0},{64,32},{96,64},{1,97},{33,1},{65,33},{97,65},{2,98}... | collective-permute-start | bytes 1179656 | tf_op jit(solution)/shard_map/ppermute | solution.py:417
  61.2 13.5 %collective-permute-start.8 = (f32[192,512]{1,0:T(8,128)S(1)}, f32[192,512]{1,0:T(8,128)S(1)}, u32[]{:S(2)}, u32[]{:S(2)}) collective-permute-start(f32[192,512]{1,0:T(8,128)S(1)} %get-tuple-element.31.refs_5_), channel_id=1, source_target_pairs={{0,32},{32,64},{64,96},{96,0},{1,33},{33,65},{65,97},{97,1},{2,34}... | collective-permute-start | bytes 1179656 | tf_op jit(solution)/shard_map/ppermute | solution.py:417
  66.8 16.3 %collective-permute-start.15 = (f32[192,512]{1,0:T(8,128)S(1)}, f32[192,512]{1,0:T(8,128)S(1)}, u32[]{:S(2)}, u32[]{:S(2)}) collective-permute-start(f32[192,512]{1,0:T(8,128)S(1)} %get-tuple-element.37), channel_id=1, source_target_pairs={{0,96},{32,0},{64,32},{96,64},{1,97},{33,1},{65,33},{97,65},{2,98}... | collective-permute-start | bytes 1179656 | tf_op jit(solution)/shard_map/ppermute | solution.py:417
  69.6 13.5 %collective-permute-start.14 = (f32[192,512]{1,0:T(8,128)S(1)}, f32[192,512]{1,0:T(8,128)S(1)}, u32[]{:S(2)}, u32[]{:S(2)}) collective-permute-start(f32[192,512]{1,0:T(8,128)S(1)} %get-tuple-element.33.refs_5_), channel_id=1, source_target_pairs={{0,32},{32,64},{64,96},{96,0},{1,33},{33,65},{65,97},{97,1},{2,34}... | collective-permute-start | bytes 1179656 | tf_op jit(solution)/shard_map/ppermute | solution.py:417
  75.3 22.9 %collective-permute-start.13 = (f32[192,512]{1,0:T(8,128)S(1)}, f32[192,512]{1,0:T(8,128)S(1)}, u32[]{:S(2)}, u32[]{:S(2)}) collective-permute-start(f32[192,512]{1,0:T(8,128)S(1)} %get-tuple-element.35), channel_id=1, source_target_pairs={{0,96},{32,0},{64,32},{96,64},{1,97},{33,1},{65,33},{97,65},{2,98}... | collective-permute-start | bytes 1179656 | tf_op jit(solution)/shard_map/ppermute | solution.py:417
  78.2 20.1 %collective-permute-start.12 = (f32[192,512]{1,0:T(8,128)S(1)}, f32[192,512]{1,0:T(8,128)}, u32[]{:S(2)}, u32[]{:S(2)}) collective-permute-start(f32[192,512]{1,0:T(8,128)S(1)} %get-tuple-element.34.refs_5_), channel_id=1, source_target_pairs={{0,32},{32,64},{64,96},{96,0},{1,33},{33,65},{65,97},{97,1},{2,34}... | collective-permute-start | bytes 1179656 | tf_op jit(solution)/shard_map/ppermute | solution.py:417
  84.5 15.4 %collective-permute-start.17 = (f32[192,512]{1,0:T(8,128)}, f32[192,512]{1,0:T(8,128)S(1)}, u32[]{:S(2)}, u32[]{:S(2)}) collective-permute-start(f32[192,512]{1,0:T(8,128)} %get-tuple-element.41), channel_id=1, source_target_pairs={{0,96},{32,0},{64,32},{96,64},{1,97},{33,1},{65,33},{97,65},{2,98}... | collective-permute-start | bytes 1179656 | tf_op jit(solution)/shard_map/ppermute | solution.py:417
  87.3 12.6 %collective-permute-start.16 = (f32[192,512]{1,0:T(8,128)S(1)}, f32[192,512]{1,0:T(8,128)S(1)}, u32[]{:S(2)}, u32[]{:S(2)}) collective-permute-start(f32[192,512]{1,0:T(8,128)S(1)} %get-tuple-element.38.refs_4_), channel_id=1, source_target_pairs={{0,32},{32,64},{64,96},{96,0},{1,33},{33,65},{65,97},{97,1},{2,34}... | collective-permute-start | bytes 1179656 | tf_op jit(solution)/shard_map/ppermute | solution.py:417
  101.8 4.3 %collective-permute-start.18 = (f32[8,768]{1,0:T(8,128)S(1)}, f32[8,768]{1,0:T(8,128)S(1)}, u32[]{:S(2)}, u32[]{:S(2)}) collective-permute-start(f32[8,768]{1,0:T(8,128)S(1)} %get-tuple-element.42.refs_0_), channel_id=1, source_target_pairs={{0,1},{1,0},{2,3},{3,2},{4,5},{5,4},{6,7},{7,6},{8,9},{9,8},{10,11... | collective-permute-start | bytes 73736 | tf_op jit(solution)/shard_map/ppermute | solution.py:423
  106.6 4.9 %collective-permute-start.21 = (f32[8,768]{1,0:T(8,128)S(1)}, f32[8,768]{1,0:T(8,128)S(1)}, u32[]{:S(2)}, u32[]{:S(2)}) collective-permute-start(f32[8,768]{1,0:T(8,128)S(1)} %shard_map.88.refs_0_), channel_id=1, source_target_pairs={{0,6},{2,0},{4,2},{6,4},{1,7},{3,1},{5,3},{7,5},{8,14},{10,8},{12,... | collective-permute-start | bytes 73736 | tf_op jit(solution)/shard_map/ppermute | solution.py:420
  110.5 4.2 %collective-permute-start.20 = (f32[8,768]{1,0:T(8,128)S(1)}, f32[8,768]{1,0:T(8,128)S(1)}, u32[]{:S(2)}, u32[]{:S(2)}) collective-permute-start(f32[8,768]{1,0:T(8,128)S(1)} %shard_map.88.refs_0_), channel_id=1, source_target_pairs={{0,4},{2,6},{4,0},{6,2},{1,5},{3,7},{5,1},{7,3},{8,12},{10,14},{12... | collective-permute-start | bytes 73736 | tf_op jit(solution)/shard_map/ppermute | solution.py:420
  110.5 4.2 %collective-permute-start.19 = (f32[8,768]{1,0:T(8,128)S(1)}, f32[8,768]{1,0:T(8,128)S(1)}, u32[]{:S(2)}, u32[]{:S(2)}) collective-permute-start(f32[8,768]{1,0:T(8,128)S(1)} %shard_map.88.refs_0_), channel_id=1, source_target_pairs={{0,2},{2,4},{4,6},{6,0},{1,3},{3,5},{5,7},{7,1},{8,10},{10,12},{12... | collective-permute-start | bytes 73736 | tf_op jit(solution)/shard_map/ppermute | solution.py:420
  115.3 3.9 %collective-permute-start.24 = (f32[8,768]{1,0:T(8,128)S(1)}, f32[8,768]{1,0:T(8,128)S(1)}, u32[]{:S(2)}, u32[]{:S(2)}) collective-permute-start(f32[8,768]{1,0:T(8,128)S(1)} %shard_map.89.refs_0_), channel_id=1, source_target_pairs={{0,24},{8,0},{16,8},{24,16},{1,25},{9,1},{17,9},{25,17},{2,26},{10... | collective-permute-start | bytes 73736 | tf_op jit(solution)/shard_map/ppermute | solution.py:420
  118.1 4.2 %collective-permute-start.23 = (f32[8,768]{1,0:T(8,128)S(1)}, f32[8,768]{1,0:T(8,128)S(1)}, u32[]{:S(2)}, u32[]{:S(2)}) collective-permute-start(f32[8,768]{1,0:T(8,128)S(1)} %shard_map.89.refs_0_), channel_id=1, source_target_pairs={{0,16},{8,24},{16,0},{24,8},{1,17},{9,25},{17,1},{25,9},{2,18},{10... | collective-permute-start | bytes 73736 | tf_op jit(solution)/shard_map/ppermute | solution.py:420
  118.5 4.1 %collective-permute-start.22 = (f32[8,768]{1,0:T(8,128)S(1)}, f32[8,768]{1,0:T(8,128)S(1)}, u32[]{:S(2)}, u32[]{:S(2)}) collective-permute-start(f32[8,768]{1,0:T(8,128)S(1)} %shard_map.89.refs_0_), channel_id=1, source_target_pairs={{0,8},{8,16},{16,24},{24,0},{1,9},{9,17},{17,25},{25,1},{2,10},{10... | collective-permute-start | bytes 73736 | tf_op jit(solution)/shard_map/ppermute | solution.py:420
  123.2 3.9 %collective-permute-start.27 = (f32[8,768]{1,0:T(8,128)S(1)}, f32[8,768]{1,0:T(8,128)S(1)}, u32[]{:S(2)}, u32[]{:S(2)}) collective-permute-start(f32[8,768]{1,0:T(8,128)S(1)} %shard_map.90.own), channel_id=1, source_target_pairs={{0,96},{32,0},{64,32},{96,64},{1,97},{33,1},{65,33},{97,65},{2,98}... | collective-permute-start | bytes 73736 | tf_op jit(solution)/shard_map/ppermute | solution.py:420
  126.2 4.2 %collective-permute-start.26 = (f32[8,768]{1,0:T(8,128)S(1)}, f32[8,768]{1,0:T(8,128)S(1)}, u32[]{:S(2)}, u32[]{:S(2)}) collective-permute-start(f32[8,768]{1,0:T(8,128)S(1)} %shard_map.90.own), channel_id=1, source_target_pairs={{0,64},{32,96},{64,0},{96,32},{1,65},{33,97},{65,1},{97,33},{2,66}... | collective-permute-start | bytes 73736 | tf_op jit(solution)/shard_map/ppermute | solution.py:420
  126.2 4.2 %collective-permute-start.25 = (f32[8,768]{1,0:T(8,128)S(1)}, f32[8,768]{1,0:T(8,128)S(1)}, u32[]{:S(2)}, u32[]{:S(2)}) collective-permute-start(f32[8,768]{1,0:T(8,128)S(1)} %shard_map.90.own), channel_id=1, source_target_pairs={{0,32},{32,64},{64,96},{96,0},{1,33},{33,65},{65,97},{97,1},{2,34}... | collective-permute-start | bytes 73736 | tf_op jit(solution)/shard_map/ppermute | solution.py:420
  134.1 8.9 %collective-permute-start.28 = (bf16[512,2304]{1,0:T(8,128)(2,1)S(1)}, bf16[512,2304]{1,0:T(8,128)(2,1)S(1)}, u32[]{:S(2)}, u32[]{:S(2)}) collective-permute-start(bf16[512,2304]{1,0:T(8,128)(2,1)S(1)} %get-tuple-element.46), channel_id=1, source_target_pairs={{0,1},{1,0},{2,3},{3,2},{4,5},{5,4},{6,7},{7,6},{8,9},{9,8},{10,11... | collective-permute-start | bytes 7077896 | tf_op jit(solution)/shard_map/ppermute | solution.py:423
  145.6 37.4 %all-to-all-start = ((bf16[64,8,2304]{2,1,0:T(8,128)(2,1)}), bf16[64,8,2304]{2,1,0:T(8,128)(2,1)S(1)}, u32[]{:S(2)}, u32[]{:S(2)}) async-start(bf16[64,8,2304]{2,1,0:T(8,128)(2,1)} %bitcast.6), calls=%async_computation | async-start | bytes 4718592 | tf_op jit(solution)/shard_map/all_to_all | solution.py:457
  183.8 3.7 %collective-permute-start.29 = (bf16[8,1536]{1,0:T(8,128)(2,1)S(1)}, bf16[8,1536]{1,0:T(8,128)(2,1)S(1)}, u32[]{:S(2)}, u32[]{:S(2)}) collective-permute-start(bf16[8,1536]{1,0:T(8,128)(2,1)S(1)} %get-tuple-element.49), channel_id=1, source_target_pairs={{0,1},{1,0},{2,3},{3,2},{4,5},{5,4},{6,7},{7,6},{8,9},{9,8},{10,11... | collective-permute-start | bytes 73736 | tf_op jit(solution)/shard_map/ppermute | solution.py:423
  (12 other events, 116.3 us)
Sparse Core Ops, SparseCore 0:
  37.1 50.3 all-gather.1

commit v4 on v3

--- a/solution.py
+++ b/solution.py
@@ -219,7 +219,7 @@
 def student(where, pick, rows, w, after):
     tokens, d = rows.shape
     cols = w.shape[1]
-    tile = d // 6
+    tile = d // 3
     specs = [
         whole(pick.shape),
         pl.BlockSpec((tokens, tile), lambda i, s: (0, i)),
@@ -228,7 +228,7 @@
     out = sds((tokens, cols), F32)
     return call(
         student_body, where, (pick, rows, w), specs, [out], [whole(out.shape)],
-        grid=(6,), after=after, spare=8, scratch=[pltpu.VMEM(out.shape, F32)],
+        grid=(3,), after=after, spare=38, scratch=[pltpu.VMEM(out.shape, F32)],
     )[0]
 
 

time: 196 us -> 194 us (0.990)
  local copies, waits for them, and re-layouts: 10.4 us -> 6.18 us
  waiting for transfers between devices: 67.4 us -> 69.8 us
    unnamed x24 -> x20, local copies, waits for them, and re-layouts: 10.4 us -> 6.18 us
    ppermute x12, waiting for transfers between devices: 15.3 us -> 17.7 us  [both_ways(): return (lax.ppermute(r, 'x', shift(1)), lax.ppermute(l, 'x', shift(-1)))]
  transfers between devices with their start and end apart: 32 -> 32, of which waited for: 21 -> 22; matrix products, arithmetic and copies ran while one was open for 2% -> 2% of each run, Pallas kernels for 16% -> 17%
where the time goes in v4:
time: 194 us
  waiting for transfers between devices  69.8 us (36%)
  starting transfers between devices  52 us (27%)
  Pallas kernels  47.1 us (24%)
  between operations  14.3 us (7%)
  local copies, waits for them, and re-layouts  6.18 us (3%)
  matrix products  4.31 us (2%)
    pallas_call x21, Pallas kernels, call(): pl.pallas_call(ordered if after else body, out_shape=outs, grid_spec=pltp...  47.1 us
    ppermute x3, waiting for transfers between devices, shards(): got = [lax.ppermute(s, 'x', shift(k + 1)) for k, s in enumerate(sends)]  18.6 us
    ppermute x12, waiting for transfers between devices, both_ways(): return (lax.ppermute(r, 'x', shift(1)), lax.ppermute(l, 'x', shift(-1)))  17.7 us
    all_to_all x1, waiting for transfers between devices, shards(): lax.all_to_all(chip.reshape(64, 8, -1), CHIPS, split_axis=0, concat_axis=...  17.5 us
    ppermute x12, starting transfers between devices, both_ways(): return (lax.ppermute(r, 'x', shift(1)), lax.ppermute(l, 'x', shift(-1)))  15.7 us
    ppermute x9, starting transfers between devices, others(): return [lax.ppermute(v, axis, shift(k)) for k in (1, 2, 3)]  12 us
    ppermute x6, starting transfers between devices, swap(): return lax.ppermute(v, 'c', SWAP)  11.9 us
    ppermute x9, waiting for transfers between devices, others(): return [lax.ppermute(v, axis, shift(k)) for k in (1, 2, 3)]  10.4 us
  transfers between devices with their start and end apart: 32, of which 22 were waited for; matrix products, arithmetic and copies ran while one was open for 2% of the time, Pallas kernels for 17%

profile of v4, /device:TPU:1, one launch (start us, length us, event | category | flops | bytes accessed | tf_op | source)
XLA Modules:
  0.0 193.7 jit_solution(9826668669491337903)
XLA Ops:
  7.3 1.9 copy-done.8
  11.2 2.1 %collective-permute-start = (bf16[112,2048]{1,0:T(8,128)(2,1)S(1)}, bf16[112,2048]{1,0:T(8,128)(2,1)S(1)}, u32[]{:S(2)}, u32[]{:S(2)}) collective-permute-start(bf16[112,2048]{1,0:T(8,128)(2,1)S(1)} %get-tuple-element.28), channel_id=1, source_target_pairs={{0,32},{32,64},{64,96},{96,0},{1,33},{33,65},{65,97},{97,1},{2,34}... | collective-permute-start | bytes 1376264 | tf_op jit(solution)/shard_map/ppermute | solution.py:426
  13.3 2.5 %collective-permute-start.1 = (bf16[112,2048]{1,0:T(8,128)(2,1)S(1)}, bf16[112,2048]{1,0:T(8,128)(2,1)S(1)}, u32[]{:S(2)}, u32[]{:S(2)}) collective-permute-start(bf16[112,2048]{1,0:T(8,128)(2,1)S(1)} %get-tuple-element.29), channel_id=1, source_target_pairs={{0,64},{32,96},{64,0},{96,32},{1,65},{33,97},{65,1},{97,33},{2,66}... | collective-permute-start | bytes 1376264 | tf_op jit(solution)/shard_map/ppermute | solution.py:426
  16.9 7.5 %collective-permute-done.g1 = bf16[112,2048]{1,0:T(8,128)(2,1)S(1)} collective-permute-done((bf16[112,2048]{1,0:T(8,128)(2,1)S(1)}, bf16[112,2048]{1,0:T(8,128)(2,1)S(1)}, u32[]{:S(2)}, u32[]{:S(2)}) %collective-permute-start) | collective-permute-done | bytes 458784 | tf_op jit(solution)/shard_map/ppermute | solution.py:426
  24.4 11.1 %collective-permute-done.1.g2 = bf16[112,2048]{1,0:T(8,128)(2,1)S(1)} collective-permute-done((bf16[112,2048]{1,0:T(8,128)(2,1)S(1)}, bf16[112,2048]{1,0:T(8,128)(2,1)S(1)}, u32[]{:S(2)}, u32[]{:S(2)}) %collective-permute-start.1) | collective-permute-done | bytes 458784 | tf_op jit(solution)/shard_map/ppermute | solution.py:426
  42.1 2.5 %fusion.6 = f32[192,512]{1,0:T(8,128)S(1)} fusion(bf16[2048,2048]{1,0:T(8,128)(2,1)} %tw.1, s32[]{:T(128)S(6)} %select_n.24, bf16[768,2048]{1,0:T(8,128)(2,1)S(1)} %shard_map.77.h), kind=kOutput, calls=%fused_computation.6 | convolution fusion | flops 402653184 | bytes 3276804 | tf_op jit(solution)/shard_map/dot_general | solution.py:435
  50.8 5.6 %shard_map.78.pr.pl_.refs_1_.refs_2_.p = f32[3,768,512]{2,1,0:T(8,128)S(1)} custom-call(s32[4]{0:T(128)S(1)} %pad_add_fusion.where.refs_0_, bf16[768,2048]{1,0:T(8,128)(2,1)S(1)} %shard_map.77.h, bf16[2048,2048]{1,0:T(8,128)(2,1)S(1)} %copy-done.7), custom_call_target="tpu_custom_call" | custom-call | flops 4831838208 | tf_op jit(solution)/shard_map/pallas_call | solution.py:39
  58.4 2.8 %collective-permute-start.9 = (f32[192,512]{1,0:T(8,128)S(1)}, f32[192,512]{1,0:T(8,128)S(1)}, u32[]{:S(2)}, u32[]{:S(2)}) collective-permute-start(f32[192,512]{1,0:T(8,128)S(1)} %get-tuple-element.32), channel_id=1, source_target_pairs={{0,96},{32,0},{64,32},{96,64},{1,97},{33,1},{65,33},{97,65},{2,98}... | collective-permute-start | bytes 1179656 | tf_op jit(solution)/shard_map/ppermute | solution.py:417
  62.2 2.5 %collective-permute-done.10.refs_3_ = f32[192,512]{1,0:T(8,128)S(1)} collective-permute-done((f32[192,512]{1,0:T(8,128)S(1)}, f32[192,512]{1,0:T(8,128)S(1)}, u32[]{:S(2)}, u32[]{:S(2)}) %collective-permute-start.10) | collective-permute-done | bytes 393248 | tf_op jit(solution)/shard_map/ppermute | solution.py:417
  66.8 2.8 %collective-permute-start.15 = (f32[192,512]{1,0:T(8,128)S(1)}, f32[192,512]{1,0:T(8,128)S(1)}, u32[]{:S(2)}, u32[]{:S(2)}) collective-permute-start(f32[192,512]{1,0:T(8,128)S(1)} %get-tuple-element.37), channel_id=1, source_target_pairs={{0,96},{32,0},{64,32},{96,64},{1,97},{33,1},{65,33},{97,65},{2,98}... | collective-permute-start | bytes 1179656 | tf_op jit(solution)/shard_map/ppermute | solution.py:417
  69.6 5.1 %collective-permute-done.9.refs_4_ = f32[192,512]{1,0:T(8,128)S(1)} collective-permute-done((f32[192,512]{1,0:T(8,128)S(1)}, f32[192,512]{1,0:T(8,128)S(1)}, u32[]{:S(2)}, u32[]{:S(2)}) %collective-permute-start.9) | collective-permute-done | bytes 393248 | tf_op jit(solution)/shard_map/ppermute | solution.py:417
  75.3 2.8 %collective-permute-start.13 = (f32[192,512]{1,0:T(8,128)S(1)}, f32[192,512]{1,0:T(8,128)S(1)}, u32[]{:S(2)}, u32[]{:S(2)}) collective-permute-start(f32[192,512]{1,0:T(8,128)S(1)} %get-tuple-element.35), channel_id=1, source_target_pairs={{0,96},{32,0},{64,32},{96,64},{1,97},{33,1},{65,33},{97,65},{2,98}... | collective-permute-start | bytes 1179656 | tf_op jit(solution)/shard_map/ppermute | solution.py:417
  78.2 4.9 %collective-permute-done.15.refs_4_ = f32[192,512]{1,0:T(8,128)S(1)} collective-permute-done((f32[192,512]{1,0:T(8,128)S(1)}, f32[192,512]{1,0:T(8,128)S(1)}, u32[]{:S(2)}, u32[]{:S(2)}) %collective-permute-start.15) | collective-permute-done | bytes 393248 | tf_op jit(solution)/shard_map/ppermute | solution.py:417
  84.5 2.8 %collective-permute-start.17 = (f32[192,512]{1,0:T(8,128)}, f32[192,512]{1,0:T(8,128)S(1)}, u32[]{:S(2)}, u32[]{:S(2)}) collective-permute-start(f32[192,512]{1,0:T(8,128)} %get-tuple-element.41), channel_id=1, source_target_pairs={{0,96},{32,0},{64,32},{96,64},{1,97},{33,1},{65,33},{97,65},{2,98}... | collective-permute-start | bytes 1179656 | tf_op jit(solution)/shard_map/ppermute | solution.py:417
  87.4 8.4 %shard_map.85.refs_5_.sl = f32[768,512]{1,0:T(8,128)S(1)} custom-call(s32[4]{0:T(128)S(1)} %pad_add_fusion.where.refs_0_, bf16[768,768]{1,0:T(8,128)(2,1)S(1)} %shard_map.80.refs_6_.refs_1_.refs_3_, bf16[768,3072]{1,0:T(8,128)(2,1)} %all-gather.2.cloned.1.call-done.refs_2_.refs_1_, bf16[3072,512]{1,0:T(8,128)(2,1)} %bitcast.7, ...), custom_call_target="tpu_custom_call" | custom-call | tf_op jit(solution)/shard_map/pallas_call | solution.py:39
  97.5 2.4 %collective-permute-done.17.l1 = f32[192,512]{1,0:T(8,128)S(1)} collective-permute-done((f32[192,512]{1,0:T(8,128)}, f32[192,512]{1,0:T(8,128)S(1)}, u32[]{:S(2)}, u32[]{:S(2)}) %collective-permute-start.17) | collective-permute-done | bytes 393248 | tf_op jit(solution)/shard_map/ppermute | solution.py:417
  101.7 1.9 collective-permute-start.18
  105.0 3.8 %collective-permute-start.21 = (f32[8,768]{1,0:T(8,128)S(1)}, f32[8,768]{1,0:T(8,128)S(1)}, u32[]{:S(2)}, u32[]{:S(2)}) collective-permute-start(f32[8,768]{1,0:T(8,128)S(1)} %shard_map.88.refs_0_), channel_id=1, source_target_pairs={{0,6},{2,0},{4,2},{6,4},{1,7},{3,1},{5,3},{7,5},{8,14},{10,8},{12,... | collective-permute-start | bytes 73736 | tf_op jit(solution)/shard_map/ppermute | solution.py:420
  109.8 3.2 %collective-permute-done.20.refs_2_ = f32[8,768]{1,0:T(8,128)S(1)} collective-permute-done((f32[8,768]{1,0:T(8,128)S(1)}, f32[8,768]{1,0:T(8,128)S(1)}, u32[]{:S(2)}, u32[]{:S(2)}) %collective-permute-start.20) | collective-permute-done | bytes 24608 | tf_op jit(solution)/shard_map/ppermute | solution.py:420
  113.6 2.8 %collective-permute-start.24 = (f32[8,768]{1,0:T(8,128)S(1)}, f32[8,768]{1,0:T(8,128)S(1)}, u32[]{:S(2)}, u32[]{:S(2)}) collective-permute-start(f32[8,768]{1,0:T(8,128)S(1)} %shard_map.89.refs_0_), channel_id=1, source_target_pairs={{0,24},{8,0},{16,8},{24,16},{1,25},{9,1},{17,9},{25,17},{2,26},{10... | collective-permute-start | bytes 73736 | tf_op jit(solution)/shard_map/ppermute | solution.py:420
  117.5 3.2 %collective-permute-done.23.refs_2_ = f32[8,768]{1,0:T(8,128)S(1)} collective-permute-done((f32[8,768]{1,0:T(8,128)S(1)}, f32[8,768]{1,0:T(8,128)S(1)}, u32[]{:S(2)}, u32[]{:S(2)}) %collective-permute-start.23) | collective-permute-done | bytes 24608 | tf_op jit(solution)/shard_map/ppermute | solution.py:420
  121.5 2.9 %collective-permute-start.27 = (f32[8,768]{1,0:T(8,128)S(1)}, f32[8,768]{1,0:T(8,128)S(1)}, u32[]{:S(2)}, u32[]{:S(2)}) collective-permute-start(f32[8,768]{1,0:T(8,128)S(1)} %shard_map.90.own), channel_id=1, source_target_pairs={{0,96},{32,0},{64,32},{96,64},{1,97},{33,1},{65,33},{97,65},{2,98}... | collective-permute-start | bytes 73736 | tf_op jit(solution)/shard_map/ppermute | solution.py:420
  125.4 3.2 %collective-permute-done.26.g2 = f32[8,768]{1,0:T(8,128)S(1)} collective-permute-done((f32[8,768]{1,0:T(8,128)S(1)}, f32[8,768]{1,0:T(8,128)S(1)}, u32[]{:S(2)}, u32[]{:S(2)}) %collective-permute-start.26) | collective-permute-done | bytes 24608 | tf_op jit(solution)/shard_map/ppermute | solution.py:420
  128.6 3.7 %shard_map.91 = (bf16[768,512]{1,0:T(8,128)(2,1)S(1)}, bf16[512,2304]{1,0:T(8,128)(2,1)S(1)}, f32[1,1]{1,0:T(1,128)}) custom-call(s32[4]{0:T(128)S(1)} %pad_add_fusion.where.refs_0_, f32[8,768]{1,0:T(8,128)S(1)} %shard_map.90.own, f32[8,768]{1,0:T(8,128)S(1)} %collective-permute-done.25.g1, f32[8,768]{1,0:T(8,128)S(1)} %collective-permute-done.26.g2, ...), custom_call_target="tpu_custom_call" | custom-call | flops 1207959552 | tf_op jit(solution)/shard_map/pallas_call | solution.py:39
  132.3 5.0 %collective-permute-start.28 = (bf16[512,2304]{1,0:T(8,128)(2,1)S(1)}, bf16[512,2304]{1,0:T(8,128)(2,1)S(1)}, u32[]{:S(2)}, u32[]{:S(2)}) collective-permute-start(bf16[512,2304]{1,0:T(8,128)(2,1)S(1)} %get-tuple-element.46), channel_id=1, source_target_pairs={{0,1},{1,0},{2,3},{3,2},{4,5},{5,4},{6,7},{7,6},{8,9},{9,8},{10,11... | collective-permute-start | bytes 7077896 | tf_op jit(solution)/shard_map/ppermute | solution.py:423
  137.3 2.6 %shard_map.92.kept = f32[512,2304]{1,0:T(8,128)S(1)} custom-call(s32[4]{0:T(128)S(1)} %pad_add_fusion.where.refs_0_, bf16[768,512]{1,0:T(8,128)(2,1)S(1)} %get-tuple-element.45.g.refs_2_, bf16[2,512,256]{2,1,0:T(8,128)(2,1)S(1)} %copy-done.6, bf16[3072,512]{1,0:T(8,128)(2,1)S(1)} %bitcast.9), custom_call_target="tpu_custom_call" | custom-call | flops 1207959552 | tf_op jit(solution)/shard_map/pallas_call | solution.py:39
  141.5 2.4 %shard_map.93.refs_4_ = bf16[512,2304]{1,0:T(8,128)(2,1)} custom-call(s32[4]{0:T(128)S(1)} %pad_add_fusion.where.refs_0_, f32[512,2304]{1,0:T(8,128)S(1)} %shard_map.92.kept, bf16[512,2304]{1,0:T(8,128)(2,1)S(1)} %collective-permute-done.28.got), custom_call_target="tpu_custom_call" | custom-call | tf_op jit(solution)/shard_map/pallas_call | solution.py:39
  143.9 6.6 %all-to-all-start = ((bf16[64,8,2304]{2,1,0:T(8,128)(2,1)}), bf16[64,8,2304]{2,1,0:T(8,128)(2,1)S(1)}, u32[]{:S(2)}, u32[]{:S(2)}) async-start(bf16[64,8,2304]{2,1,0:T(8,128)(2,1)} %bitcast.6), calls=%async_computation | async-start | bytes 4718592 | tf_op jit(solution)/shard_map/all_to_all | solution.py:457
  150.5 2.3 %copy-done.3 = bf16[768,3072]{1,0:T(8,128)(2,1)S(1)} copy-done((bf16[768,3072]{1,0:T(8,128)(2,1)S(1)}, bf16[768,3072]{1,0:T(8,128)(2,1)}, u32[]{:S(2)}) %copy-start.3) | copy-done | bytes 4718616
  154.0 9.6 %shard_map.94 = (f32[3072,1,512]{2,1,0:T(1,128)}, f32[8,128]{1,0:T(8,128)S(1)}) custom-call(s32[4]{0:T(128)S(1)} %pad_add_fusion.where.refs_0_, bf16[768,3072]{1,0:T(8,128)(2,1)S(1)} %copy-done.3, bf16[768,512]{1,0:T(8,128)(2,1)S(1)} %copy-done.5, bf16[768,768]{1,0:T(8,128)(2,1)S(1)} %shard_map.80.refs_6_.refs_1_.refs_3_, bf16[512,2304]{1,0:T(8,128)(2,1)} %shard_map.93.refs_4_), custom_call_target="tpu_custom_call" | custom-call | flops 2415919104 | tf_op jit(solution)/shard_map/pallas_call | solution.py:39
  163.6 17.5 %all-to-all-done.refs_1_ = bf16[64,8,2304]{2,1,0:T(8,128)(2,1)S(1)} async-done(((bf16[64,8,2304]{2,1,0:T(8,128)(2,1)}), bf16[64,8,2304]{2,1,0:T(8,128)(2,1)S(1)}, u32[]{:S(2)}, u32[]{:S(2)}) %all-to-all-start) | async-done | bytes 2359328 | tf_op jit(solution)/shard_map/all_to_all | solution.py:457
  182.0 2.9 %collective-permute-start.29 = (bf16[8,1536]{1,0:T(8,128)(2,1)S(1)}, bf16[8,1536]{1,0:T(8,128)(2,1)S(1)}, u32[]{:S(2)}, u32[]{:S(2)}) collective-permute-start(bf16[8,1536]{1,0:T(8,128)(2,1)S(1)} %get-tuple-element.49), channel_id=1, source_target_pairs={{0,1},{1,0},{2,3},{3,2},{4,5},{5,4},{6,7},{7,6},{8,9},{9,8},{10,11... | collective-permute-start | bytes 73736 | tf_op jit(solution)/shard_map/ppermute | solution.py:423
  (79 shorter events, 38.0 us)
Async XLA Ops:
  7.2 80.3 %all-gather.2.cloned.1.call-start = ((), (), s32[]{:S(2)}) async-start(), calls=%async_computation.1 | async-start | bytes 4866048 | tf_op jit(solution)/shard_map/all_gather | solution.py:429
  11.2 13.2 %collective-permute-start = (bf16[112,2048]{1,0:T(8,128)(2,1)S(1)}, bf16[112,2048]{1,0:T(8,128)(2,1)S(1)}, u32[]{:S(2)}, u32[]{:S(2)}) collective-permute-start(bf16[112,2048]{1,0:T(8,128)(2,1)S(1)} %get-tuple-element.28), channel_id=1, source_target_pairs={{0,32},{32,64},{64,96},{96,0},{1,33},{33,65},{65,97},{97,1},{2,34}... | collective-permute-start | bytes 1376264 | tf_op jit(solution)/shard_map/ppermute | solution.py:426
  13.3 22.2 %collective-permute-start.1 = (bf16[112,2048]{1,0:T(8,128)(2,1)S(1)}, bf16[112,2048]{1,0:T(8,128)(2,1)S(1)}, u32[]{:S(2)}, u32[]{:S(2)}) collective-permute-start(bf16[112,2048]{1,0:T(8,128)(2,1)S(1)} %get-tuple-element.29), channel_id=1, source_target_pairs={{0,64},{32,96},{64,0},{96,32},{1,65},{33,97},{65,1},{97,33},{2,66}... | collective-permute-start | bytes 1376264 | tf_op jit(solution)/shard_map/ppermute | solution.py:426
  15.8 19.8 %collective-permute-start.2 = (bf16[112,2048]{1,0:T(8,128)(2,1)S(1)}, bf16[112,2048]{1,0:T(8,128)(2,1)S(1)}, u32[]{:S(2)}, u32[]{:S(2)}) collective-permute-start(bf16[112,2048]{1,0:T(8,128)(2,1)S(1)} %get-tuple-element.30), channel_id=1, source_target_pairs={{0,96},{32,0},{64,32},{96,64},{1,97},{33,1},{65,33},{97,65},{2,98}... | collective-permute-start | bytes 1376264 | tf_op jit(solution)/shard_map/ppermute | solution.py:426
  37.0 3.1 %collective-permute-start.3 = (bf16[112,2048]{1,0:T(8,128)(2,1)S(1)}, bf16[112,2048]{1,0:T(8,128)(2,1)S(1)}, u32[]{:S(2)}, u32[]{:S(2)}) collective-permute-start(bf16[112,2048]{1,0:T(8,128)(2,1)S(1)} %collective-permute-done.g1), channel_id=1, source_target_pairs={{0,1},{1,0},{2,3},{3,2},{4,5},{5,4},{6,7},{7,6},{8,9},{9,8},{10,11... | collective-permute-start | bytes 1376264 | tf_op jit(solution)/shard_map/ppermute | solution.py:423
  38.6 2.1 %collective-permute-start.4 = (bf16[112,2048]{1,0:T(8,128)(2,1)S(1)}, bf16[112,2048]{1,0:T(8,128)(2,1)S(1)}, u32[]{:S(2)}, u32[]{:S(2)}) collective-permute-start(bf16[112,2048]{1,0:T(8,128)(2,1)S(1)} %collective-permute-done.1.g2), channel_id=1, source_target_pairs={{0,1},{1,0},{2,3},{3,2},{4,5},{5,4},{6,7},{7,6},{8,9},{9,8},{10,11... | collective-permute-start | bytes 1376264 | tf_op jit(solution)/shard_map/ppermute | solution.py:423
  38.7 2.7 %collective-permute-start.5 = (bf16[112,2048]{1,0:T(8,128)(2,1)S(1)}, bf16[112,2048]{1,0:T(8,128)(2,1)S(1)}, u32[]{:S(2)}, u32[]{:S(2)}) collective-permute-start(bf16[112,2048]{1,0:T(8,128)(2,1)S(1)} %collective-permute-done.2.g3), channel_id=1, source_target_pairs={{0,1},{1,0},{2,3},{3,2},{4,5},{5,4},{6,7},{7,6},{8,9},{9,8},{10,11... | collective-permute-start | bytes 1376264 | tf_op jit(solution)/shard_map/ppermute | solution.py:423
  44.6 11.8 %collective-permute-start.6 = (f32[192,512]{1,0:T(8,128)S(1)}, f32[192,512]{1,0:T(8,128)S(1)}, u32[]{:S(2)}, u32[]{:S(2)}) collective-permute-start(f32[192,512]{1,0:T(8,128)S(1)} %fusion.6), channel_id=1, source_target_pairs={{0,32},{32,64},{64,96},{96,0},{1,33},{33,65},{65,97},{97,1},{2,34}... | collective-permute-start | bytes 1179656 | tf_op jit(solution)/shard_map/ppermute | solution.py:417
  46.2 18.4 %collective-permute-start.10 = (f32[192,512]{1,0:T(8,128)S(1)}, f32[192,512]{1,0:T(8,128)S(1)}, u32[]{:S(2)}, u32[]{:S(2)}) collective-permute-start(f32[192,512]{1,0:T(8,128)S(1)} %fusion.4), channel_id=1, source_target_pairs={{0,32},{32,64},{64,96},{96,0},{1,33},{33,65},{65,97},{97,1},{2,34}... | collective-permute-start | bytes 1179656 | tf_op jit(solution)/shard_map/ppermute | solution.py:417
  48.0 9.8 %collective-permute-start.7 = (f32[192,512]{1,0:T(8,128)S(1)}, f32[192,512]{1,0:T(8,128)S(1)}, u32[]{:S(2)}, u32[]{:S(2)}) collective-permute-start(f32[192,512]{1,0:T(8,128)S(1)} %fusion.2), channel_id=1, source_target_pairs={{0,96},{32,0},{64,32},{96,64},{1,97},{33,1},{65,33},{97,65},{2,98}... | collective-permute-start | bytes 1179656 | tf_op jit(solution)/shard_map/ppermute | solution.py:417
  50.2 15.9 %collective-permute-start.11 = (f32[192,512]{1,0:T(8,128)S(1)}, f32[192,512]{1,0:T(8,128)S(1)}, u32[]{:S(2)}, u32[]{:S(2)}) collective-permute-start(f32[192,512]{1,0:T(8,128)S(1)} %fusion), channel_id=1, source_target_pairs={{0,96},{32,0},{64,32},{96,64},{1,97},{33,1},{65,33},{97,65},{2,98}... | collective-permute-start | bytes 1179656 | tf_op jit(solution)/shard_map/ppermute | solution.py:417
  58.4 16.3 %collective-permute-start.9 = (f32[192,512]{1,0:T(8,128)S(1)}, f32[192,512]{1,0:T(8,128)S(1)}, u32[]{:S(2)}, u32[]{:S(2)}) collective-permute-start(f32[192,512]{1,0:T(8,128)S(1)} %get-tuple-element.32), channel_id=1, source_target_pairs={{0,96},{32,0},{64,32},{96,64},{1,97},{33,1},{65,33},{97,65},{2,98}... | collective-permute-start | bytes 1179656 | tf_op jit(solution)/shard_map/ppermute | solution.py:417
  61.2 13.5 %collective-permute-start.8 = (f32[192,512]{1,0:T(8,128)S(1)}, f32[192,512]{1,0:T(8,128)S(1)}, u32[]{:S(2)}, u32[]{:S(2)}) collective-permute-start(f32[192,512]{1,0:T(8,128)S(1)} %get-tuple-element.31.refs_5_), channel_id=1, source_target_pairs={{0,32},{32,64},{64,96},{96,0},{1,33},{33,65},{65,97},{97,1},{2,34}... | collective-permute-start | bytes 1179656 | tf_op jit(solution)/shard_map/ppermute | solution.py:417
  66.8 16.3 %collective-permute-start.15 = (f32[192,512]{1,0:T(8,128)S(1)}, f32[192,512]{1,0:T(8,128)S(1)}, u32[]{:S(2)}, u32[]{:S(2)}) collective-permute-start(f32[192,512]{1,0:T(8,128)S(1)} %get-tuple-element.37), channel_id=1, source_target_pairs={{0,96},{32,0},{64,32},{96,64},{1,97},{33,1},{65,33},{97,65},{2,98}... | collective-permute-start | bytes 1179656 | tf_op jit(solution)/shard_map/ppermute | solution.py:417
  69.6 13.5 %collective-permute-start.14 = (f32[192,512]{1,0:T(8,128)S(1)}, f32[192,512]{1,0:T(8,128)S(1)}, u32[]{:S(2)}, u32[]{:S(2)}) collective-permute-start(f32[192,512]{1,0:T(8,128)S(1)} %get-tuple-element.33.refs_5_), channel_id=1, source_target_pairs={{0,32},{32,64},{64,96},{96,0},{1,33},{33,65},{65,97},{97,1},{2,34}... | collective-permute-start | bytes 1179656 | tf_op jit(solution)/shard_map/ppermute | solution.py:417
  75.3 20.5 %collective-permute-start.13 = (f32[192,512]{1,0:T(8,128)S(1)}, f32[192,512]{1,0:T(8,128)S(1)}, u32[]{:S(2)}, u32[]{:S(2)}) collective-permute-start(f32[192,512]{1,0:T(8,128)S(1)} %get-tuple-element.35), channel_id=1, source_target_pairs={{0,96},{32,0},{64,32},{96,64},{1,97},{33,1},{65,33},{97,65},{2,98}... | collective-permute-start | bytes 1179656 | tf_op jit(solution)/shard_map/ppermute | solution.py:417
  78.2 17.7 %collective-permute-start.12 = (f32[192,512]{1,0:T(8,128)S(1)}, f32[192,512]{1,0:T(8,128)}, u32[]{:S(2)}, u32[]{:S(2)}) collective-permute-start(f32[192,512]{1,0:T(8,128)S(1)} %get-tuple-element.34.refs_5_), channel_id=1, source_target_pairs={{0,32},{32,64},{64,96},{96,0},{1,33},{33,65},{65,97},{97,1},{2,34}... | collective-permute-start | bytes 1179656 | tf_op jit(solution)/shard_map/ppermute | solution.py:417
  84.5 15.4 %collective-permute-start.17 = (f32[192,512]{1,0:T(8,128)}, f32[192,512]{1,0:T(8,128)S(1)}, u32[]{:S(2)}, u32[]{:S(2)}) collective-permute-start(f32[192,512]{1,0:T(8,128)} %get-tuple-element.41), channel_id=1, source_target_pairs={{0,96},{32,0},{64,32},{96,64},{1,97},{33,1},{65,33},{97,65},{2,98}... | collective-permute-start | bytes 1179656 | tf_op jit(solution)/shard_map/ppermute | solution.py:417
  87.3 12.6 %collective-permute-start.16 = (f32[192,512]{1,0:T(8,128)S(1)}, f32[192,512]{1,0:T(8,128)S(1)}, u32[]{:S(2)}, u32[]{:S(2)}) collective-permute-start(f32[192,512]{1,0:T(8,128)S(1)} %get-tuple-element.38.refs_4_), channel_id=1, source_target_pairs={{0,32},{32,64},{64,96},{96,0},{1,33},{33,65},{65,97},{97,1},{2,34}... | collective-permute-start | bytes 1179656 | tf_op jit(solution)/shard_map/ppermute | solution.py:417
  101.7 2.8 %collective-permute-start.18 = (f32[8,768]{1,0:T(8,128)S(1)}, f32[8,768]{1,0:T(8,128)S(1)}, u32[]{:S(2)}, u32[]{:S(2)}) collective-permute-start(f32[8,768]{1,0:T(8,128)S(1)} %get-tuple-element.42.refs_0_), channel_id=1, source_target_pairs={{0,1},{1,0},{2,3},{3,2},{4,5},{5,4},{6,7},{7,6},{8,9},{9,8},{10,11... | collective-permute-start | bytes 73736 | tf_op jit(solution)/shard_map/ppermute | solution.py:423
  105.0 4.8 %collective-permute-start.21 = (f32[8,768]{1,0:T(8,128)S(1)}, f32[8,768]{1,0:T(8,128)S(1)}, u32[]{:S(2)}, u32[]{:S(2)}) collective-permute-start(f32[8,768]{1,0:T(8,128)S(1)} %shard_map.88.refs_0_), channel_id=1, source_target_pairs={{0,6},{2,0},{4,2},{6,4},{1,7},{3,1},{5,3},{7,5},{8,14},{10,8},{12,... | collective-permute-start | bytes 73736 | tf_op jit(solution)/shard_map/ppermute | solution.py:420
  108.8 4.2 %collective-permute-start.20 = (f32[8,768]{1,0:T(8,128)S(1)}, f32[8,768]{1,0:T(8,128)S(1)}, u32[]{:S(2)}, u32[]{:S(2)}) collective-permute-start(f32[8,768]{1,0:T(8,128)S(1)} %shard_map.88.refs_0_), channel_id=1, source_target_pairs={{0,4},{2,6},{4,0},{6,2},{1,5},{3,7},{5,1},{7,3},{8,12},{10,14},{12... | collective-permute-start | bytes 73736 | tf_op jit(solution)/shard_map/ppermute | solution.py:420
  108.8 4.2 %collective-permute-start.19 = (f32[8,768]{1,0:T(8,128)S(1)}, f32[8,768]{1,0:T(8,128)S(1)}, u32[]{:S(2)}, u32[]{:S(2)}) collective-permute-start(f32[8,768]{1,0:T(8,128)S(1)} %shard_map.88.refs_0_), channel_id=1, source_target_pairs={{0,2},{2,4},{4,6},{6,0},{1,3},{3,5},{5,7},{7,1},{8,10},{10,12},{12... | collective-permute-start | bytes 73736 | tf_op jit(solution)/shard_map/ppermute | solution.py:420
  113.6 3.8 %collective-permute-start.24 = (f32[8,768]{1,0:T(8,128)S(1)}, f32[8,768]{1,0:T(8,128)S(1)}, u32[]{:S(2)}, u32[]{:S(2)}) collective-permute-start(f32[8,768]{1,0:T(8,128)S(1)} %shard_map.89.refs_0_), channel_id=1, source_target_pairs={{0,24},{8,0},{16,8},{24,16},{1,25},{9,1},{17,9},{25,17},{2,26},{10... | collective-permute-start | bytes 73736 | tf_op jit(solution)/shard_map/ppermute | solution.py:420
  116.4 4.2 %collective-permute-start.23 = (f32[8,768]{1,0:T(8,128)S(1)}, f32[8,768]{1,0:T(8,128)S(1)}, u32[]{:S(2)}, u32[]{:S(2)}) collective-permute-start(f32[8,768]{1,0:T(8,128)S(1)} %shard_map.89.refs_0_), channel_id=1, source_target_pairs={{0,16},{8,24},{16,0},{24,8},{1,17},{9,25},{17,1},{25,9},{2,18},{10... | collective-permute-start | bytes 73736 | tf_op jit(solution)/shard_map/ppermute | solution.py:420
  116.8 4.1 %collective-permute-start.22 = (f32[8,768]{1,0:T(8,128)S(1)}, f32[8,768]{1,0:T(8,128)S(1)}, u32[]{:S(2)}, u32[]{:S(2)}) collective-permute-start(f32[8,768]{1,0:T(8,128)S(1)} %shard_map.89.refs_0_), channel_id=1, source_target_pairs={{0,8},{8,16},{16,24},{24,0},{1,9},{9,17},{17,25},{25,1},{2,10},{10... | collective-permute-start | bytes 73736 | tf_op jit(solution)/shard_map/ppermute | solution.py:420
  121.5 3.9 %collective-permute-start.27 = (f32[8,768]{1,0:T(8,128)S(1)}, f32[8,768]{1,0:T(8,128)S(1)}, u32[]{:S(2)}, u32[]{:S(2)}) collective-permute-start(f32[8,768]{1,0:T(8,128)S(1)} %shard_map.90.own), channel_id=1, source_target_pairs={{0,96},{32,0},{64,32},{96,64},{1,97},{33,1},{65,33},{97,65},{2,98}... | collective-permute-start | bytes 73736 | tf_op jit(solution)/shard_map/ppermute | solution.py:420
  124.4 4.2 %collective-permute-start.26 = (f32[8,768]{1,0:T(8,128)S(1)}, f32[8,768]{1,0:T(8,128)S(1)}, u32[]{:S(2)}, u32[]{:S(2)}) collective-permute-start(f32[8,768]{1,0:T(8,128)S(1)} %shard_map.90.own), channel_id=1, source_target_pairs={{0,64},{32,96},{64,0},{96,32},{1,65},{33,97},{65,1},{97,33},{2,66}... | collective-permute-start | bytes 73736 | tf_op jit(solution)/shard_map/ppermute | solution.py:420
  124.4 4.2 %collective-permute-start.25 = (f32[8,768]{1,0:T(8,128)S(1)}, f32[8,768]{1,0:T(8,128)S(1)}, u32[]{:S(2)}, u32[]{:S(2)}) collective-permute-start(f32[8,768]{1,0:T(8,128)S(1)} %shard_map.90.own), channel_id=1, source_target_pairs={{0,32},{32,64},{64,96},{96,0},{1,33},{33,65},{65,97},{97,1},{2,34}... | collective-permute-start | bytes 73736 | tf_op jit(solution)/shard_map/ppermute | solution.py:420
  132.3 9.2 %collective-permute-start.28 = (bf16[512,2304]{1,0:T(8,128)(2,1)S(1)}, bf16[512,2304]{1,0:T(8,128)(2,1)S(1)}, u32[]{:S(2)}, u32[]{:S(2)}) collective-permute-start(bf16[512,2304]{1,0:T(8,128)(2,1)S(1)} %get-tuple-element.46), channel_id=1, source_target_pairs={{0,1},{1,0},{2,3},{3,2},{4,5},{5,4},{6,7},{7,6},{8,9},{9,8},{10,11... | collective-permute-start | bytes 7077896 | tf_op jit(solution)/shard_map/ppermute | solution.py:423
  143.9 37.1 %all-to-all-start = ((bf16[64,8,2304]{2,1,0:T(8,128)(2,1)}), bf16[64,8,2304]{2,1,0:T(8,128)(2,1)S(1)}, u32[]{:S(2)}, u32[]{:S(2)}) async-start(bf16[64,8,2304]{2,1,0:T(8,128)(2,1)} %bitcast.6), calls=%async_computation | async-start | bytes 4718592 | tf_op jit(solution)/shard_map/all_to_all | solution.py:457
  182.0 3.7 %collective-permute-start.29 = (bf16[8,1536]{1,0:T(8,128)(2,1)S(1)}, bf16[8,1536]{1,0:T(8,128)(2,1)S(1)}, u32[]{:S(2)}, u32[]{:S(2)}) collective-permute-start(bf16[8,1536]{1,0:T(8,128)(2,1)S(1)} %get-tuple-element.49), channel_id=1, source_target_pairs={{0,1},{1,0},{2,3},{3,2},{4,5},{5,4},{6,7},{7,6},{8,9},{9,8},{10,11... | collective-permute-start | bytes 73736 | tf_op jit(solution)/shard_map/ppermute | solution.py:423
  (10 other events, 110.7 us)
Sparse Core Ops, SparseCore 0:
  37.1 50.3 all-gather.1

commit v5 on v4

--- a/solution.py
+++ b/solution.py
@@ -435,7 +435,11 @@
         return jnp.dot(rows, block, preferred_element_type=F32)
 
     n = h.shape[0] // 4
-    chains = [both_ways(product(h[i * n : (i + 1) * n], 3), product(h[(i + 2) * n : (i + 3) * n], 1)) for i in (0, 1)]
+    chains, source = [], h
+    for i in (0, 1):
+        r, l = product(source[i * n : (i + 1) * n], 3), product(source[(i + 2) * n : (i + 3) * n], 1)
+        chains.append(both_ways(r, l))
+        source = lax.optimization_barrier((h, l))[0]
     p = rest(where, h, tw)
     pick = pick_of(where, piece, (p,))
     before = ()

time: 194 us -> 193 us (level)
  starting transfers between devices: 52 us -> 44.8 us
  waiting for transfers between devices: 69.8 us -> 75.4 us
    ppermute x12, starting transfers between devices: 15.7 us -> 10.8 us  [both_ways(): return (lax.ppermute(r, 'x', shift(1)), lax.ppermute(l, 'x', shift(-1)))]
    ppermute x12, waiting for transfers between devices: 17.7 us -> 22.5 us  [both_ways(): return (lax.ppermute(r, 'x', shift(1)), lax.ppermute(l, 'x', shift(-1)))]
    ppermute x9, starting transfers between devices: 12 us -> 10 us  [others(): return [lax.ppermute(v, axis, shift(k)) for k in (1, 2, 3)]]
  transfers between devices with their start and end apart: 32 -> 32, of which waited for: 22 -> 24; matrix products, arithmetic and copies ran while one was open for 2% -> 2% of each run, Pallas kernels for 17% -> 17%
where the time goes in v5:
time: 193 us; the launch traced here: 192 us
  waiting for transfers between devices  75.4 us (39%)
  Pallas kernels  47.1 us (24%)
  starting transfers between devices  44.8 us (23%)
  between operations  14.3 us (7%)
  local copies, waits for them, and re-layouts  6.18 us (3%)
  matrix products  4.32 us (2%)
    pallas_call x21, Pallas kernels, call(): pl.pallas_call(ordered if after else body, out_shape=outs, grid_spec=pltp...  47.1 us
    ppermute x12, waiting for transfers between devices, both_ways(): return (lax.ppermute(r, 'x', shift(1)), lax.ppermute(l, 'x', shift(-1)))  22.5 us
    ppermute x3, waiting for transfers between devices, shards(): got = [lax.ppermute(s, 'x', shift(k + 1)) for k, s in enumerate(sends)]  18.6 us
    all_to_all x1, waiting for transfers between devices, shards(): lax.all_to_all(chip.reshape(64, 8, -1), CHIPS, split_axis=0, concat_axis=...  17.5 us
    ppermute x6, starting transfers between devices, swap(): return lax.ppermute(v, 'c', SWAP)  11.6 us
    ppermute x12, starting transfers between devices, both_ways(): return (lax.ppermute(r, 'x', shift(1)), lax.ppermute(l, 'x', shift(-1)))  10.8 us
    ppermute x9, waiting for transfers between devices, others(): return [lax.ppermute(v, axis, shift(k)) for k in (1, 2, 3)]  10.5 us
    ppermute x9, starting transfers between devices, others(): return [lax.ppermute(v, axis, shift(k)) for k in (1, 2, 3)]  10 us
  transfers between devices with their start and end apart: 32, of which 24 were waited for; matrix products, arithmetic and copies ran while one was open for 2% of the time, Pallas kernels for 17%

profile of v5, /device:TPU:1, one launch (start us, length us, event | category | flops | bytes accessed | tf_op | source)
XLA Modules:
  0.0 192.2 jit_solution(14964005024154454454)
XLA Ops:
  7.3 1.9 copy-done.8
  11.2 2.1 %collective-permute-start = (bf16[112,2048]{1,0:T(8,128)(2,1)S(1)}, bf16[112,2048]{1,0:T(8,128)(2,1)S(1)}, u32[]{:S(2)}, u32[]{:S(2)}) collective-permute-start(bf16[112,2048]{1,0:T(8,128)(2,1)S(1)} %get-tuple-element.29), channel_id=1, source_target_pairs={{0,32},{32,64},{64,96},{96,0},{1,33},{33,65},{65,97},{97,1},{2,34}... | collective-permute-start | bytes 1376264 | tf_op jit(solution)/shard_map/ppermute | solution.py:426
  13.3 2.5 %collective-permute-start.1 = (bf16[112,2048]{1,0:T(8,128)(2,1)S(1)}, bf16[112,2048]{1,0:T(8,128)(2,1)S(1)}, u32[]{:S(2)}, u32[]{:S(2)}) collective-permute-start(bf16[112,2048]{1,0:T(8,128)(2,1)S(1)} %get-tuple-element.30), channel_id=1, source_target_pairs={{0,64},{32,96},{64,0},{96,32},{1,65},{33,97},{65,1},{97,33},{2,66}... | collective-permute-start | bytes 1376264 | tf_op jit(solution)/shard_map/ppermute | solution.py:426
  16.9 7.5 %collective-permute-done.g1 = bf16[112,2048]{1,0:T(8,128)(2,1)S(1)} collective-permute-done((bf16[112,2048]{1,0:T(8,128)(2,1)S(1)}, bf16[112,2048]{1,0:T(8,128)(2,1)S(1)}, u32[]{:S(2)}, u32[]{:S(2)}) %collective-permute-start) | collective-permute-done | bytes 458784 | tf_op jit(solution)/shard_map/ppermute | solution.py:426
  24.4 11.1 %collective-permute-done.1.g2 = bf16[112,2048]{1,0:T(8,128)(2,1)S(1)} collective-permute-done((bf16[112,2048]{1,0:T(8,128)(2,1)S(1)}, bf16[112,2048]{1,0:T(8,128)(2,1)S(1)}, u32[]{:S(2)}, u32[]{:S(2)}) %collective-permute-start.1) | collective-permute-done | bytes 458784 | tf_op jit(solution)/shard_map/ppermute | solution.py:426
  37.0 1.6 collective-permute-start.3
  42.1 2.5 %fusion.2 = f32[192,512]{1,0:T(8,128)S(1)} fusion(bf16[2048,2048]{1,0:T(8,128)(2,1)} %tw.1, s32[]{:T(128)S(6)} %select_n.26, bf16[768,2048]{1,0:T(8,128)(2,1)S(1)} %shard_map.77.h), kind=kOutput, calls=%fused_computation.2 | convolution fusion | flops 402653184 | bytes 3276804 | tf_op jit(solution)/shard_map/dot_general | solution.py:435
  44.6 1.9 %collective-permute-start.7 = (f32[192,512]{1,0:T(8,128)S(1)}, f32[192,512]{1,0:T(8,128)S(1)}, u32[]{:S(2)}, u32[]{:S(2)}) collective-permute-start(f32[192,512]{1,0:T(8,128)S(1)} %fusion.2), channel_id=1, source_target_pairs={{0,96},{32,0},{64,32},{96,64},{1,97},{33,1},{65,33},{97,65},{2,98}... | collective-permute-start | bytes 1179656 | tf_op jit(solution)/shard_map/ppermute | solution.py:417
  49.4 1.9 collective-permute-start.11
  51.3 5.6 %shard_map.78.pr.pl_.refs_1_.refs_2_.p = f32[3,768,512]{2,1,0:T(8,128)S(1)} custom-call(s32[4]{0:T(128)S(1)} %pad_add_fusion.where.refs_0_, bf16[768,2048]{1,0:T(8,128)(2,1)S(1)} %shard_map.77.h, bf16[2048,2048]{1,0:T(8,128)(2,1)S(1)} %copy-done.7), custom_call_target="tpu_custom_call" | custom-call | flops 4831838208 | tf_op jit(solution)/shard_map/pallas_call | solution.py:39
  61.6 5.3 %collective-permute-done.10.refs_3_ = f32[192,512]{1,0:T(8,128)S(1)} collective-permute-done((f32[192,512]{1,0:T(8,128)S(1)}, f32[192,512]{1,0:T(8,128)S(1)}, u32[]{:S(2)}, u32[]{:S(2)}) %collective-permute-start.10) | collective-permute-done | bytes 393248 | tf_op jit(solution)/shard_map/ppermute | solution.py:417
  69.0 2.8 %collective-permute-done.9.refs_4_ = f32[192,512]{1,0:T(8,128)S(1)} collective-permute-done((f32[192,512]{1,0:T(8,128)S(1)}, f32[192,512]{1,0:T(8,128)S(1)}, u32[]{:S(2)}, u32[]{:S(2)}) %collective-permute-start.9) | collective-permute-done | bytes 393248 | tf_op jit(solution)/shard_map/ppermute | solution.py:417
  71.8 3.6 %collective-permute-done.8.refs_3_ = f32[192,512]{1,0:T(8,128)S(1)} collective-permute-done((f32[192,512]{1,0:T(8,128)S(1)}, f32[192,512]{1,0:T(8,128)S(1)}, u32[]{:S(2)}, u32[]{:S(2)}) %collective-permute-start.8) | collective-permute-done | bytes 393248 | tf_op jit(solution)/shard_map/ppermute | solution.py:417
  77.6 2.8 %collective-permute-done.15.refs_4_ = f32[192,512]{1,0:T(8,128)S(1)} collective-permute-done((f32[192,512]{1,0:T(8,128)S(1)}, f32[192,512]{1,0:T(8,128)S(1)}, u32[]{:S(2)}, u32[]{:S(2)}) %collective-permute-start.15) | collective-permute-done | bytes 393248 | tf_op jit(solution)/shard_map/ppermute | solution.py:417
  80.4 3.5 %collective-permute-done.14.refs_3_ = f32[192,512]{1,0:T(8,128)S(1)} collective-permute-done((f32[192,512]{1,0:T(8,128)S(1)}, f32[192,512]{1,0:T(8,128)S(1)}, u32[]{:S(2)}, u32[]{:S(2)}) %collective-permute-start.14) | collective-permute-done | bytes 393248 | tf_op jit(solution)/shard_map/ppermute | solution.py:417
  87.6 8.4 %shard_map.85.refs_5_.sl = f32[768,512]{1,0:T(8,128)S(1)} custom-call(s32[4]{0:T(128)S(1)} %pad_add_fusion.where.refs_0_, bf16[768,768]{1,0:T(8,128)(2,1)S(1)} %shard_map.80.refs_6_.refs_1_.refs_3_, bf16[768,3072]{1,0:T(8,128)(2,1)} %all-gather.2.cloned.1.call-done.refs_2_.refs_1_, bf16[3072,512]{1,0:T(8,128)(2,1)} %bitcast.7, ...), custom_call_target="tpu_custom_call" | custom-call | tf_op jit(solution)/shard_map/pallas_call | solution.py:39
  96.0 1.6 shard_map.86
  97.6 2.9 %collective-permute-done.16.r1 = f32[192,512]{1,0:T(8,128)S(1)} collective-permute-done((f32[192,512]{1,0:T(8,128)S(1)}, f32[192,512]{1,0:T(8,128)S(1)}, u32[]{:S(2)}, u32[]{:S(2)}) %collective-permute-start.16) | collective-permute-done | bytes 393248 | tf_op jit(solution)/shard_map/ppermute | solution.py:417
  100.6 1.8 shard_map.87
  105.4 3.9 %collective-permute-start.21 = (f32[8,768]{1,0:T(8,128)S(1)}, f32[8,768]{1,0:T(8,128)S(1)}, u32[]{:S(2)}, u32[]{:S(2)}) collective-permute-start(f32[8,768]{1,0:T(8,128)S(1)} %shard_map.88.refs_0_), channel_id=1, source_target_pairs={{0,6},{2,0},{4,2},{6,4},{1,7},{3,1},{5,3},{7,5},{8,14},{10,8},{12,... | collective-permute-start | bytes 73736 | tf_op jit(solution)/shard_map/ppermute | solution.py:420
  110.2 3.2 %collective-permute-done.20.refs_2_ = f32[8,768]{1,0:T(8,128)S(1)} collective-permute-done((f32[8,768]{1,0:T(8,128)S(1)}, f32[8,768]{1,0:T(8,128)S(1)}, u32[]{:S(2)}, u32[]{:S(2)}) %collective-permute-start.20) | collective-permute-done | bytes 24608 | tf_op jit(solution)/shard_map/ppermute | solution.py:420
  114.1 2.8 %collective-permute-start.24 = (f32[8,768]{1,0:T(8,128)S(1)}, f32[8,768]{1,0:T(8,128)S(1)}, u32[]{:S(2)}, u32[]{:S(2)}) collective-permute-start(f32[8,768]{1,0:T(8,128)S(1)} %shard_map.89.refs_0_), channel_id=1, source_target_pairs={{0,24},{8,0},{16,8},{24,16},{1,25},{9,1},{17,9},{25,17},{2,26},{10... | collective-permute-start | bytes 73736 | tf_op jit(solution)/shard_map/ppermute | solution.py:420
  117.9 3.2 %collective-permute-done.23.refs_2_ = f32[8,768]{1,0:T(8,128)S(1)} collective-permute-done((f32[8,768]{1,0:T(8,128)S(1)}, f32[8,768]{1,0:T(8,128)S(1)}, u32[]{:S(2)}, u32[]{:S(2)}) %collective-permute-start.23) | collective-permute-done | bytes 24608 | tf_op jit(solution)/shard_map/ppermute | solution.py:420
  127.1 3.7 %shard_map.91 = (bf16[768,512]{1,0:T(8,128)(2,1)S(1)}, bf16[512,2304]{1,0:T(8,128)(2,1)S(1)}, f32[1,1]{1,0:T(1,128)}) custom-call(s32[4]{0:T(128)S(1)} %pad_add_fusion.where.refs_0_, f32[8,768]{1,0:T(8,128)S(1)} %shard_map.90.own, f32[8,768]{1,0:T(8,128)S(1)} %collective-permute-done.25.g1, f32[8,768]{1,0:T(8,128)S(1)} %collective-permute-done.26.g2, ...), custom_call_target="tpu_custom_call" | custom-call | flops 1207959552 | tf_op jit(solution)/shard_map/pallas_call | solution.py:39
  130.8 5.0 %collective-permute-start.28 = (bf16[512,2304]{1,0:T(8,128)(2,1)S(1)}, bf16[512,2304]{1,0:T(8,128)(2,1)S(1)}, u32[]{:S(2)}, u32[]{:S(2)}) collective-permute-start(bf16[512,2304]{1,0:T(8,128)(2,1)S(1)} %get-tuple-element.48), channel_id=1, source_target_pairs={{0,1},{1,0},{2,3},{3,2},{4,5},{5,4},{6,7},{7,6},{8,9},{9,8},{10,11... | collective-permute-start | bytes 7077896 | tf_op jit(solution)/shard_map/ppermute | solution.py:423
  135.8 2.6 %shard_map.92.kept = f32[512,2304]{1,0:T(8,128)S(1)} custom-call(s32[4]{0:T(128)S(1)} %pad_add_fusion.where.refs_0_, bf16[768,512]{1,0:T(8,128)(2,1)S(1)} %get-tuple-element.47.g.refs_2_, bf16[2,512,256]{2,1,0:T(8,128)(2,1)S(1)} %copy-done.6, bf16[3072,512]{1,0:T(8,128)(2,1)S(1)} %bitcast.9), custom_call_target="tpu_custom_call" | custom-call | flops 1207959552 | tf_op jit(solution)/shard_map/pallas_call | solution.py:39
  140.0 2.4 %shard_map.93.refs_4_ = bf16[512,2304]{1,0:T(8,128)(2,1)} custom-call(s32[4]{0:T(128)S(1)} %pad_add_fusion.where.refs_0_, f32[512,2304]{1,0:T(8,128)S(1)} %shard_map.92.kept, bf16[512,2304]{1,0:T(8,128)(2,1)S(1)} %collective-permute-done.28.got), custom_call_target="tpu_custom_call" | custom-call | tf_op jit(solution)/shard_map/pallas_call | solution.py:39
  142.4 6.6 %all-to-all-start = ((bf16[64,8,2304]{2,1,0:T(8,128)(2,1)}), bf16[64,8,2304]{2,1,0:T(8,128)(2,1)S(1)}, u32[]{:S(2)}, u32[]{:S(2)}) async-start(bf16[64,8,2304]{2,1,0:T(8,128)(2,1)} %bitcast.6), calls=%async_computation | async-start | bytes 4718592 | tf_op jit(solution)/shard_map/all_to_all | solution.py:461
  149.0 2.3 %copy-done.3 = bf16[768,3072]{1,0:T(8,128)(2,1)S(1)} copy-done((bf16[768,3072]{1,0:T(8,128)(2,1)S(1)}, bf16[768,3072]{1,0:T(8,128)(2,1)}, u32[]{:S(2)}) %copy-start.3) | copy-done | bytes 4718616
  152.5 9.6 %shard_map.94 = (f32[3072,1,512]{2,1,0:T(1,128)}, f32[8,128]{1,0:T(8,128)S(1)}) custom-call(s32[4]{0:T(128)S(1)} %pad_add_fusion.where.refs_0_, bf16[768,3072]{1,0:T(8,128)(2,1)S(1)} %copy-done.3, bf16[768,512]{1,0:T(8,128)(2,1)S(1)} %copy-done.5, bf16[768,768]{1,0:T(8,128)(2,1)S(1)} %shard_map.80.refs_6_.refs_1_.refs_3_, bf16[512,2304]{1,0:T(8,128)(2,1)} %shard_map.93.refs_4_), custom_call_target="tpu_custom_call" | custom-call | flops 2415919104 | tf_op jit(solution)/shard_map/pallas_call | solution.py:39
  162.1 17.5 %all-to-all-done.refs_1_ = bf16[64,8,2304]{2,1,0:T(8,128)(2,1)S(1)} async-done(((bf16[64,8,2304]{2,1,0:T(8,128)(2,1)}), bf16[64,8,2304]{2,1,0:T(8,128)(2,1)S(1)}, u32[]{:S(2)}, u32[]{:S(2)}) %all-to-all-start) | async-done | bytes 2359328 | tf_op jit(solution)/shard_map/all_to_all | solution.py:461
  180.5 2.9 %collective-permute-start.29 = (bf16[8,1536]{1,0:T(8,128)(2,1)S(1)}, bf16[8,1536]{1,0:T(8,128)(2,1)S(1)}, u32[]{:S(2)}, u32[]{:S(2)}) collective-permute-start(bf16[8,1536]{1,0:T(8,128)(2,1)S(1)} %get-tuple-element.51), channel_id=1, source_target_pairs={{0,1},{1,0},{2,3},{3,2},{4,5},{5,4},{6,7},{7,6},{8,9},{9,8},{10,11... | collective-permute-start | bytes 73736 | tf_op jit(solution)/shard_map/ppermute | solution.py:423
  (79 shorter events, 40.9 us)
Async XLA Ops:
  7.2 80.4 %all-gather.2.cloned.1.call-start = ((), (), s32[]{:S(2)}) async-start(), calls=%async_computation.1 | async-start | bytes 4866048 | tf_op jit(solution)/shard_map/all_gather | solution.py:429
  11.2 13.2 %collective-permute-start = (bf16[112,2048]{1,0:T(8,128)(2,1)S(1)}, bf16[112,2048]{1,0:T(8,128)(2,1)S(1)}, u32[]{:S(2)}, u32[]{:S(2)}) collective-permute-start(bf16[112,2048]{1,0:T(8,128)(2,1)S(1)} %get-tuple-element.29), channel_id=1, source_target_pairs={{0,32},{32,64},{64,96},{96,0},{1,33},{33,65},{65,97},{97,1},{2,34}... | collective-permute-start | bytes 1376264 | tf_op jit(solution)/shard_map/ppermute | solution.py:426
  13.3 22.2 %collective-permute-start.1 = (bf16[112,2048]{1,0:T(8,128)(2,1)S(1)}, bf16[112,2048]{1,0:T(8,128)(2,1)S(1)}, u32[]{:S(2)}, u32[]{:S(2)}) collective-permute-start(bf16[112,2048]{1,0:T(8,128)(2,1)S(1)} %get-tuple-element.30), channel_id=1, source_target_pairs={{0,64},{32,96},{64,0},{96,32},{1,65},{33,97},{65,1},{97,33},{2,66}... | collective-permute-start | bytes 1376264 | tf_op jit(solution)/shard_map/ppermute | solution.py:426
  15.8 19.8 %collective-permute-start.2 = (bf16[112,2048]{1,0:T(8,128)(2,1)S(1)}, bf16[112,2048]{1,0:T(8,128)(2,1)S(1)}, u32[]{:S(2)}, u32[]{:S(2)}) collective-permute-start(bf16[112,2048]{1,0:T(8,128)(2,1)S(1)} %get-tuple-element.31), channel_id=1, source_target_pairs={{0,96},{32,0},{64,32},{96,64},{1,97},{33,1},{65,33},{97,65},{2,98}... | collective-permute-start | bytes 1376264 | tf_op jit(solution)/shard_map/ppermute | solution.py:426
  37.0 3.1 %collective-permute-start.3 = (bf16[112,2048]{1,0:T(8,128)(2,1)S(1)}, bf16[112,2048]{1,0:T(8,128)(2,1)S(1)}, u32[]{:S(2)}, u32[]{:S(2)}) collective-permute-start(bf16[112,2048]{1,0:T(8,128)(2,1)S(1)} %collective-permute-done.g1), channel_id=1, source_target_pairs={{0,1},{1,0},{2,3},{3,2},{4,5},{5,4},{6,7},{7,6},{8,9},{9,8},{10,11... | collective-permute-start | bytes 1376264 | tf_op jit(solution)/shard_map/ppermute | solution.py:423
  38.6 2.1 %collective-permute-start.4 = (bf16[112,2048]{1,0:T(8,128)(2,1)S(1)}, bf16[112,2048]{1,0:T(8,128)(2,1)S(1)}, u32[]{:S(2)}, u32[]{:S(2)}) collective-permute-start(bf16[112,2048]{1,0:T(8,128)(2,1)S(1)} %collective-permute-done.1.g2), channel_id=1, source_target_pairs={{0,1},{1,0},{2,3},{3,2},{4,5},{5,4},{6,7},{7,6},{8,9},{9,8},{10,11... | collective-permute-start | bytes 1376264 | tf_op jit(solution)/shard_map/ppermute | solution.py:423
  38.7 2.7 %collective-permute-start.5 = (bf16[112,2048]{1,0:T(8,128)(2,1)S(1)}, bf16[112,2048]{1,0:T(8,128)(2,1)S(1)}, u32[]{:S(2)}, u32[]{:S(2)}) collective-permute-start(bf16[112,2048]{1,0:T(8,128)(2,1)S(1)} %collective-permute-done.2.g3), channel_id=1, source_target_pairs={{0,1},{1,0},{2,3},{3,2},{4,5},{5,4},{6,7},{7,6},{8,9},{9,8},{10,11... | collective-permute-start | bytes 1376264 | tf_op jit(solution)/shard_map/ppermute | solution.py:423
  44.6 13.9 %collective-permute-start.7 = (f32[192,512]{1,0:T(8,128)S(1)}, f32[192,512]{1,0:T(8,128)S(1)}, u32[]{:S(2)}, u32[]{:S(2)}) collective-permute-start(f32[192,512]{1,0:T(8,128)S(1)} %fusion.2), channel_id=1, source_target_pairs={{0,96},{32,0},{64,32},{96,64},{1,97},{33,1},{65,33},{97,65},{2,98}... | collective-permute-start | bytes 1179656 | tf_op jit(solution)/shard_map/ppermute | solution.py:417
  47.2 11.3 %collective-permute-start.6 = (f32[192,512]{1,0:T(8,128)S(1)}, f32[192,512]{1,0:T(8,128)S(1)}, u32[]{:S(2)}, u32[]{:S(2)}) collective-permute-start(f32[192,512]{1,0:T(8,128)S(1)} %fusion.6), channel_id=1, source_target_pairs={{0,32},{32,64},{64,96},{96,0},{1,33},{33,65},{65,97},{97,1},{2,34}... | collective-permute-start | bytes 1179656 | tf_op jit(solution)/shard_map/ppermute | solution.py:417
  47.9 19.0 %collective-permute-start.10 = (f32[192,512]{1,0:T(8,128)S(1)}, f32[192,512]{1,0:T(8,128)S(1)}, u32[]{:S(2)}, u32[]{:S(2)}) collective-permute-start(f32[192,512]{1,0:T(8,128)S(1)} %fusion.4), channel_id=1, source_target_pairs={{0,32},{32,64},{64,96},{96,0},{1,33},{33,65},{65,97},{97,1},{2,34}... | collective-permute-start | bytes 1179656 | tf_op jit(solution)/shard_map/ppermute | solution.py:417
  49.4 17.5 %collective-permute-start.11 = (f32[192,512]{1,0:T(8,128)S(1)}, f32[192,512]{1,0:T(8,128)S(1)}, u32[]{:S(2)}, u32[]{:S(2)}) collective-permute-start(f32[192,512]{1,0:T(8,128)S(1)} %fusion), channel_id=1, source_target_pairs={{0,96},{32,0},{64,32},{96,64},{1,97},{33,1},{65,33},{97,65},{2,98}... | collective-permute-start | bytes 1179656 | tf_op jit(solution)/shard_map/ppermute | solution.py:417
  59.1 12.8 %collective-permute-start.9 = (f32[192,512]{1,0:T(8,128)S(1)}, f32[192,512]{1,0:T(8,128)S(1)}, u32[]{:S(2)}, u32[]{:S(2)}) collective-permute-start(f32[192,512]{1,0:T(8,128)S(1)} %get-tuple-element.33), channel_id=1, source_target_pairs={{0,96},{32,0},{64,32},{96,64},{1,97},{33,1},{65,33},{97,65},{2,98}... | collective-permute-start | bytes 1179656 | tf_op jit(solution)/shard_map/ppermute | solution.py:417
  59.2 16.2 %collective-permute-start.8 = (f32[192,512]{1,0:T(8,128)S(1)}, f32[192,512]{1,0:T(8,128)S(1)}, u32[]{:S(2)}, u32[]{:S(2)}) collective-permute-start(f32[192,512]{1,0:T(8,128)S(1)} %get-tuple-element.32.refs_5_), channel_id=1, source_target_pairs={{0,32},{32,64},{64,96},{96,0},{1,33},{33,65},{65,97},{97,1},{2,34}... | collective-permute-start | bytes 1179656 | tf_op jit(solution)/shard_map/ppermute | solution.py:417
  67.5 12.9 %collective-permute-start.15 = (f32[192,512]{1,0:T(8,128)S(1)}, f32[192,512]{1,0:T(8,128)S(1)}, u32[]{:S(2)}, u32[]{:S(2)}) collective-permute-start(f32[192,512]{1,0:T(8,128)S(1)} %get-tuple-element.39), channel_id=1, source_target_pairs={{0,96},{32,0},{64,32},{96,64},{1,97},{33,1},{65,33},{97,65},{2,98}... | collective-permute-start | bytes 1179656 | tf_op jit(solution)/shard_map/ppermute | solution.py:417
  67.6 16.2 %collective-permute-start.14 = (f32[192,512]{1,0:T(8,128)S(1)}, f32[192,512]{1,0:T(8,128)S(1)}, u32[]{:S(2)}, u32[]{:S(2)}) collective-permute-start(f32[192,512]{1,0:T(8,128)S(1)} %get-tuple-element.35.refs_5_), channel_id=1, source_target_pairs={{0,32},{32,64},{64,96},{96,0},{1,33},{33,65},{65,97},{97,1},{2,34}... | collective-permute-start | bytes 1179656 | tf_op jit(solution)/shard_map/ppermute | solution.py:417
  76.0 19.9 %collective-permute-start.13 = (f32[192,512]{1,0:T(8,128)S(1)}, f32[192,512]{1,0:T(8,128)S(1)}, u32[]{:S(2)}, u32[]{:S(2)}) collective-permute-start(f32[192,512]{1,0:T(8,128)S(1)} %get-tuple-element.37), channel_id=1, source_target_pairs={{0,96},{32,0},{64,32},{96,64},{1,97},{33,1},{65,33},{97,65},{2,98}... | collective-permute-start | bytes 1179656 | tf_op jit(solution)/shard_map/ppermute | solution.py:417
  76.1 19.9 %collective-permute-start.12 = (f32[192,512]{1,0:T(8,128)S(1)}, f32[192,512]{1,0:T(8,128)}, u32[]{:S(2)}, u32[]{:S(2)}) collective-permute-start(f32[192,512]{1,0:T(8,128)S(1)} %get-tuple-element.36.refs_5_), channel_id=1, source_target_pairs={{0,32},{32,64},{64,96},{96,0},{1,33},{33,65},{65,97},{97,1},{2,34}... | collective-permute-start | bytes 1179656 | tf_op jit(solution)/shard_map/ppermute | solution.py:417
  85.2 12.4 %collective-permute-start.17 = (f32[192,512]{1,0:T(8,128)}, f32[192,512]{1,0:T(8,128)S(1)}, u32[]{:S(2)}, u32[]{:S(2)}) collective-permute-start(f32[192,512]{1,0:T(8,128)} %get-tuple-element.43), channel_id=1, source_target_pairs={{0,96},{32,0},{64,32},{96,64},{1,97},{33,1},{65,33},{97,65},{2,98}... | collective-permute-start | bytes 1179656 | tf_op jit(solution)/shard_map/ppermute | solution.py:417
  85.2 15.4 %collective-permute-start.16 = (f32[192,512]{1,0:T(8,128)S(1)}, f32[192,512]{1,0:T(8,128)S(1)}, u32[]{:S(2)}, u32[]{:S(2)}) collective-permute-start(f32[192,512]{1,0:T(8,128)S(1)} %get-tuple-element.40.refs_4_), channel_id=1, source_target_pairs={{0,32},{32,64},{64,96},{96,0},{1,33},{33,65},{65,97},{97,1},{2,34}... | collective-permute-start | bytes 1179656 | tf_op jit(solution)/shard_map/ppermute | solution.py:417
  102.4 2.4 %collective-permute-start.18 = (f32[8,768]{1,0:T(8,128)S(1)}, f32[8,768]{1,0:T(8,128)S(1)}, u32[]{:S(2)}, u32[]{:S(2)}) collective-permute-start(f32[8,768]{1,0:T(8,128)S(1)} %get-tuple-element.44.refs_0_), channel_id=1, source_target_pairs={{0,1},{1,0},{2,3},{3,2},{4,5},{5,4},{6,7},{7,6},{8,9},{9,8},{10,11... | collective-permute-start | bytes 73736 | tf_op jit(solution)/shard_map/ppermute | solution.py:423
  105.4 4.9 %collective-permute-start.21 = (f32[8,768]{1,0:T(8,128)S(1)}, f32[8,768]{1,0:T(8,128)S(1)}, u32[]{:S(2)}, u32[]{:S(2)}) collective-permute-start(f32[8,768]{1,0:T(8,128)S(1)} %shard_map.88.refs_0_), channel_id=1, source_target_pairs={{0,6},{2,0},{4,2},{6,4},{1,7},{3,1},{5,3},{7,5},{8,14},{10,8},{12,... | collective-permute-start | bytes 73736 | tf_op jit(solution)/shard_map/ppermute | solution.py:420
  109.3 4.2 %collective-permute-start.20 = (f32[8,768]{1,0:T(8,128)S(1)}, f32[8,768]{1,0:T(8,128)S(1)}, u32[]{:S(2)}, u32[]{:S(2)}) collective-permute-start(f32[8,768]{1,0:T(8,128)S(1)} %shard_map.88.refs_0_), channel_id=1, source_target_pairs={{0,4},{2,6},{4,0},{6,2},{1,5},{3,7},{5,1},{7,3},{8,12},{10,14},{12... | collective-permute-start | bytes 73736 | tf_op jit(solution)/shard_map/ppermute | solution.py:420
  109.3 4.2 %collective-permute-start.19 = (f32[8,768]{1,0:T(8,128)S(1)}, f32[8,768]{1,0:T(8,128)S(1)}, u32[]{:S(2)}, u32[]{:S(2)}) collective-permute-start(f32[8,768]{1,0:T(8,128)S(1)} %shard_map.88.refs_0_), channel_id=1, source_target_pairs={{0,2},{2,4},{4,6},{6,0},{1,3},{3,5},{5,7},{7,1},{8,10},{10,12},{12... | collective-permute-start | bytes 73736 | tf_op jit(solution)/shard_map/ppermute | solution.py:420
  114.1 3.8 %collective-permute-start.24 = (f32[8,768]{1,0:T(8,128)S(1)}, f32[8,768]{1,0:T(8,128)S(1)}, u32[]{:S(2)}, u32[]{:S(2)}) collective-permute-start(f32[8,768]{1,0:T(8,128)S(1)} %shard_map.89.refs_0_), channel_id=1, source_target_pairs={{0,24},{8,0},{16,8},{24,16},{1,25},{9,1},{17,9},{25,17},{2,26},{10... | collective-permute-start | bytes 73736 | tf_op jit(solution)/shard_map/ppermute | solution.py:420
  116.9 4.2 %collective-permute-start.23 = (f32[8,768]{1,0:T(8,128)S(1)}, f32[8,768]{1,0:T(8,128)S(1)}, u32[]{:S(2)}, u32[]{:S(2)}) collective-permute-start(f32[8,768]{1,0:T(8,128)S(1)} %shard_map.89.refs_0_), channel_id=1, source_target_pairs={{0,16},{8,24},{16,0},{24,8},{1,17},{9,25},{17,1},{25,9},{2,18},{10... | collective-permute-start | bytes 73736 | tf_op jit(solution)/shard_map/ppermute | solution.py:420
  117.2 4.1 %collective-permute-start.22 = (f32[8,768]{1,0:T(8,128)S(1)}, f32[8,768]{1,0:T(8,128)S(1)}, u32[]{:S(2)}, u32[]{:S(2)}) collective-permute-start(f32[8,768]{1,0:T(8,128)S(1)} %shard_map.89.refs_0_), channel_id=1, source_target_pairs={{0,8},{8,16},{16,24},{24,0},{1,9},{9,17},{17,25},{25,1},{2,10},{10... | collective-permute-start | bytes 73736 | tf_op jit(solution)/shard_map/ppermute | solution.py:420
  121.9 2.7 %collective-permute-start.27 = (f32[8,768]{1,0:T(8,128)S(1)}, f32[8,768]{1,0:T(8,128)S(1)}, u32[]{:S(2)}, u32[]{:S(2)}) collective-permute-start(f32[8,768]{1,0:T(8,128)S(1)} %shard_map.90.own), channel_id=1, source_target_pairs={{0,96},{32,0},{64,32},{96,64},{1,97},{33,1},{65,33},{97,65},{2,98}... | collective-permute-start | bytes 73736 | tf_op jit(solution)/shard_map/ppermute | solution.py:420
  122.0 4.3 %collective-permute-start.26 = (f32[8,768]{1,0:T(8,128)S(1)}, f32[8,768]{1,0:T(8,128)S(1)}, u32[]{:S(2)}, u32[]{:S(2)}) collective-permute-start(f32[8,768]{1,0:T(8,128)S(1)} %shard_map.90.own), channel_id=1, source_target_pairs={{0,64},{32,96},{64,0},{96,32},{1,65},{33,97},{65,1},{97,33},{2,66}... | collective-permute-start | bytes 73736 | tf_op jit(solution)/shard_map/ppermute | solution.py:420
  122.6 4.5 %collective-permute-start.25 = (f32[8,768]{1,0:T(8,128)S(1)}, f32[8,768]{1,0:T(8,128)S(1)}, u32[]{:S(2)}, u32[]{:S(2)}) collective-permute-start(f32[8,768]{1,0:T(8,128)S(1)} %shard_map.90.own), channel_id=1, source_target_pairs={{0,32},{32,64},{64,96},{96,0},{1,33},{33,65},{65,97},{97,1},{2,34}... | collective-permute-start | bytes 73736 | tf_op jit(solution)/shard_map/ppermute | solution.py:420
  130.8 9.2 %collective-permute-start.28 = (bf16[512,2304]{1,0:T(8,128)(2,1)S(1)}, bf16[512,2304]{1,0:T(8,128)(2,1)S(1)}, u32[]{:S(2)}, u32[]{:S(2)}) collective-permute-start(bf16[512,2304]{1,0:T(8,128)(2,1)S(1)} %get-tuple-element.48), channel_id=1, source_target_pairs={{0,1},{1,0},{2,3},{3,2},{4,5},{5,4},{6,7},{7,6},{8,9},{9,8},{10,11... | collective-permute-start | bytes 7077896 | tf_op jit(solution)/shard_map/ppermute | solution.py:423
  142.4 37.2 %all-to-all-start = ((bf16[64,8,2304]{2,1,0:T(8,128)(2,1)}), bf16[64,8,2304]{2,1,0:T(8,128)(2,1)S(1)}, u32[]{:S(2)}, u32[]{:S(2)}) async-start(bf16[64,8,2304]{2,1,0:T(8,128)(2,1)} %bitcast.6), calls=%async_computation | async-start | bytes 4718592 | tf_op jit(solution)/shard_map/all_to_all | solution.py:461
  180.5 3.7 %collective-permute-start.29 = (bf16[8,1536]{1,0:T(8,128)(2,1)S(1)}, bf16[8,1536]{1,0:T(8,128)(2,1)S(1)}, u32[]{:S(2)}, u32[]{:S(2)}) collective-permute-start(bf16[8,1536]{1,0:T(8,128)(2,1)S(1)} %get-tuple-element.51), channel_id=1, source_target_pairs={{0,1},{1,0},{2,3},{3,2},{4,5},{5,4},{6,7},{7,6},{8,9},{9,8},{10,11... | collective-permute-start | bytes 73736 | tf_op jit(solution)/shard_map/ppermute | solution.py:423
  (10 other events, 107.4 us)
Sparse Core Ops, SparseCore 0:
  37.1 50.4 all-gather.1
